TPU v7x, 32 devices: a whole 2x2x4 slice. The times are simulated.
32 devices in a mesh: parts: 2 (over y), gx: 4 (over x, core), gy: 4 (over z).
Axes of the slice: x: 2, y: 2, z: 4, core: 2. Of those that a mesh axis runs over, the one named last changes fastest.
Arguments:
- hidden_states: bfloat16 [128, 16384], P(('parts', 'gy'), 'gx'), parts along dimension 0, may hold values from -400 to 400
- norm_gain: bfloat16 [16384], P('gx'), may hold values from 0.099609375 to 1.8984375
- w_query: bfloat16 [16384, 8192], P('gx', 'gy'), may hold values from -0.046875 to 0.046875
- key_weight: bfloat16 [16384, 512], P('gx', 'gy'), may hold values from -0.046875 to 0.046875
- value_weight: bfloat16 [16384, 512], P('gx', 'gy'), may hold values from -0.046875 to 0.046875
- w_output: bfloat16 [8192, 16384], P('gy', 'gx'), may hold values from -0.25 to 0.25
- stored_key_cache: bfloat16 [128, 256, 512], P(('parts', 'gx', 'gy')), parts along dimension 0, may hold values from -120 to 120
- stored_value_cache: bfloat16 [128, 256, 512], P(('parts', 'gx', 'gy')), parts along dimension 0, may hold values from -6 to 6
- filled_lengths: int32 [128], P(('parts', 'gx', 'gy')), parts along dimension 0, may hold values from 1 to 256
Outputs:
- attn_out: bfloat16 [128, 16384], P(('parts', 'gy'), 'gx'), parts along dimension 0
There are 2 independent parts, one for each index of `parts`. A program takes and returns all parts, laid end to end along the dimension named above; an argument that names none is the same for every part. Nothing has to cross between parts.
All inputs are finite; a program needn't handle non-finite values.
Results may differ from a plain program's by a relative error of at most 0.03.
Values may be sent and summed in bfloat16 or wider, within the bound.
No kernel may reach another device: no remote copies, remote signals or barrier semaphores. Data moves between devices by JAX's collectives and lax.ppermute only.
A program may use at most 128 MiB of HBM per device.

v0:
```python
import jax
import jax.numpy as jnp
from jax import lax
from jax.sharding import PartitionSpec as P

MODEL_WIDTH = 16384
QUERY_HEADS = 64
KEY_VALUE_HEADS = 4
HEAD_SIZE = 128


def rotary_angles(heads, positions):
    half = HEAD_SIZE // 2
    freqs = 500000.0 ** (-(jnp.arange(half, dtype=jnp.float32) * 2.0 / HEAD_SIZE))
    angles = positions.astype(jnp.float32)[:, None, None] * freqs[None, None, :]
    first = heads[..., :half]
    second_factor = heads[..., half:]
    cosine = jnp.cos(angles)
    sine = jnp.sin(angles)
    return jnp.concatenate(
        [first * cosine - second_factor * sine, second_factor * cosine + first * sine], axis=-1
    )


def attend(query_vector, key_rows, value_rows, fresh_key, fresh_value, lengths):
    item_count = query_vector.shape[0]
    slot_positions = key_rows.shape[1]
    group_count = QUERY_HEADS // KEY_VALUE_HEADS
    scale = 1.0 / HEAD_SIZE**0.5
    query_head_rows = query_vector.reshape(item_count, KEY_VALUE_HEADS, group_count, HEAD_SIZE)
    key_head_rows = key_rows.reshape(item_count, slot_positions, KEY_VALUE_HEADS, HEAD_SIZE)
    value_head_rows = value_rows.reshape(item_count, slot_positions, KEY_VALUE_HEADS, HEAD_SIZE)
    scores = (
        jnp.einsum(
            "nkgd,nlkd->nkgl", query_head_rows, key_head_rows, preferred_element_type=jnp.float32
        )
        * scale
    )
    own = (
        jnp.einsum(
            "nkgd,nkd->nkg",
            query_head_rows,
            fresh_key.reshape(item_count, KEY_VALUE_HEADS, HEAD_SIZE),
            preferred_element_type=jnp.float32,
        )
        * scale
    )
    valid = jnp.arange(slot_positions)[None, None, None, :] < lengths[:, None, None, None]
    scores = jnp.where(valid, scores, -1e30)
    top = jnp.maximum(jnp.max(scores, axis=-1), own)
    weights = jnp.where(valid, jnp.exp(scores - top[..., None]), 0.0)
    own_weight = jnp.exp(own - top)
    total = jnp.sum(weights, axis=-1) + own_weight
    rounded = weights.astype(jnp.bfloat16)
    local_rounded = own_weight.astype(jnp.bfloat16).astype(jnp.float32)
    mixed_output = jnp.einsum(
        "nkgl,nlkd->nkgd", rounded, value_head_rows, preferred_element_type=jnp.float32
    )
    mixed_output = mixed_output + local_rounded[..., None] * fresh_value.reshape(
        item_count, KEY_VALUE_HEADS, 1, HEAD_SIZE
    ).astype(jnp.float32)
    return (
        (mixed_output / total[..., None])
        .reshape(item_count, QUERY_HEADS * HEAD_SIZE)
        .astype(jnp.bfloat16)
    )


def per_device(
    hidden_states,
    norm_gain,
    w_query,
    key_weight,
    value_weight,
    w_output,
    stored_key_cache,
    stored_value_cache,
    filled_lengths,
):
    down = lax.axis_size("gy")
    local_share = stored_key_cache.shape[0]
    gathered = lax.all_gather(hidden_states, "gy", axis=0, tiled=True)
    states = gathered.astype(jnp.float32)
    squares = lax.psum(jnp.sum(states * states, axis=1), "gx")
    scaled = (states * norm_gain.astype(jnp.float32)[None, :]).astype(jnp.bfloat16)
    part_query = jnp.dot(scaled, w_query, preferred_element_type=jnp.float32)
    part_key = jnp.dot(scaled, key_weight, preferred_element_type=jnp.float32)
    part_value = jnp.dot(scaled, value_weight, preferred_element_type=jnp.float32)
    summed_query, summed_key, summed_value = (
        lax.psum_scatter(
            part_query.astype(jnp.bfloat16), "gx", scatter_dimension=0, tiled=True
        ).astype(jnp.float32),
        lax.psum_scatter(
            part_key.astype(jnp.bfloat16), "gx", scatter_dimension=0, tiled=True
        ).astype(jnp.float32),
        lax.psum_scatter(
            part_value.astype(jnp.bfloat16), "gx", scatter_dimension=0, tiled=True
        ).astype(jnp.float32),
    )
    query_sum, key_total, value_sum = (
        lax.all_to_all(
            summed_query.astype(jnp.bfloat16), "gy", split_axis=0, concat_axis=1, tiled=True
        ).astype(summed_query.dtype),
        lax.all_to_all(
            summed_key.astype(jnp.bfloat16), "gy", split_axis=0, concat_axis=1, tiled=True
        ).astype(summed_key.dtype),
        lax.all_to_all(
            summed_value.astype(jnp.bfloat16), "gy", split_axis=0, concat_axis=1, tiled=True
        ).astype(summed_value.dtype),
    )
    owner = lax.axis_index("gx") * down + lax.axis_index("gy")
    own_squares = lax.dynamic_slice_in_dim(squares, owner * local_share, local_share, 0)
    row_scaling = lax.rsqrt(own_squares / MODEL_WIDTH + 1e-05)
    query_vector = rotary_angles(
        (row_scaling[:, None] * query_sum).reshape(local_share, QUERY_HEADS, HEAD_SIZE),
        filled_lengths,
    )
    query_vector = query_vector.reshape(local_share, QUERY_HEADS * HEAD_SIZE).astype(jnp.bfloat16)
    fresh_key = rotary_angles(
        (row_scaling[:, None] * key_total).reshape(local_share, KEY_VALUE_HEADS, HEAD_SIZE),
        filled_lengths,
    )
    fresh_key = fresh_key.reshape(local_share, KEY_VALUE_HEADS * HEAD_SIZE).astype(jnp.bfloat16)
    fresh_value = (row_scaling[:, None] * value_sum).astype(jnp.bfloat16)
    attention_result = attend(
        query_vector, stored_key_cache, stored_value_cache, fresh_key, fresh_value, filled_lengths
    )
    head_block = lax.all_to_all(attention_result, "gy", split_axis=1, concat_axis=0, tiled=True)
    all_rows = lax.all_gather(head_block, "gx", axis=0, tiled=True)
    return lax.psum_scatter(
        jnp.dot(all_rows, w_output, preferred_element_type=jnp.float32).astype(jnp.bfloat16),
        "gy",
        scatter_dimension=0,
        tiled=True,
    )


def solution(mesh):
    placed = (
        P(("parts", "gy"), "gx"),
        P("gx"),
        P("gx", "gy"),
        P("gx", "gy"),
        P("gx", "gy"),
        P("gy", "gx"),
        P(("parts", "gx", "gy"), None, None),
        P(("parts", "gx", "gy"), None, None),
        P(("parts", "gx", "gy")),
    )
    return jax.shard_map(
        per_device, mesh=mesh, in_specs=placed, out_specs=P(("parts", "gy"), "gx"), check_vma=False
    )
```

profile of v0, /device:TPU:0, one launch (start us, length us, event | category | flops | bytes accessed | tf_op | source)
XLA Modules:
  0.0 155.9 jit_solution(12715975447384096761)
XLA Ops:
  6.5 0.0 copy-start
  6.5 0.0 copy-start.2
  6.5 0.0 copy-start.1
  6.5 0.0 reduce-scatter.7.cloned.1.call-start
  6.5 17.7 %all_gather.6 = bf16[64,4096]{1,0:T(8,128)(2,1)S(1)} all-gather(bf16[16,4096]{1,0:T(8,128)(2,1)} %param.9), channel_id=1, replica_groups=mesh['parts'=2,'gx'=4,'gy'=4] {'gy'}, dimensions={0}, use_global_device_ids=true | all-gather | bytes 655360 | tf_op jit(solution)/shard_map/all_gather | solution.py:82
  24.2 0.7 convert_element_type.87
  24.9 2.1 %convolution_convert_fusion.3 = bf16[64,128]{1,0:T(8,128)(2,1)} fusion(bf16[4096,128]{1,0:T(8,128)(2,1)} %param.12, bf16[64,4096]{1,0:T(8,128)(2,1)S(1)} %all_gather.6, f32[4096]{0:T(1024)S(1)} %convert_element_type.87), kind=kOutput, calls=%fused_computation.10 | convolution fusion | flops 67903488 | bytes 1605632 | tf_op jit(solution)/shard_map/dot_general | solution.py:87
  27.1 0.0 reduce-scatter.7.cloned.1.call-update
  27.1 0.0 reduce-scatter.9.cloned.1.call-start
  27.2 2.1 %convolution_convert_fusion.2 = bf16[64,128]{1,0:T(8,128)(2,1)} fusion(bf16[4096,128]{1,0:T(8,128)(2,1)} %param.13, bf16[64,4096]{1,0:T(8,128)(2,1)S(1)} %all_gather.6, f32[4096]{0:T(1024)S(1)} %convert_element_type.87), kind=kOutput, calls=%fused_computation.9 | convolution fusion | flops 67903488 | bytes 1605632 | tf_op jit(solution)/shard_map/dot_general | solution.py:88
  29.3 0.0 reduce-scatter.9.cloned.1.call-update
  29.3 0.0 reduce-scatter.5.cloned.1.call-start
  29.4 9.5 %convolution_convert_fusion.1 = bf16[64,2048]{1,0:T(8,128)(2,1)} fusion(bf16[4096,2048]{1,0:T(8,128)(2,1)} %param.11, bf16[64,4096]{1,0:T(8,128)(2,1)S(1)} %all_gather.6, f32[4096]{0:T(1024)S(1)} %convert_element_type.87), kind=kOutput, calls=%fused_computation.1 | convolution fusion | flops 1074659328 | bytes 17580032 | tf_op jit(solution)/shard_map/dot_general | solution.py:86
  38.9 0.0 reduce-scatter.5.cloned.1.call-update
  38.9 0.0 copy-done.2
  39.0 0.1 iota_compare_fusion
  39.0 0.1 multiply_cosine_fusion
  39.1 9.2 %reduce-scatter.7.cloned.1.call-done = bf16[16,128]{1,0:T(8,128)(2,1)} async-done(((bf16[64,128]{1,0:T(8,128)(2,1)}), bf16[16,128]{1,0:T(8,128)(2,1)}) %reduce-scatter.7.cloned.1.call-update) | async-done | bytes 4112 | tf_op jit(solution)/shard_map/reduce_scatter | solution.py:93
  48.3 4.6 %all-to-all-start.1 = ((bf16[4,4,128]{2,1,0:T(4,128)(2,1)}), bf16[4,4,128]{2,1,0:T(4,128)(2,1)S(1)}, u32[]{:S(2)}, u32[]{:S(2)}) async-start(bf16[4,4,128]{2,1,0:T(4,128)(2,1)} %bitcast.45), calls=%async_computation.3 | async-start | bytes 8192 | tf_op jit(solution)/shard_map/all_to_all | solution.py:104
  52.9 0.2 fusion.3
  53.2 6.0 %psum.7 = f32[64]{0:T(128)S(1)} all-reduce(f32[64]{0:T(128)S(1)} %fusion.3), channel_id=1, replica_groups=mesh['parts'=2,'gx'=4,'gy'=4] {'gx'}, use_global_device_ids=true, to_apply=%region_1.0 | all-reduce | flops 64 | bytes 512 | tf_op jit(solution)/shard_map/psum | solution.py:84
  59.1 11.1 %reduce-scatter.9.cloned.1.call-done = bf16[16,128]{1,0:T(8,128)(2,1)} async-done(((bf16[64,128]{1,0:T(8,128)(2,1)}), bf16[16,128]{1,0:T(8,128)(2,1)}) %reduce-scatter.9.cloned.1.call-update) | async-done | bytes 4112 | tf_op jit(solution)/shard_map/reduce_scatter | solution.py:96
  70.2 0.0 all-to-all-done.1
  70.2 4.6 %all-to-all-start.2 = ((bf16[4,4,128]{2,1,0:T(4,128)(2,1)}), bf16[4,4,128]{2,1,0:T(4,128)(2,1)S(1)}, u32[]{:S(2)}, u32[]{:S(2)}) async-start(bf16[4,4,128]{2,1,0:T(4,128)(2,1)} %bitcast.44), calls=%async_computation.5 | async-start | bytes 8192 | tf_op jit(solution)/shard_map/all_to_all | solution.py:107
  74.8 0.1 add_rsqrt_fusion
  74.9 5.5 %all-to-all-done.2 = bf16[4,4,128]{2,1,0:T(4,128)(2,1)S(1)} async-done(((bf16[4,4,128]{2,1,0:T(4,128)(2,1)}), bf16[4,4,128]{2,1,0:T(4,128)(2,1)S(1)}, u32[]{:S(2)}, u32[]{:S(2)}) %all-to-all-start.2) | async-done | bytes 4128 | tf_op jit(solution)/shard_map/all_to_all | solution.py:107
  80.4 0.1 convert_bitcast_fusion.1
  80.5 0.1 subtract_convert_fusion.1
  80.6 12.2 %reduce-scatter.5.cloned.1.call-done = bf16[16,2048]{1,0:T(8,128)(2,1)} async-done(((bf16[64,2048]{1,0:T(8,128)(2,1)}), bf16[16,2048]{1,0:T(8,128)(2,1)}) %reduce-scatter.5.cloned.1.call-update) | async-done | bytes 65552 | tf_op jit(solution)/shard_map/reduce_scatter | solution.py:90
  92.8 1.5 all_to_all.42
  94.3 4.6 %all-to-all-start = ((bf16[4,4,2048]{2,1,0:T(4,128)(2,1)}), bf16[4,4,2048]{2,1,0:T(4,128)(2,1)S(1)}, u32[]{:S(2)}, u32[]{:S(2)}) async-start(bf16[4,4,2048]{2,1,0:T(4,128)(2,1)} %all_to_all.42), calls=%async_computation.1 | async-start | bytes 131072 | tf_op jit(solution)/shard_map/all_to_all | solution.py:101
  98.9 0.0 reduce-scatter.11.cloned.1.call-start
  98.9 0.1 maximum_bitcast_fusion
  99.0 5.7 %all-to-all-done = bf16[4,4,2048]{2,1,0:T(4,128)(2,1)S(1)} async-done(((bf16[4,4,2048]{2,1,0:T(4,128)(2,1)}), bf16[4,4,2048]{2,1,0:T(4,128)(2,1)S(1)}, u32[]{:S(2)}, u32[]{:S(2)}) %all-to-all-start) | async-done | bytes 65568 | tf_op jit(solution)/shard_map/all_to_all | solution.py:101
  104.7 0.1 copy.18
  104.7 0.1 reshape.137
  104.8 0.1 broadcast_multiply_fusion
  104.9 0.1 subtract_convert_fusion
  105.0 0.1 pad_maximum_fusion
  105.1 0.1 fusion.18
  105.3 0.0 copy-done
  105.3 0.5 fusion.22
  105.8 0.2 fusion.12
  106.0 0.0 copy-done.1
  106.0 0.3 fusion.2
  106.4 0.1 copy.22
  106.4 8.1 %all_to_all.55 = bf16[4,4,2048]{2,0,1:T(4,128)(2,1)S(1)} all-to-all(bf16[4,4,2048]{2,0,1:T(4,128)(2,1)S(1)} %copy.22), channel_id=1, replica_groups=mesh['parts'=2,'gx'=4,'gy'=4] {'gy'}, dimensions={1} | all-to-all | bytes 131072 | tf_op jit(solution)/shard_map/all_to_all | solution.py:128
  114.6 5.8 %all_gather.7 = bf16[64,2048]{1,0:T(8,128)(2,1)S(1)} all-gather(bf16[16,2048]{1,0:T(8,128)(2,1)S(1)} %all_to_all.50), channel_id=1, replica_groups=mesh['parts'=2,'gx'=4,'gy'=4] {'gx'}, dimensions={0}, use_global_device_ids=true | all-gather | bytes 327680 | tf_op jit(solution)/shard_map/all_gather | solution.py:129
  120.4 9.6 %convolution_convert_fusion = bf16[64,4096]{1,0:T(8,128)(2,1)} fusion(bf16[64,2048]{1,0:T(8,128)(2,1)S(1)} %all_gather.7, bf16[2048,4096]{1,0:T(8,128)(2,1)} %param.14), kind=kOutput, calls=%fused_computation | convolution fusion | flops 1074003968 | bytes 17563648 | tf_op jit(solution)/shard_map/dot_general | solution.py:131
  129.9 0.0 reduce-scatter.11.cloned.1.call-update
  130.0 19.4 %reduce-scatter.11.cloned.1.call-done = bf16[16,4096]{1,0:T(8,128)(2,1)} async-done(((bf16[64,4096]{1,0:T(8,128)(2,1)}), bf16[16,4096]{1,0:T(8,128)(2,1)}) %reduce-scatter.11.cloned.1.call-update) | async-done | bytes 131088 | tf_op jit(solution)/shard_map/reduce_scatter | solution.py:130
  (8 shorter events, 0.1 us)
Async XLA Ops:
  6.5 98.7 %copy-start = (bf16[4,256,512]{2,1,0:T(8,128)(2,1)S(1)}, bf16[4,256,512]{2,1,0:T(8,128)(2,1)}, u32[]{:S(2)}) copy-start(bf16[4,256,512]{2,1,0:T(8,128)(2,1)} %param.15) | copy-start | bytes 3145732
  6.5 32.4 %copy-start.2 = (s32[4]{0:T(128)S(1)}, s32[4]{0:T(128)}, u32[]{:S(2)}) copy-start(s32[4]{0:T(128)} %param.17) | copy-start | bytes 52
  6.5 99.5 %copy-start.1 = (bf16[4,256,512]{2,1,0:T(8,128)(2,1)S(1)}, bf16[4,256,512]{2,1,0:T(8,128)(2,1)}, u32[]{:S(2)}) copy-start(bf16[4,256,512]{2,1,0:T(8,128)(2,1)} %param.16) | copy-start | bytes 3145732
  6.5 41.8 %reduce-scatter.7.cloned.1.call-start = ((), (), s32[]{:S(2)}) async-start(), calls=%async_computation.9 | async-start | bytes 20480 | tf_op jit(solution)/shard_map/reduce_scatter | solution.py:93
  27.1 43.1 %reduce-scatter.9.cloned.1.call-start = ((), (), s32[]{:S(2)}) async-start(), calls=%async_computation.10 | async-start | bytes 20480 | tf_op jit(solution)/shard_map/reduce_scatter | solution.py:96
  29.3 63.5 %reduce-scatter.5.cloned.1.call-start = ((), (), s32[]{:S(2)}) async-start(), calls=%async_computation.8 | async-start | bytes 327680 | tf_op jit(solution)/shard_map/reduce_scatter | solution.py:90
  48.3 21.9 %all-to-all-start.1 = ((bf16[4,4,128]{2,1,0:T(4,128)(2,1)}), bf16[4,4,128]{2,1,0:T(4,128)(2,1)S(1)}, u32[]{:S(2)}, u32[]{:S(2)}) async-start(bf16[4,4,128]{2,1,0:T(4,128)(2,1)} %bitcast.45), calls=%async_computation.3 | async-start | bytes 8192 | tf_op jit(solution)/shard_map/all_to_all | solution.py:104
  70.2 10.2 %all-to-all-start.2 = ((bf16[4,4,128]{2,1,0:T(4,128)(2,1)}), bf16[4,4,128]{2,1,0:T(4,128)(2,1)S(1)}, u32[]{:S(2)}, u32[]{:S(2)}) async-start(bf16[4,4,128]{2,1,0:T(4,128)(2,1)} %bitcast.44), calls=%async_computation.5 | async-start | bytes 8192 | tf_op jit(solution)/shard_map/all_to_all | solution.py:107
  94.3 10.3 %all-to-all-start = ((bf16[4,4,2048]{2,1,0:T(4,128)(2,1)}), bf16[4,4,2048]{2,1,0:T(4,128)(2,1)S(1)}, u32[]{:S(2)}, u32[]{:S(2)}) async-start(bf16[4,4,2048]{2,1,0:T(4,128)(2,1)} %all_to_all.42), calls=%async_computation.1 | async-start | bytes 131072 | tf_op jit(solution)/shard_map/all_to_all | solution.py:101
  98.9 50.5 %reduce-scatter.11.cloned.1.call-start = ((), (), s32[]{:S(2)}) async-start(), calls=%async_computation.11 | async-start | bytes 655360 | tf_op jit(solution)/shard_map/reduce_scatter | solution.py:130
Sparse Core Ops, SparseCore 0:
  27.2 21.0 reduce-scatter.6
  50.9 19.2 reduce-scatter.8
  72.7 20.0 reduce-scatter.4
  130.1 19.2 reduce-scatter.10
where the time goes:
time: 157 us; the launch traced here: 156 us
  waiting for transfers between devices  63.2 us (40%)
  blocking collectives  37.6 us (24%)
  matrix products  24.3 us (15%)
  starting transfers between devices  13.9 us (9%)
  between operations  13.2 us (8%)
  other arithmetic  1.94 us (1%)
  local copies, waits for them, and re-layouts  1.78 us (1%)
    reduce_scatter x1, waiting for transfers between devices, per_device(): lax.psum_scatter(jnp.dot(all_rows, w_output, preferred_element_type=jnp.f...  19.4 us
    all_gather x1, blocking collectives, per_device(): gathered = lax.all_gather(hidden_states, 'gy', axis=0, tiled=True)  17.7 us
    reduce_scatter x1, waiting for transfers between devices, per_device(): lax.psum_scatter(part_query.astype(jnp.bfloat16), 'gx', scatter_dimension...  12.2 us
    reduce_scatter x1, waiting for transfers between devices, per_device(): lax.psum_scatter(part_value.astype(jnp.bfloat16), 'gx', scatter_dimension...  11.1 us
    dot_general x1, matrix products, per_device(): jnp.dot(all_rows, w_output, preferred_element_type=jnp.float32)  9.59 us
    dot_general x1, matrix products, per_device(): part_query = jnp.dot(scaled, w_query, preferred_element_type=jnp.float32)  9.52 us
    reduce_scatter x1, waiting for transfers between devices, per_device(): lax.psum_scatter(part_key.astype(jnp.bfloat16), 'gx', scatter_dimension=0...  9.2 us
    all_to_all x1, blocking collectives, per_device(): lax.all_to_all(attention_result, 'gy', split_axis=1, concat_axis=0, tiled...  8.11 us
  transfers between devices with their start and end apart: 7, of which 6 were waited for; matrix products, arithmetic and copies ran while one was open for 8% of the time, Pallas kernels for 0%

commit v1 on v0

v1 whole, which is shorter than its diff:
```python
import functools

import jax
import jax.numpy as jnp
from jax import lax
from jax.experimental import pallas as pl
from jax.experimental.pallas import tpu as pltpu
from jax.sharding import PartitionSpec as P

HEAD_SIZE = 128
LANES = 128
EPSILON = 1e-05
VMEM = pl.BlockSpec(memory_space=pltpu.VMEM)


def square_lanes(total):
    high = total.astype(jnp.bfloat16).astype(jnp.float32)
    rest = total - high
    middle = rest.astype(jnp.bfloat16).astype(jnp.float32)
    lane = lax.broadcasted_iota(jnp.int32, (total.shape[0], LANES), 1)
    low = rest - middle
    return jnp.where(lane == 0, high, jnp.where(lane == 1, middle, jnp.where(lane == 2, low, 0.0)))


def project_kernel(count, width, *refs):
    pieces, (gain, w_query, key_weight, value_weight) = refs[:count], refs[count : count + 4]
    outs, (scaled, squares) = refs[count + 4 : 2 * count + 4], refs[2 * count + 4 :]
    flip = lax.axis_index("gx") ^ lax.axis_index("gy")
    gains = gain[...].astype(jnp.float32)
    for offset in range(count):
        states = pieces[offset][...].astype(jnp.float32)
        scaled[flip ^ offset] = (states * gains).astype(jnp.bfloat16)
        squares[flip ^ offset] = square_lanes(jnp.sum(states * states, axis=1, keepdims=True))
    rows = scaled.shape[1]
    left = scaled[...].reshape(count * rows, scaled.shape[2])
    start = 0
    for weight in (w_query, key_weight, value_weight):
        columns = weight.shape[1]
        step = min(columns, 512)
        for first in range(0, columns, step):
            product = jnp.dot(
                left, weight[:, first : first + step], preferred_element_type=jnp.float32
            ).astype(jnp.bfloat16)
            for offset in range(count):
                outs[offset][:, start : start + step] = product[offset * rows : (offset + 1) * rows]
            start += step
    for offset in range(count):
        if start < width - LANES:
            outs[offset][:, start : width - LANES] = jnp.zeros(
                (rows, width - LANES - start), jnp.bfloat16
            )
        outs[offset][:, width - LANES :] = squares[offset].astype(jnp.bfloat16)


def combine_kernel(count, *refs):
    pieces, outs, (held,) = refs[:count], refs[count : 2 * count], refs[2 * count :]
    total = pieces[0][...].astype(jnp.float32)
    for piece in pieces[1:]:
        total = total + piece[...].astype(jnp.float32)
    share = held.shape[1]
    width = total.shape[1]
    squares = square_lanes(jnp.sum(total[:, width - LANES :], axis=1, keepdims=True))
    for owner in range(count):
        rows = slice(owner * share, (owner + 1) * share)
        held[owner, :, : width - LANES] = total[rows, : width - LANES]
        held[owner, :, width - LANES :] = squares[rows]
    me = lax.axis_index("gy")
    for offset in range(count):
        outs[offset][...] = held[me ^ offset].astype(jnp.bfloat16)


def attend_kernel(count, group, features, *refs):
    pieces, (keys, values, cosines, sines, lengths) = refs[:count], refs[count : count + 5]
    outs = refs[count + 5 :]
    share, slots = keys.shape[0], keys.shape[1]
    rows = share * group
    scale = 1.0 / HEAD_SIZE**0.5
    width = pieces[0].shape[1]
    me = lax.axis_index("gy")
    cosine, sine = cosines[...], sines[...]
    squares = jnp.sum(
        pieces[0][:, width - LANES :].astype(jnp.float32), axis=1, keepdims=True
    )
    row_scale = lax.rsqrt(squares / features + EPSILON)
    row_scales = jnp.concatenate([row_scale] * group, axis=0)
    item = lax.broadcasted_iota(jnp.int32, (rows, 1), 0) % share
    valid = lax.broadcasted_iota(jnp.int32, (rows, slots), 1) < lengths[...]
    for offset in range(count):
        piece = pieces[offset][...].astype(jnp.float32)
        head = me ^ offset
        lanes = pl.ds(pl.multiple_of(head * HEAD_SIZE, HEAD_SIZE), HEAD_SIZE)
        query = jnp.concatenate(
            [piece[:, h * HEAD_SIZE : (h + 1) * HEAD_SIZE] for h in range(group)], axis=0
        )
        query = query * row_scales
        query = query * cosine + pltpu.roll(query, HEAD_SIZE // 2, 1) * sine
        query = query.astype(jnp.bfloat16)
        first = group * HEAD_SIZE
        fresh_key = jnp.concatenate([piece[:, first : first + HEAD_SIZE]] * group, axis=0)
        fresh_key = fresh_key * row_scales
        fresh_key = fresh_key * cosine + pltpu.roll(fresh_key, HEAD_SIZE // 2, 1) * sine
        fresh_key = fresh_key.astype(jnp.bfloat16).astype(jnp.float32)
        first = first + HEAD_SIZE
        fresh_value = jnp.concatenate([piece[:, first : first + HEAD_SIZE]] * group, axis=0)
        fresh_value = (fresh_value * row_scales).astype(jnp.bfloat16).astype(jnp.float32)
        own = jnp.sum(query.astype(jnp.float32) * fresh_key, axis=1, keepdims=True) * scale
        scores = jnp.zeros((rows, slots), jnp.float32)
        for n in range(share):
            product = lax.dot_general(
                query,
                keys[n, :, lanes],
                (((1,), (1,)), ((), ())),
                preferred_element_type=jnp.float32,
            )
            scores = jnp.where(item == n, product, scores)
        scores = jnp.where(valid, scores * scale, -1e30)
        top = jnp.maximum(jnp.max(scores, axis=1, keepdims=True), own)
        weights = jnp.where(valid, jnp.exp(scores - top), 0.0)
        own_weight = jnp.exp(own - top)
        total = jnp.sum(weights, axis=1, keepdims=True) + own_weight
        mixed = own_weight.astype(jnp.bfloat16).astype(jnp.float32) * fresh_value
        for n in range(share):
            mixed = mixed + jnp.dot(
                jnp.where(item == n, weights, 0.0).astype(jnp.bfloat16),
                values[n, :, lanes],
                preferred_element_type=jnp.float32,
            )
        mixed = mixed / total
        outs[offset][...] = jnp.concatenate(
            [mixed[h * share : (h + 1) * share] for h in range(group)], axis=1
        ).astype(jnp.bfloat16)


def assemble_kernel(count, *refs):
    pieces, out, held = refs[:count], refs[count], refs[count + 1]
    me = lax.axis_index("gy")
    for offset in range(count):
        held[me ^ offset] = pieces[offset][...].astype(jnp.float32)
    out[...] = jnp.concatenate([held[n] for n in range(count)], axis=0).astype(jnp.bfloat16)


def output_kernel(count, *refs):
    pieces, weight = refs[:count], refs[count]
    outs, (held,) = refs[count + 1 : 2 * count + 1], refs[2 * count + 1 :]
    flip = lax.axis_index("gx") ^ lax.axis_index("gy")
    for offset in range(count):
        held[flip ^ offset] = pieces[offset][...]
    rows = held.shape[1]
    left = held[...].reshape(count * rows, held.shape[2])
    columns = weight.shape[1]
    step = min(columns, 512)
    for first in range(0, columns, step):
        product = jnp.dot(
            left, weight[:, first : first + step], preferred_element_type=jnp.float32
        ).astype(jnp.bfloat16)
        for offset in range(count):
            outs[offset][:, first : first + step] = product[offset * rows : (offset + 1) * rows]


def add_kernel(count, *refs):
    total = refs[0][...].astype(jnp.float32)
    for piece in refs[1:count]:
        total = total + piece[...].astype(jnp.float32)
    refs[count][...] = total.astype(jnp.bfloat16)


def call(kernel, outs, scratch, args, name, limit=None):
    return pl.pallas_call(
        kernel,
        out_shape=outs,
        in_specs=[VMEM] * len(args),
        out_specs=jax.tree.map(lambda _: VMEM, outs),
        scratch_shapes=scratch,
        compiler_params=pltpu.CompilerParams(vmem_limit_bytes=limit),
        name=name,
    )(*args)


def array(shape, dtype=jnp.bfloat16):
    return jax.ShapeDtypeStruct(shape, dtype)


def exchange(pieces, axis):
    count = len(pieces)
    result = list(pieces)
    for offset in range(count - 1, 0, -1):
        result[offset] = lax.ppermute(
            pieces[offset], axis, [(n, n ^ offset) for n in range(count)]
        )
    return result


def per_device(
    hidden_states,
    norm_gain,
    w_query,
    key_weight,
    value_weight,
    w_output,
    stored_key_cache,
    stored_value_cache,
    filled_lengths,
):
    across, down = lax.axis_size("gx"), lax.axis_size("gy")
    assert across == down and across & (across - 1) == 0
    count = down
    share, slots, cache_width = stored_key_cache.shape
    rows, depth = hidden_states.shape
    features = depth * across
    query_columns, key_columns = w_query.shape[1], key_weight.shape[1]
    kv_heads = cache_width // HEAD_SIZE
    group = query_columns * down // HEAD_SIZE // kv_heads
    half = HEAD_SIZE // 2

    with jax.named_scope("gather_hidden"):
        gathered = exchange([hidden_states] * count, "gy")

    with jax.named_scope("angles"):
        freqs = 500000.0 ** (-(jnp.arange(half, dtype=jnp.float32) * 2.0 / HEAD_SIZE))
        angles = filled_lengths.astype(jnp.float32)[:, None] * freqs[None, :]
        cosine, sine = jnp.cos(angles), jnp.sin(angles)
        cosine = jnp.concatenate([cosine, cosine], axis=1)
        sine = jnp.concatenate([-sine, sine], axis=1)

    used = query_columns + 2 * key_columns
    width = -(-used // LANES) * LANES + LANES
    with jax.named_scope("project"):
        partial = call(
            functools.partial(project_kernel, count, width),
            [array((rows, width))] * count,
            [
                pltpu.VMEM((count, rows, depth), jnp.bfloat16),
                pltpu.VMEM((count, rows, LANES), jnp.float32),
            ],
            [
                *gathered,
                norm_gain[None, :],
                *(
                    pltpu.with_memory_space_constraint(w, pltpu.VMEM)
                    for w in (w_query, key_weight, value_weight)
                ),
            ],
            "project",
            40 << 20,
        )
    with jax.named_scope("sum_gx"):
        received = exchange(partial, "gx")
        owned = call(
            functools.partial(combine_kernel, count),
            [array((share, width))] * count,
            [pltpu.VMEM((count, share, width), jnp.float32)],
            received,
            "combine",
        )
    with jax.named_scope("to_owner"):
        owned = exchange(owned, "gy")

    if key_columns == HEAD_SIZE:
        with jax.named_scope("attend"):
            attended = call(
                functools.partial(attend_kernel, count, group, features),
                [array((share, query_columns))] * count,
                [],
                [
                    *owned,
                    stored_key_cache,
                    stored_value_cache,
                    jnp.tile(cosine, (group, 1)),
                    jnp.tile(sine, (group, 1)),
                    jnp.tile(filled_lengths, group)[:, None],
                ],
                "attend",
                24 << 20,
            )
    else:
        with jax.named_scope("attend"):
            attended = attend_narrow(
                owned, used, features, stored_key_cache, stored_value_cache, cosine, sine,
                filled_lengths, query_columns, key_columns,
            )

    with jax.named_scope("to_head_rows"):
        attended = exchange(attended, "gy")
        block = call(
            functools.partial(assemble_kernel, count),
            array((count * share, query_columns)),
            [pltpu.VMEM((count, share, query_columns), jnp.float32)],
            attended,
            "assemble",
        )
    with jax.named_scope("gather_gx"):
        blocks = exchange([block] * count, "gx")
    with jax.named_scope("output"):
        products = call(
            functools.partial(output_kernel, count),
            [array((count * share, w_output.shape[1]))] * count,
            [pltpu.VMEM((count, count * share, query_columns), jnp.bfloat16)],
            [*blocks, pltpu.with_memory_space_constraint(w_output, pltpu.VMEM)],
            "output",
            40 << 20,
        )
    with jax.named_scope("sum_gy"):
        products = exchange(products, "gy")
        return call(
            functools.partial(add_kernel, count),
            array((rows, w_output.shape[1])),
            [],
            products,
            "add",
        )


def attend_narrow(
    owned, used, features, key_rows, value_rows, cosine, sine, lengths, query_columns, key_columns
):
    count = len(owned)
    share, slots, cache_width = key_rows.shape
    kv_heads = cache_width // HEAD_SIZE
    group = query_columns * count // HEAD_SIZE // kv_heads
    me = lax.axis_index("gy")
    order = me ^ jnp.arange(count)
    stacked = jnp.stack(owned).astype(jnp.float32)
    squares = jnp.sum(stacked[0, :, -LANES:], axis=1)
    row_scale = lax.rsqrt(squares / features + EPSILON)[:, None]
    stacked = jnp.take(stacked, order, axis=0)

    def columns(first, size):
        block = stacked[:, :, first : first + size]
        return row_scale * block.transpose(1, 0, 2).reshape(share, count * size)

    def rotary(heads):
        swapped = jnp.concatenate(
            [heads[..., HEAD_SIZE // 2 :], heads[..., : HEAD_SIZE // 2]], axis=-1
        )
        shape = (share,) + (1,) * (heads.ndim - 2) + (HEAD_SIZE,)
        return (heads * cosine.reshape(shape) + swapped * sine.reshape(shape)).astype(jnp.bfloat16)

    query = rotary(columns(0, query_columns).reshape(share, kv_heads, group, HEAD_SIZE))
    fresh_key = rotary(
        columns(query_columns, key_columns).reshape(share, kv_heads, HEAD_SIZE)
    )
    fresh_value = columns(query_columns + key_columns, key_columns).astype(jnp.bfloat16)
    key_heads = key_rows.reshape(share, slots, kv_heads, HEAD_SIZE)
    value_heads = value_rows.reshape(share, slots, kv_heads, HEAD_SIZE)
    scale = 1.0 / HEAD_SIZE**0.5
    scores = scale * jnp.einsum(
        "nkgd,nlkd->nkgl", query, key_heads, preferred_element_type=jnp.float32
    )
    own = scale * jnp.einsum(
        "nkgd,nkd->nkg", query, fresh_key, preferred_element_type=jnp.float32
    )
    valid = jnp.arange(slots)[None, None, None, :] < lengths[:, None, None, None]
    scores = jnp.where(valid, scores, -1e30)
    top = jnp.maximum(jnp.max(scores, axis=-1), own)
    weights = jnp.where(valid, jnp.exp(scores - top[..., None]), 0.0)
    own_weight = jnp.exp(own - top)
    total = jnp.sum(weights, axis=-1) + own_weight
    mixed = jnp.einsum(
        "nkgl,nlkd->nkgd",
        weights.astype(jnp.bfloat16),
        value_heads,
        preferred_element_type=jnp.float32,
    )
    own_weight = own_weight.astype(jnp.bfloat16).astype(jnp.float32)
    mixed = mixed + own_weight[..., None] * fresh_value.reshape(
        share, kv_heads, 1, HEAD_SIZE
    ).astype(jnp.float32)
    mixed = (mixed / total[..., None]).astype(jnp.bfloat16)
    blocks = mixed.reshape(share, count, query_columns).transpose(1, 0, 2)
    blocks = jnp.take(blocks, order, axis=0)
    return [blocks[offset] for offset in range(count)]


def solution(mesh):
    placed = (
        P(("parts", "gy"), "gx"),
        P("gx"),
        P("gx", "gy"),
        P("gx", "gy"),
        P("gx", "gy"),
        P("gy", "gx"),
        P(("parts", "gx", "gy"), None, None),
        P(("parts", "gx", "gy"), None, None),
        P(("parts", "gx", "gy")),
    )
    return jax.shard_map(
        per_device, mesh=mesh, in_specs=placed, out_specs=P(("parts", "gy"), "gx"), check_vma=False
    )
```

time: 157 us -> 93.8 us (0.60)
  blocking collectives: 37.6 us -> 0 us
  waiting for transfers between devices: 63.2 us -> 33.3 us
  matrix products: 24.3 us -> 0 us
  local copies, waits for them, and re-layouts: 1.78 us -> 20.6 us
  Pallas kernels: 0 us -> 16.8 us
  between operations: 13.2 us -> 0.11 us
  starting transfers between devices: 13.9 us -> 21.6 us
    reduce_scatter x4 -> x0, waiting for transfers between devices: 52 us -> none  [the longest x1 19.4 us: per_device(): lax.psum_scatter(jnp.dot(all_rows, w_output, preferred_element_type=jnp.f...]
    ppermute x0 -> x18, waiting for transfers between devices: none -> 33.3 us  [exchange(): lax.ppermute(pieces[offset], axis, [(n, n ^ offset) for n in range(count)])]
    dot_general x7 -> x0, matrix products: 24.3 us -> none  [the longest x1 9.59 us: per_device(): jnp.dot(all_rows, w_output, preferred_element_type=jnp.float32)]
    all_gather x2 -> x0, blocking collectives: 23.5 us -> none  [the longest x1 17.7 us: per_device(): gathered = lax.all_gather(hidden_states, 'gy', axis=0, tiled=True)]
    ppermute x0 -> x18, starting transfers between devices: none -> 21.6 us  [exchange(): lax.ppermute(pieces[offset], axis, [(n, n ^ offset) for n in range(count)])]
    unnamed x6 -> x48, local copies, waits for them, and re-layouts: 0.01 us -> 19.2 us
    pallas_call x0 -> x6, Pallas kernels: none -> 16.8 us  [call(): pl.pallas_call(kernel, out_shape=outs, in_specs=[VMEM] * len(args), out_s...]
    all_to_all x3 -> x0, starting transfers between devices: 13.8 us -> none  [the longest x1 4.6 us: per_device(): lax.all_to_all(summed_query.astype(jnp.bfloat16), 'gy', split_axis=0, con...]
  transfers between devices with their start and end apart: 7 -> 18, of which waited for: 6 -> 13; matrix products, arithmetic and copies ran while one was open for 8% -> 2% of each run, Pallas kernels for 0% -> 0%
where the time goes in v1:
time: 93.8 us; the launch traced here: 93.3 us
  waiting for transfers between devices  33.3 us (36%)
  starting transfers between devices  21.6 us (23%)
  local copies, waits for them, and re-layouts  20.6 us (22%)
  Pallas kernels  16.8 us (18%)
    ppermute x18, waiting for transfers between devices, exchange(): lax.ppermute(pieces[offset], axis, [(n, n ^ offset) for n in range(count)])  33.3 us
    ppermute x18, starting transfers between devices, exchange(): lax.ppermute(pieces[offset], axis, [(n, n ^ offset) for n in range(count)])  21.6 us
    unnamed x48, local copies, waits for them, and re-layouts  19.2 us
    pallas_call x6, Pallas kernels, call(): pl.pallas_call(kernel, out_shape=outs, in_specs=[VMEM] * len(args), out_s...  16.8 us
  transfers between devices with their start and end apart: 18, of which 13 were waited for; matrix products, arithmetic and copies ran while one was open for 2% of the time, Pallas kernels for 0%

profile of v1, /device:TPU:0, one launch (start us, length us, event | category | flops | bytes accessed | tf_op | source)
XLA Modules:
  0.0 93.3 jit_solution(6555384007251121876)
XLA Ops:
  0.0 3.0 %collective-permute-start = (bf16[16,4096]{1,0:T(8,128)(2,1)}, bf16[16,4096]{1,0:T(8,128)(2,1)S(1)}, u32[]{:S(2)}, u32[]{:S(2)}) collective-permute-start(bf16[16,4096]{1,0:T(8,128)(2,1)} %refs_0_.1), channel_id=1, source_target_pairs={{0,1},{1,0},{2,3},{3,2},{4,5},{5,4},{6,7},{7,6},{8,9},{9,8},{10,11... | collective-permute-start | bytes 393224 | tf_op jit(solution)/shard_map/gather_hidden/ppermute | solution.py:187
  3.0 2.6 %collective-permute-start.1 = (bf16[16,4096]{1,0:T(8,128)(2,1)}, bf16[16,4096]{1,0:T(8,128)(2,1)S(1)}, u32[]{:S(2)}, u32[]{:S(2)}) collective-permute-start(bf16[16,4096]{1,0:T(8,128)(2,1)} %refs_0_.1), channel_id=1, source_target_pairs={{0,2},{1,3},{2,0},{3,1},{4,6},{5,7},{6,4},{7,5},{8,10},{9,11},{10,... | collective-permute-start | bytes 393224 | tf_op jit(solution)/shard_map/gather_hidden/ppermute | solution.py:187
  5.6 0.0 collective-permute-start.2
  5.6 1.3 %broadcast_in_dim.2.refs_4_ = bf16[1,4096]{1,0:T(2,128)(2,1)} reshape(bf16[4096]{0:T(1024)(128)(2,1)} %param.10) | data formatting | bytes 16384 | tf_op jit(solution)/shard_map/project/broadcast_in_dim | solution.py:237
  6.9 0.7 convert_element_type.3
  7.6 0.7 collective-permute-done.refs_1_
  8.3 7.9 %collective-permute-done.1.refs_2_ = bf16[16,4096]{1,0:T(8,128)(2,1)S(1)} collective-permute-done((bf16[16,4096]{1,0:T(8,128)(2,1)}, bf16[16,4096]{1,0:T(8,128)(2,1)S(1)}, u32[]{:S(2)}, u32[]{:S(2)}) %collective-permute-start.1) | collective-permute-done | bytes 131104 | tf_op jit(solution)/shard_map/gather_hidden/ppermute | solution.py:187
  16.2 0.0 collective-permute-done.2.refs_3_
  16.2 0.6 copy-done.9
  16.8 0.7 copy-done.10
  17.5 5.8 %copy-done = bf16[4096,2048]{1,0:T(8,128)(2,1)S(1)} copy-done((bf16[4096,2048]{1,0:T(8,128)(2,1)S(1)}, bf16[4096,2048]{1,0:T(8,128)(2,1)}, u32[]{:S(2)}) %copy-start) | copy-done | bytes 16777240
  23.3 1.2 %copy-done.2 = bf16[4096,128]{1,0:T(8,128)(2,1)S(1)} copy-done((bf16[4096,128]{1,0:T(8,128)(2,1)S(1)}, bf16[4096,128]{1,0:T(8,128)(2,1)}, u32[]{:S(2)}) %copy-start.2) | copy-done | bytes 1048600
  24.5 1.2 %copy-done.3 = bf16[4096,128]{1,0:T(8,128)(2,1)S(1)} copy-done((bf16[4096,128]{1,0:T(8,128)(2,1)S(1)}, bf16[4096,128]{1,0:T(8,128)(2,1)}, u32[]{:S(2)}) %copy-start.3) | copy-done | bytes 1048600
  25.7 5.5 %project.1 = (bf16[16,2432]{1,0:T(8,128)(2,1)}, bf16[16,2432]{1,0:T(8,128)(2,1)}, bf16[16,2432]{1,0:T(8,128)(2,1)}, bf16[16,2432]{1,0:T(8,128)(2,1)}) custom-call(bf16[16,4096]{1,0:T(8,128)(2,1)} %refs_0_.1, bf16[16,4096]{1,0:T(8,128)(2,1)} %copy-done.8, bf16[16,4096]{1,0:T(8,128)(2,1)} %copy-done.9, bf16[16,4096]{1,0:T(8,128)(2,1)} %copy-done.10, ...), custom_call_target="tpu_custom_call" | custom-call | tf_op jit(solution)/shard_map/project/project/pallas_call | solution.py:168
  31.2 0.0 collective-permute-start.3
  31.2 1.5 %collective-permute-start.4 = (bf16[16,2432]{1,0:T(8,128)(2,1)}, bf16[16,2432]{1,0:T(8,128)(2,1)S(1)}, u32[]{:S(2)}, u32[]{:S(2)}) collective-permute-start(bf16[16,2432]{1,0:T(8,128)(2,1)} %get-tuple-element.23), channel_id=1, source_target_pairs={{0,8},{4,12},{8,0},{12,4},{1,9},{5,13},{9,1},{13,5},{2,10},{6,14},... | collective-permute-start | bytes 233480 | tf_op jit(solution)/shard_map/sum_gx/ppermute | solution.py:187
  32.7 0.4 collective-permute-start.5
  33.0 0.1 fusion
  33.2 0.0 collective-permute-done.3.refs_1_
  33.2 0.0 copy-start.14
  33.2 3.3 %collective-permute-done.4.refs_2_ = bf16[16,2432]{1,0:T(8,128)(2,1)S(1)} collective-permute-done((bf16[16,2432]{1,0:T(8,128)(2,1)}, bf16[16,2432]{1,0:T(8,128)(2,1)S(1)}, u32[]{:S(2)}, u32[]{:S(2)}) %collective-permute-start.4) | collective-permute-done | bytes 77856 | tf_op jit(solution)/shard_map/sum_gx/ppermute | solution.py:187
  36.5 1.1 %collective-permute-done.5.refs_3_ = bf16[16,2432]{1,0:T(8,128)(2,1)S(1)} collective-permute-done((bf16[16,2432]{1,0:T(8,128)(2,1)}, bf16[16,2432]{1,0:T(8,128)(2,1)S(1)}, u32[]{:S(2)}, u32[]{:S(2)}) %collective-permute-start.5) | collective-permute-done | bytes 77856 | tf_op jit(solution)/shard_map/sum_gx/ppermute | solution.py:187
  37.5 0.0 copy-done.14
  37.6 0.6 copy-done.16
  38.2 1.7 %combine.1 = (bf16[4,2432]{1,0:T(4,128)(2,1)}, bf16[4,2432]{1,0:T(4,128)(2,1)}, bf16[4,2432]{1,0:T(4,128)(2,1)}, bf16[4,2432]{1,0:T(4,128)(2,1)}) custom-call(bf16[16,2432]{1,0:T(8,128)(2,1)} %get-tuple-element.21.refs_0_, bf16[16,2432]{1,0:T(8,128)(2,1)} %copy-done.14, bf16[16,2432]{1,0:T(8,128)(2,1)} %copy-done.15, bf16[16,2432]{1,0:T(8,128)(2,1)} %copy-done.16), custom_call_target="tpu_custom_call" | custom-call | tf_op jit(solution)/shard_map/sum_gx/combine/pallas_call | solution.py:168
  39.9 1.3 %collective-permute-start.6 = (bf16[4,2432]{1,0:T(4,128)(2,1)}, bf16[4,2432]{1,0:T(4,128)(2,1)S(1)}, u32[]{:S(2)}, u32[]{:S(2)}) collective-permute-start(bf16[4,2432]{1,0:T(4,128)(2,1)} %get-tuple-element.26), channel_id=1, source_target_pairs={{0,1},{1,0},{2,3},{3,2},{4,5},{5,4},{6,7},{7,6},{8,9},{9,8},{10,11... | collective-permute-start | bytes 58376 | tf_op jit(solution)/shard_map/to_owner/ppermute | solution.py:187
  41.2 1.5 %collective-permute-start.7 = (bf16[4,2432]{1,0:T(4,128)(2,1)}, bf16[4,2432]{1,0:T(4,128)(2,1)S(1)}, u32[]{:S(2)}, u32[]{:S(2)}) collective-permute-start(bf16[4,2432]{1,0:T(4,128)(2,1)} %get-tuple-element.27), channel_id=1, source_target_pairs={{0,2},{1,3},{2,0},{3,1},{4,6},{5,7},{6,4},{7,5},{8,10},{9,11},{10,... | collective-permute-start | bytes 58376 | tf_op jit(solution)/shard_map/to_owner/ppermute | solution.py:187
  42.8 1.5 %collective-permute-start.8 = (bf16[4,2432]{1,0:T(4,128)(2,1)}, bf16[4,2432]{1,0:T(4,128)(2,1)S(1)}, u32[]{:S(2)}, u32[]{:S(2)}) collective-permute-start(bf16[4,2432]{1,0:T(4,128)(2,1)} %get-tuple-element.28), channel_id=1, source_target_pairs={{0,3},{1,2},{2,1},{3,0},{4,7},{5,6},{6,5},{7,4},{8,11},{9,10},{10,... | collective-permute-start | bytes 58376 | tf_op jit(solution)/shard_map/to_owner/ppermute | solution.py:187
  44.3 0.1 pad_maximum_fusion
  44.4 0.1 tile.33.refs_8_
  44.5 0.0 collective-permute-done.6.refs_1_
  44.5 1.9 %collective-permute-done.7.refs_2_ = bf16[4,2432]{1,0:T(4,128)(2,1)S(1)} collective-permute-done((bf16[4,2432]{1,0:T(4,128)(2,1)}, bf16[4,2432]{1,0:T(4,128)(2,1)S(1)}, u32[]{:S(2)}, u32[]{:S(2)}) %collective-permute-start.7) | collective-permute-done | bytes 19488 | tf_op jit(solution)/shard_map/to_owner/ppermute | solution.py:187
  46.4 2.1 %collective-permute-done.8.refs_3_ = bf16[4,2432]{1,0:T(4,128)(2,1)S(1)} collective-permute-done((bf16[4,2432]{1,0:T(4,128)(2,1)}, bf16[4,2432]{1,0:T(4,128)(2,1)S(1)}, u32[]{:S(2)}, u32[]{:S(2)}) %collective-permute-start.8) | collective-permute-done | bytes 19488 | tf_op jit(solution)/shard_map/to_owner/ppermute | solution.py:187
  48.6 0.7 copy-done.6
  49.3 1.6 %attend.1 = (bf16[4,2048]{1,0:T(4,128)(2,1)S(1)}, bf16[4,2048]{1,0:T(4,128)(2,1)S(1)}, bf16[4,2048]{1,0:T(4,128)(2,1)S(1)}, bf16[4,2048]{1,0:T(4,128)(2,1)S(1)}) custom-call(bf16[4,2432]{1,0:T(4,128)(2,1)S(1)} %copy-done.6, bf16[4,2432]{1,0:T(4,128)(2,1)S(1)} %collective-permute-done.6.refs_1_, bf16[4,2432]{1,0:T(4,128)(2,1)S(1)} %collective-permute-done.7.refs_2_, ...), custom_call_target="tpu_custom_call" | custom-call | tf_op jit(solution)/shard_map/attend/attend/pallas_call | solution.py:168
  50.9 0.0 copy-start.7
  51.0 0.6 copy-done.7
  51.6 0.0 collective-permute-start.10
  51.6 2.0 %collective-permute-start.11 = (bf16[4,2048]{1,0:T(4,128)(2,1)S(1)}, bf16[4,2048]{1,0:T(4,128)(2,1)S(1)}, u32[]{:S(2)}, u32[]{:S(2)}) collective-permute-start(bf16[4,2048]{1,0:T(4,128)(2,1)S(1)} %get-tuple-element.32), channel_id=1, source_target_pairs={{0,3},{1,2},{2,1},{3,0},{4,7},{5,6},{6,5},{7,4},{8,11},{9,10},{10,... | collective-permute-start | bytes 49160 | tf_op jit(solution)/shard_map/to_head_rows/ppermute | solution.py:187
  53.6 1.4 %collective-permute-start.9 = (bf16[4,2048]{1,0:T(4,128)(2,1)S(1)}, bf16[4,2048]{1,0:T(4,128)(2,1)S(1)}, u32[]{:S(2)}, u32[]{:S(2)}) collective-permute-start(bf16[4,2048]{1,0:T(4,128)(2,1)S(1)} %get-tuple-element.30), channel_id=1, source_target_pairs={{0,1},{1,0},{2,3},{3,2},{4,5},{5,4},{6,7},{7,6},{8,9},{9,8},{10,11... | collective-permute-start | bytes 49160 | tf_op jit(solution)/shard_map/to_head_rows/ppermute | solution.py:187
  55.0 1.1 %collective-permute-done.10.refs_2_ = bf16[4,2048]{1,0:T(4,128)(2,1)S(1)} collective-permute-done((bf16[4,2048]{1,0:T(4,128)(2,1)S(1)}, bf16[4,2048]{1,0:T(4,128)(2,1)S(1)}, u32[]{:S(2)}, u32[]{:S(2)}) %collective-permute-start.10) | collective-permute-done | bytes 16416 | tf_op jit(solution)/shard_map/to_head_rows/ppermute | solution.py:187
  56.2 0.9 collective-permute-done.11.refs_3_
  57.1 0.2 collective-permute-done.9.refs_1_
  57.4 0.3 copy-done.21
  57.7 0.3 copy-done.22
  57.9 1.4 %assemble.1.refs_0_ = bf16[16,2048]{1,0:T(8,128)(2,1)} custom-call(bf16[4,2048]{1,0:T(4,128)(2,1)} %copy-done.7, bf16[4,2048]{1,0:T(4,128)(2,1)} %copy-done.22, bf16[4,2048]{1,0:T(4,128)(2,1)} %copy-done.20, bf16[4,2048]{1,0:T(4,128)(2,1)} %copy-done.21), custom_call_target="tpu_custom_call" | custom-call | tf_op jit(solution)/shard_map/to_head_rows/assemble/pallas_call | solution.py:168
  59.4 0.0 collective-permute-start.12
  59.4 1.4 %collective-permute-start.13 = (bf16[16,2048]{1,0:T(8,128)(2,1)}, bf16[16,2048]{1,0:T(8,128)(2,1)S(1)}, u32[]{:S(2)}, u32[]{:S(2)}) collective-permute-start(bf16[16,2048]{1,0:T(8,128)(2,1)} %assemble.1.refs_0_), channel_id=1, source_target_pairs={{0,8},{4,12},{8,0},{12,4},{1,9},{5,13},{9,1},{13,5},{2,10},{6,14},... | collective-permute-start | bytes 196616 | tf_op jit(solution)/shard_map/gather_gx/ppermute | solution.py:187
  60.8 0.5 collective-permute-start.14
  61.2 0.0 collective-permute-done.12.refs_1_
  61.2 3.0 %collective-permute-done.13.refs_2_ = bf16[16,2048]{1,0:T(8,128)(2,1)S(1)} collective-permute-done((bf16[16,2048]{1,0:T(8,128)(2,1)}, bf16[16,2048]{1,0:T(8,128)(2,1)S(1)}, u32[]{:S(2)}, u32[]{:S(2)}) %collective-permute-start.13) | collective-permute-done | bytes 65568 | tf_op jit(solution)/shard_map/gather_gx/ppermute | solution.py:187
  64.2 1.0 %collective-permute-done.14.refs_3_ = bf16[16,2048]{1,0:T(8,128)(2,1)S(1)} collective-permute-done((bf16[16,2048]{1,0:T(8,128)(2,1)}, bf16[16,2048]{1,0:T(8,128)(2,1)S(1)}, u32[]{:S(2)}, u32[]{:S(2)}) %collective-permute-start.14) | collective-permute-done | bytes 65568 | tf_op jit(solution)/shard_map/gather_gx/ppermute | solution.py:187
  65.2 0.6 copy-done.19
  65.8 5.8 %copy-done.1 = bf16[2048,4096]{1,0:T(8,128)(2,1)S(1)} copy-done((bf16[2048,4096]{1,0:T(8,128)(2,1)S(1)}, bf16[2048,4096]{1,0:T(8,128)(2,1)}, u32[]{:S(2)}) %copy-start.1) | copy-done | bytes 16777240
  71.6 4.7 %output.1 = (bf16[16,4096]{1,0:T(8,128)(2,1)}, bf16[16,4096]{1,0:T(8,128)(2,1)}, bf16[16,4096]{1,0:T(8,128)(2,1)}, bf16[16,4096]{1,0:T(8,128)(2,1)}) custom-call(bf16[16,2048]{1,0:T(8,128)(2,1)} %assemble.1.refs_0_, bf16[16,2048]{1,0:T(8,128)(2,1)} %copy-done.17, bf16[16,2048]{1,0:T(8,128)(2,1)} %copy-done.18, bf16[16,2048]{1,0:T(8,128)(2,1)} %copy-done.19, ...), custom_call_target="tpu_custom_call" | custom-call | tf_op jit(solution)/shard_map/output/output/pallas_call | solution.py:168
  76.3 1.4 %collective-permute-start.15 = (bf16[16,4096]{1,0:T(8,128)(2,1)}, bf16[16,4096]{1,0:T(8,128)(2,1)S(1)}, u32[]{:S(2)}, u32[]{:S(2)}) collective-permute-start(bf16[16,4096]{1,0:T(8,128)(2,1)} %get-tuple-element.34), channel_id=1, source_target_pairs={{0,1},{1,0},{2,3},{3,2},{4,5},{5,4},{6,7},{7,6},{8,9},{9,8},{10,11... | collective-permute-start | bytes 393224 | tf_op jit(solution)/shard_map/sum_gy/ppermute | solution.py:187
  77.8 1.1 %collective-permute-start.16 = (bf16[16,4096]{1,0:T(8,128)(2,1)}, bf16[16,4096]{1,0:T(8,128)(2,1)S(1)}, u32[]{:S(2)}, u32[]{:S(2)}) collective-permute-start(bf16[16,4096]{1,0:T(8,128)(2,1)} %get-tuple-element.35), channel_id=1, source_target_pairs={{0,2},{1,3},{2,0},{3,1},{4,6},{5,7},{6,4},{7,5},{8,10},{9,11},{10,... | collective-permute-start | bytes 393224 | tf_op jit(solution)/shard_map/sum_gy/ppermute | solution.py:187
  78.8 1.9 %collective-permute-start.17 = (bf16[16,4096]{1,0:T(8,128)(2,1)}, bf16[16,4096]{1,0:T(8,128)(2,1)S(1)}, u32[]{:S(2)}, u32[]{:S(2)}) collective-permute-start(bf16[16,4096]{1,0:T(8,128)(2,1)} %get-tuple-element.36), channel_id=1, source_target_pairs={{0,3},{1,2},{2,1},{3,0},{4,7},{5,6},{6,5},{7,4},{8,11},{9,10},{10,... | collective-permute-start | bytes 393224 | tf_op jit(solution)/shard_map/sum_gy/ppermute | solution.py:187
  80.7 3.0 %collective-permute-done.15.refs_1_ = bf16[16,4096]{1,0:T(8,128)(2,1)S(1)} collective-permute-done((bf16[16,4096]{1,0:T(8,128)(2,1)}, bf16[16,4096]{1,0:T(8,128)(2,1)S(1)}, u32[]{:S(2)}, u32[]{:S(2)}) %collective-permute-start.15) | collective-permute-done | bytes 131104 | tf_op jit(solution)/shard_map/sum_gy/ppermute | solution.py:187
  83.7 7.1 %collective-permute-done.16.refs_2_ = bf16[16,4096]{1,0:T(8,128)(2,1)S(1)} collective-permute-done((bf16[16,4096]{1,0:T(8,128)(2,1)}, bf16[16,4096]{1,0:T(8,128)(2,1)S(1)}, u32[]{:S(2)}, u32[]{:S(2)}) %collective-permute-start.16) | collective-permute-done | bytes 131104 | tf_op jit(solution)/shard_map/sum_gy/ppermute | solution.py:187
  90.8 0.0 collective-permute-done.17.refs_3_
  90.8 0.6 copy-done.12
  91.4 0.1 copy-done.13
  91.5 1.8 %add.1 = bf16[16,4096]{1,0:T(8,128)(2,1)} custom-call(bf16[16,4096]{1,0:T(8,128)(2,1)} %get-tuple-element.33.refs_0_, bf16[16,4096]{1,0:T(8,128)(2,1)} %copy-done.11, bf16[16,4096]{1,0:T(8,128)(2,1)} %copy-done.12, bf16[16,4096]{1,0:T(8,128)(2,1)} %copy-done.13), custom_call_target="tpu_custom_call" | custom-call | tf_op jit(solution)/shard_map/sum_gy/add/pallas_call | solution.py:168
  (35 shorter events, 0.1 us)
Async XLA Ops:
  0.0 44.4 %copy-start.23 = (s32[4]{0:T(128)S(1)}, s32[4]{0:T(128)}, u32[]{:S(2)}) copy-start(s32[4]{0:T(128)} %param.17) | copy-start | bytes 52
  0.0 8.3 %collective-permute-start = (bf16[16,4096]{1,0:T(8,128)(2,1)}, bf16[16,4096]{1,0:T(8,128)(2,1)S(1)}, u32[]{:S(2)}, u32[]{:S(2)}) collective-permute-start(bf16[16,4096]{1,0:T(8,128)(2,1)} %refs_0_.1), channel_id=1, source_target_pairs={{0,1},{1,0},{2,3},{3,2},{4,5},{5,4},{6,7},{7,6},{8,9},{9,8},{10,11... | collective-permute-start | bytes 393224 | tf_op jit(solution)/shard_map/gather_hidden/ppermute | solution.py:187
  3.0 13.2 %collective-permute-start.1 = (bf16[16,4096]{1,0:T(8,128)(2,1)}, bf16[16,4096]{1,0:T(8,128)(2,1)S(1)}, u32[]{:S(2)}, u32[]{:S(2)}) collective-permute-start(bf16[16,4096]{1,0:T(8,128)(2,1)} %refs_0_.1), channel_id=1, source_target_pairs={{0,2},{1,3},{2,0},{3,1},{4,6},{5,7},{6,4},{7,5},{8,10},{9,11},{10,... | collective-permute-start | bytes 393224 | tf_op jit(solution)/shard_map/gather_hidden/ppermute | solution.py:187
  5.6 10.6 %collective-permute-start.2 = (bf16[16,4096]{1,0:T(8,128)(2,1)}, bf16[16,4096]{1,0:T(8,128)(2,1)S(1)}, u32[]{:S(2)}, u32[]{:S(2)}) collective-permute-start(bf16[16,4096]{1,0:T(8,128)(2,1)} %refs_0_.1), channel_id=1, source_target_pairs={{0,3},{1,2},{2,1},{3,0},{4,7},{5,6},{6,5},{7,4},{8,11},{9,10},{10,... | collective-permute-start | bytes 393224 | tf_op jit(solution)/shard_map/gather_hidden/ppermute | solution.py:187
  8.3 7.9 %copy-start.8 = (bf16[16,4096]{1,0:T(8,128)(2,1)}, bf16[16,4096]{1,0:T(8,128)(2,1)S(1)}, u32[]{:S(2)}) copy-start(bf16[16,4096]{1,0:T(8,128)(2,1)S(1)} %collective-permute-done.refs_1_) | copy-start | bytes 393220
  16.2 0.6 copy-start.9
  16.8 0.7 copy-start.10
  17.5 5.8 %copy-start = (bf16[4096,2048]{1,0:T(8,128)(2,1)S(1)}, bf16[4096,2048]{1,0:T(8,128)(2,1)}, u32[]{:S(2)}) copy-start(bf16[4096,2048]{1,0:T(8,128)(2,1)} %refs_5_.2) | copy-start | bytes 50331652
  23.3 1.2 %copy-start.2 = (bf16[4096,128]{1,0:T(8,128)(2,1)S(1)}, bf16[4096,128]{1,0:T(8,128)(2,1)}, u32[]{:S(2)}) copy-start(bf16[4096,128]{1,0:T(8,128)(2,1)} %refs_6_.1) | copy-start | bytes 3145732
  24.5 1.2 %copy-start.3 = (bf16[4096,128]{1,0:T(8,128)(2,1)S(1)}, bf16[4096,128]{1,0:T(8,128)(2,1)}, u32[]{:S(2)}) copy-start(bf16[4096,128]{1,0:T(8,128)(2,1)} %refs_7_.1) | copy-start | bytes 3145732
  25.7 22.8 %copy-start.4 = (bf16[4,256,512]{2,1,0:T(8,128)(2,1)S(1)}, bf16[4,256,512]{2,1,0:T(8,128)(2,1)}, u32[]{:S(2)}) copy-start(bf16[4,256,512]{2,1,0:T(8,128)(2,1)} %refs_4_.2) | copy-start | bytes 3145732
  25.7 22.9 %copy-start.5 = (bf16[4,256,512]{2,1,0:T(8,128)(2,1)S(1)}, bf16[4,256,512]{2,1,0:T(8,128)(2,1)}, u32[]{:S(2)}) copy-start(bf16[4,256,512]{2,1,0:T(8,128)(2,1)} %refs_5_.3) | copy-start | bytes 3145732
  31.2 2.0 %collective-permute-start.3 = (bf16[16,2432]{1,0:T(8,128)(2,1)}, bf16[16,2432]{1,0:T(8,128)(2,1)S(1)}, u32[]{:S(2)}, u32[]{:S(2)}) collective-permute-start(bf16[16,2432]{1,0:T(8,128)(2,1)} %get-tuple-element.22), channel_id=1, source_target_pairs={{0,4},{4,0},{8,12},{12,8},{1,5},{5,1},{9,13},{13,9},{2,6},{6,2},{1... | collective-permute-start | bytes 233480 | tf_op jit(solution)/shard_map/sum_gx/ppermute | solution.py:187
  31.2 5.3 %collective-permute-start.4 = (bf16[16,2432]{1,0:T(8,128)(2,1)}, bf16[16,2432]{1,0:T(8,128)(2,1)S(1)}, u32[]{:S(2)}, u32[]{:S(2)}) collective-permute-start(bf16[16,2432]{1,0:T(8,128)(2,1)} %get-tuple-element.23), channel_id=1, source_target_pairs={{0,8},{4,12},{8,0},{12,4},{1,9},{5,13},{9,1},{13,5},{2,10},{6,14},... | collective-permute-start | bytes 233480 | tf_op jit(solution)/shard_map/sum_gx/ppermute | solution.py:187
  32.7 4.9 %collective-permute-start.5 = (bf16[16,2432]{1,0:T(8,128)(2,1)}, bf16[16,2432]{1,0:T(8,128)(2,1)S(1)}, u32[]{:S(2)}, u32[]{:S(2)}) collective-permute-start(bf16[16,2432]{1,0:T(8,128)(2,1)} %get-tuple-element.24), channel_id=1, source_target_pairs={{0,12},{4,8},{8,4},{12,0},{1,13},{5,9},{9,5},{13,1},{2,14},{6,10},... | collective-permute-start | bytes 233480 | tf_op jit(solution)/shard_map/sum_gx/ppermute | solution.py:187
  33.2 4.4 %copy-start.14 = (bf16[16,2432]{1,0:T(8,128)(2,1)}, bf16[16,2432]{1,0:T(8,128)(2,1)S(1)}, u32[]{:S(2)}) copy-start(bf16[16,2432]{1,0:T(8,128)(2,1)S(1)} %collective-permute-done.3.refs_1_) | copy-start | bytes 233476
  36.5 1.1 %copy-start.15 = (bf16[16,2432]{1,0:T(8,128)(2,1)}, bf16[16,2432]{1,0:T(8,128)(2,1)S(1)}, u32[]{:S(2)}) copy-start(bf16[16,2432]{1,0:T(8,128)(2,1)S(1)} %collective-permute-done.4.refs_2_) | copy-start | bytes 233476
  37.5 0.6 copy-start.16
  39.9 4.5 %collective-permute-start.6 = (bf16[4,2432]{1,0:T(4,128)(2,1)}, bf16[4,2432]{1,0:T(4,128)(2,1)S(1)}, u32[]{:S(2)}, u32[]{:S(2)}) collective-permute-start(bf16[4,2432]{1,0:T(4,128)(2,1)} %get-tuple-element.26), channel_id=1, source_target_pairs={{0,1},{1,0},{2,3},{3,2},{4,5},{5,4},{6,7},{7,6},{8,9},{9,8},{10,11... | collective-permute-start | bytes 58376 | tf_op jit(solution)/shard_map/to_owner/ppermute | solution.py:187
  41.2 5.2 %collective-permute-start.7 = (bf16[4,2432]{1,0:T(4,128)(2,1)}, bf16[4,2432]{1,0:T(4,128)(2,1)S(1)}, u32[]{:S(2)}, u32[]{:S(2)}) collective-permute-start(bf16[4,2432]{1,0:T(4,128)(2,1)} %get-tuple-element.27), channel_id=1, source_target_pairs={{0,2},{1,3},{2,0},{3,1},{4,6},{5,7},{6,4},{7,5},{8,10},{9,11},{10,... | collective-permute-start | bytes 58376 | tf_op jit(solution)/shard_map/to_owner/ppermute | solution.py:187
  42.8 5.8 %collective-permute-start.8 = (bf16[4,2432]{1,0:T(4,128)(2,1)}, bf16[4,2432]{1,0:T(4,128)(2,1)S(1)}, u32[]{:S(2)}, u32[]{:S(2)}) collective-permute-start(bf16[4,2432]{1,0:T(4,128)(2,1)} %get-tuple-element.28), channel_id=1, source_target_pairs={{0,3},{1,2},{2,1},{3,0},{4,7},{5,6},{6,5},{7,4},{8,11},{9,10},{10,... | collective-permute-start | bytes 58376 | tf_op jit(solution)/shard_map/to_owner/ppermute | solution.py:187
  48.6 0.7 copy-start.6
  50.9 0.6 copy-start.7
  51.6 4.6 %collective-permute-start.10 = (bf16[4,2048]{1,0:T(4,128)(2,1)S(1)}, bf16[4,2048]{1,0:T(4,128)(2,1)S(1)}, u32[]{:S(2)}, u32[]{:S(2)}) collective-permute-start(bf16[4,2048]{1,0:T(4,128)(2,1)S(1)} %get-tuple-element.31), channel_id=1, source_target_pairs={{0,2},{1,3},{2,0},{3,1},{4,6},{5,7},{6,4},{7,5},{8,10},{9,11},{10,... | collective-permute-start | bytes 49160 | tf_op jit(solution)/shard_map/to_head_rows/ppermute | solution.py:187
  51.6 5.5 %collective-permute-start.11 = (bf16[4,2048]{1,0:T(4,128)(2,1)S(1)}, bf16[4,2048]{1,0:T(4,128)(2,1)S(1)}, u32[]{:S(2)}, u32[]{:S(2)}) collective-permute-start(bf16[4,2048]{1,0:T(4,128)(2,1)S(1)} %get-tuple-element.32), channel_id=1, source_target_pairs={{0,3},{1,2},{2,1},{3,0},{4,7},{5,6},{6,5},{7,4},{8,11},{9,10},{10,... | collective-permute-start | bytes 49160 | tf_op jit(solution)/shard_map/to_head_rows/ppermute | solution.py:187
  53.6 3.7 %collective-permute-start.9 = (bf16[4,2048]{1,0:T(4,128)(2,1)S(1)}, bf16[4,2048]{1,0:T(4,128)(2,1)S(1)}, u32[]{:S(2)}, u32[]{:S(2)}) collective-permute-start(bf16[4,2048]{1,0:T(4,128)(2,1)S(1)} %get-tuple-element.30), channel_id=1, source_target_pairs={{0,1},{1,0},{2,3},{3,2},{4,5},{5,4},{6,7},{7,6},{8,9},{9,8},{10,11... | collective-permute-start | bytes 49160 | tf_op jit(solution)/shard_map/to_head_rows/ppermute | solution.py:187
  56.2 1.2 %copy-start.20 = (bf16[4,2048]{1,0:T(4,128)(2,1)}, bf16[4,2048]{1,0:T(4,128)(2,1)S(1)}, u32[]{:S(2)}) copy-start(bf16[4,2048]{1,0:T(4,128)(2,1)S(1)} %collective-permute-done.10.refs_2_) | copy-start | bytes 49156
  57.1 0.6 copy-start.21
  57.3 0.6 copy-start.22
  59.4 1.9 %collective-permute-start.12 = (bf16[16,2048]{1,0:T(8,128)(2,1)}, bf16[16,2048]{1,0:T(8,128)(2,1)S(1)}, u32[]{:S(2)}, u32[]{:S(2)}) collective-permute-start(bf16[16,2048]{1,0:T(8,128)(2,1)} %assemble.1.refs_0_), channel_id=1, source_target_pairs={{0,4},{4,0},{8,12},{12,8},{1,5},{5,1},{9,13},{13,9},{2,6},{6,2},{1... | collective-permute-start | bytes 196616 | tf_op jit(solution)/shard_map/gather_gx/ppermute | solution.py:187
  59.4 4.9 %collective-permute-start.13 = (bf16[16,2048]{1,0:T(8,128)(2,1)}, bf16[16,2048]{1,0:T(8,128)(2,1)S(1)}, u32[]{:S(2)}, u32[]{:S(2)}) collective-permute-start(bf16[16,2048]{1,0:T(8,128)(2,1)} %assemble.1.refs_0_), channel_id=1, source_target_pairs={{0,8},{4,12},{8,0},{12,4},{1,9},{5,13},{9,1},{13,5},{2,10},{6,14},... | collective-permute-start | bytes 196616 | tf_op jit(solution)/shard_map/gather_gx/ppermute | solution.py:187
  60.8 4.4 %collective-permute-start.14 = (bf16[16,2048]{1,0:T(8,128)(2,1)}, bf16[16,2048]{1,0:T(8,128)(2,1)S(1)}, u32[]{:S(2)}, u32[]{:S(2)}) collective-permute-start(bf16[16,2048]{1,0:T(8,128)(2,1)} %assemble.1.refs_0_), channel_id=1, source_target_pairs={{0,12},{4,8},{8,4},{12,0},{1,13},{5,9},{9,5},{13,1},{2,14},{6,10},... | collective-permute-start | bytes 196616 | tf_op jit(solution)/shard_map/gather_gx/ppermute | solution.py:187
  61.2 4.0 %copy-start.17 = (bf16[16,2048]{1,0:T(8,128)(2,1)}, bf16[16,2048]{1,0:T(8,128)(2,1)S(1)}, u32[]{:S(2)}) copy-start(bf16[16,2048]{1,0:T(8,128)(2,1)S(1)} %collective-permute-done.12.refs_1_) | copy-start | bytes 196612
  64.2 1.0 %copy-start.18 = (bf16[16,2048]{1,0:T(8,128)(2,1)}, bf16[16,2048]{1,0:T(8,128)(2,1)S(1)}, u32[]{:S(2)}) copy-start(bf16[16,2048]{1,0:T(8,128)(2,1)S(1)} %collective-permute-done.13.refs_2_) | copy-start | bytes 196612
  65.2 0.6 copy-start.19
  65.8 5.8 %copy-start.1 = (bf16[2048,4096]{1,0:T(8,128)(2,1)S(1)}, bf16[2048,4096]{1,0:T(8,128)(2,1)}, u32[]{:S(2)}) copy-start(bf16[2048,4096]{1,0:T(8,128)(2,1)} %refs_4_.3) | copy-start | bytes 50331652
  76.3 7.4 %collective-permute-start.15 = (bf16[16,4096]{1,0:T(8,128)(2,1)}, bf16[16,4096]{1,0:T(8,128)(2,1)S(1)}, u32[]{:S(2)}, u32[]{:S(2)}) collective-permute-start(bf16[16,4096]{1,0:T(8,128)(2,1)} %get-tuple-element.34), channel_id=1, source_target_pairs={{0,1},{1,0},{2,3},{3,2},{4,5},{5,4},{6,7},{7,6},{8,9},{9,8},{10,11... | collective-permute-start | bytes 393224 | tf_op jit(solution)/shard_map/sum_gy/ppermute | solution.py:187
  77.8 13.0 %collective-permute-start.16 = (bf16[16,4096]{1,0:T(8,128)(2,1)}, bf16[16,4096]{1,0:T(8,128)(2,1)S(1)}, u32[]{:S(2)}, u32[]{:S(2)}) collective-permute-start(bf16[16,4096]{1,0:T(8,128)(2,1)} %get-tuple-element.35), channel_id=1, source_target_pairs={{0,2},{1,3},{2,0},{3,1},{4,6},{5,7},{6,4},{7,5},{8,10},{9,11},{10,... | collective-permute-start | bytes 393224 | tf_op jit(solution)/shard_map/sum_gy/ppermute | solution.py:187
  78.8 11.9 %collective-permute-start.17 = (bf16[16,4096]{1,0:T(8,128)(2,1)}, bf16[16,4096]{1,0:T(8,128)(2,1)S(1)}, u32[]{:S(2)}, u32[]{:S(2)}) collective-permute-start(bf16[16,4096]{1,0:T(8,128)(2,1)} %get-tuple-element.36), channel_id=1, source_target_pairs={{0,3},{1,2},{2,1},{3,0},{4,7},{5,6},{6,5},{7,4},{8,11},{9,10},{10,... | collective-permute-start | bytes 393224 | tf_op jit(solution)/shard_map/sum_gy/ppermute | solution.py:187
  83.7 7.1 %copy-start.11 = (bf16[16,4096]{1,0:T(8,128)(2,1)}, bf16[16,4096]{1,0:T(8,128)(2,1)S(1)}, u32[]{:S(2)}) copy-start(bf16[16,4096]{1,0:T(8,128)(2,1)S(1)} %collective-permute-done.15.refs_1_) | copy-start | bytes 393220
  90.8 0.6 copy-start.12
  90.8 0.7 copy-start.13

commit v2 on v1

--- a/solution.py
+++ b/solution.py
@@ -1,4 +1,5 @@
 import functools
+import math
 
 import jax
 import jax.numpy as jnp
@@ -10,6 +11,8 @@
 HEAD_SIZE = 128
 LANES = 128
 EPSILON = 1e-05
+CUTS = (4,)
+LOADS = len(CUTS) + 1
 VMEM = pl.BlockSpec(memory_space=pltpu.VMEM)
 
 
@@ -23,10 +26,11 @@
 
 
 def project_kernel(count, width, *refs):
-    pieces, (gain, w_query, key_weight, value_weight) = refs[:count], refs[count : count + 4]
+    pieces = [refs[wide_order(count).index(offset)] for offset in range(count)]
+    gain, w_query, key_weight, value_weight = refs[count : count + 4]
     outs, (scaled, squares) = refs[count + 4 : 2 * count + 4], refs[2 * count + 4 :]
     flip = lax.axis_index("gx") ^ lax.axis_index("gy")
-    gains = gain[...].astype(jnp.float32)
+    gains = gain[...].astype(jnp.float32)[None, :]
     for offset in range(count):
         states = pieces[offset][...].astype(jnp.float32)
         scaled[flip ^ offset] = (states * gains).astype(jnp.bfloat16)
@@ -53,7 +57,8 @@
 
 
 def combine_kernel(count, *refs):
-    pieces, outs, (held,) = refs[:count], refs[count : 2 * count], refs[2 * count :]
+    pieces = [refs[wide_order(count).index(offset)] for offset in range(count)]
+    outs, (held,) = refs[count : 2 * count], refs[2 * count :]
     total = pieces[0][...].astype(jnp.float32)
     for piece in pieces[1:]:
         total = total + piece[...].astype(jnp.float32)
@@ -69,8 +74,16 @@
         outs[offset][...] = held[me ^ offset].astype(jnp.bfloat16)
 
 
+def spread(rows, group):
+    repeat = min(group, max(1, 8 // rows.shape[0]))
+    tile = jnp.concatenate([rows] * repeat, axis=0) if repeat > 1 else rows
+    wide = jnp.broadcast_to(tile[None], (group // repeat, *tile.shape))
+    return wide.reshape(group * rows.shape[0], rows.shape[1])
+
+
 def attend_kernel(count, group, features, *refs):
-    pieces, (keys, values, cosines, sines, lengths) = refs[:count], refs[count : count + 5]
+    pieces = [refs[order(count).index(offset)] for offset in range(count)]
+    keys, values, cosines, sines, filled = refs[count : count + 5]
     outs = refs[count + 5 :]
     share, slots = keys.shape[0], keys.shape[1]
     rows = share * group
@@ -82,9 +95,9 @@
         pieces[0][:, width - LANES :].astype(jnp.float32), axis=1, keepdims=True
     )
     row_scale = lax.rsqrt(squares / features + EPSILON)
-    row_scales = jnp.concatenate([row_scale] * group, axis=0)
+    row_scales = spread(row_scale, group)
     item = lax.broadcasted_iota(jnp.int32, (rows, 1), 0) % share
-    valid = lax.broadcasted_iota(jnp.int32, (rows, slots), 1) < lengths[...]
+    valid = lax.broadcasted_iota(jnp.int32, (rows, slots), 1) < filled[:, :1]
     for offset in range(count):
         piece = pieces[offset][...].astype(jnp.float32)
         head = me ^ offset
@@ -96,12 +109,12 @@
         query = query * cosine + pltpu.roll(query, HEAD_SIZE // 2, 1) * sine
         query = query.astype(jnp.bfloat16)
         first = group * HEAD_SIZE
-        fresh_key = jnp.concatenate([piece[:, first : first + HEAD_SIZE]] * group, axis=0)
+        fresh_key = spread(piece[:, first : first + HEAD_SIZE], group)
         fresh_key = fresh_key * row_scales
         fresh_key = fresh_key * cosine + pltpu.roll(fresh_key, HEAD_SIZE // 2, 1) * sine
         fresh_key = fresh_key.astype(jnp.bfloat16).astype(jnp.float32)
         first = first + HEAD_SIZE
-        fresh_value = jnp.concatenate([piece[:, first : first + HEAD_SIZE]] * group, axis=0)
+        fresh_value = spread(piece[:, first : first + HEAD_SIZE], group)
         fresh_value = (fresh_value * row_scales).astype(jnp.bfloat16).astype(jnp.float32)
         own = jnp.sum(query.astype(jnp.float32) * fresh_key, axis=1, keepdims=True) * scale
         scores = jnp.zeros((rows, slots), jnp.float32)
@@ -132,7 +145,8 @@
 
 
 def assemble_kernel(count, *refs):
-    pieces, out, held = refs[:count], refs[count], refs[count + 1]
+    pieces = [refs[order(count).index(offset)] for offset in range(count)]
+    out, held = refs[count], refs[count + 1]
     me = lax.axis_index("gy")
     for offset in range(count):
         held[me ^ offset] = pieces[offset][...].astype(jnp.float32)
@@ -140,19 +154,27 @@
 
 
 def output_kernel(count, *refs):
-    pieces, weight = refs[:count], refs[count]
-    outs, (held,) = refs[count + 1 : 2 * count + 1], refs[2 * count + 1 :]
+    pieces = [refs[wide_order(count).index(offset)] for offset in range(count)]
+    weights = refs[count : count + LOADS]
+    outs, (held,) = refs[count + LOADS : 2 * count + LOADS], refs[2 * count + LOADS :]
     flip = lax.axis_index("gx") ^ lax.axis_index("gy")
     for offset in range(count):
         held[flip ^ offset] = pieces[offset][...]
     rows = held.shape[1]
     left = held[...].reshape(count * rows, held.shape[2])
-    columns = weight.shape[1]
+    columns = weights[0].shape[1]
     step = min(columns, 512)
     for first in range(0, columns, step):
-        product = jnp.dot(
-            left, weight[:, first : first + step], preferred_element_type=jnp.float32
-        ).astype(jnp.bfloat16)
+        product, start = 0.0, 0
+        for weight in weights:
+            depth = weight.shape[0]
+            product = product + jnp.dot(
+                left[:, start : start + depth],
+                weight[:, first : first + step],
+                preferred_element_type=jnp.float32,
+            )
+            start += depth
+        product = product.astype(jnp.bfloat16)
         for offset in range(count):
             outs[offset][:, first : first + step] = product[offset * rows : (offset + 1) * rows]
 
@@ -164,20 +186,76 @@
     refs[count][...] = total.astype(jnp.bfloat16)
 
 
-def call(kernel, outs, scratch, args, name, limit=None):
-    return pl.pallas_call(
-        kernel,
-        out_shape=outs,
-        in_specs=[VMEM] * len(args),
-        out_specs=jax.tree.map(lambda _: VMEM, outs),
-        scratch_shapes=scratch,
-        compiler_params=pltpu.CompilerParams(vmem_limit_bytes=limit),
+def rotary_kernel(share, lengths, cosines, sines, filled):
+    rows = cosines.shape[0]
+    item = lax.broadcasted_iota(jnp.int32, (rows, HEAD_SIZE), 0) % share
+    column = lax.broadcasted_iota(jnp.int32, (rows, HEAD_SIZE), 1)
+    half = HEAD_SIZE // 2
+    length = jnp.zeros((rows, HEAD_SIZE), jnp.int32)
+    for n in range(share):
+        length = jnp.where(item == n, lengths[n], length)
+    power = (column % half).astype(jnp.float32) * (2.0 / HEAD_SIZE)
+    angles = length.astype(jnp.float32) * jnp.exp(-math.log(500000.0) * power)
+    sine = jnp.sin(angles)
+    cosines[...] = jnp.cos(angles)
+    sines[...] = jnp.where(column < half, -sine, sine)
+    filled[...] = length
+
+
+def loading(kernel, loads, counts, *refs):
+    inputs, outputs = counts
+    many = len(loads)
+    sources, refs = refs[:many], refs[many:]
+    if many:
+        targets, sems = refs[inputs + outputs : inputs + outputs + many], refs[-1]
+        refs = refs[: inputs + outputs] + refs[inputs + outputs + many : -1]
+    copies = [
+        pltpu.make_async_copy(sources[n].at[pl.ds(first, rows)], targets[n], sems.at[n])
+        for n, (first, rows) in enumerate(loads)
+    ]
+    for copy in copies:
+        copy.start()
+    if kernel is not None and copies:
+        pl.when(lax.axis_index("gy") >= 0)(lambda: kernel(*refs))
+    elif kernel is not None:
+        kernel(*refs)
+    for copy in copies:
+        copy.wait()
+
+
+def call(kernel, outs, scratch, args, name, limit, scalars=0, loads=(), flops=0):
+    arrays = [pltpu.with_memory_space_constraint(load[0], pltpu.HBM) for load in loads]
+    parts = [load[1:] for load in loads]
+    size = sum(2 * rows * array.shape[1] for array, _, rows in loads)
+    results = pl.pallas_call(
+        functools.partial(loading, kernel, parts, (len(args), len(outs))),
+        out_shape=[*outs, *(pltpu.VMEM((rows, a.shape[1]), a.dtype) for a, _, rows in loads)],
+        in_specs=[pl.BlockSpec(memory_space=pltpu.HBM)] * len(loads)
+        + [VMEM] * (len(args) - scalars)
+        + [pl.BlockSpec(memory_space=pltpu.SMEM)] * scalars,
+        out_specs=[VMEM] * (len(outs) + len(loads)),
+        scratch_shapes=scratch
+        + ([pltpu.SemaphoreType.DMA((len(loads),))] if loads else []),
+        cost_estimate=pl.CostEstimate(
+            flops=flops, bytes_accessed=2 * size + (1 << 16), transcendentals=0
+        ),
+        compiler_params=pltpu.CompilerParams(vmem_limit_bytes=limit << 20),
         name=name,
-    )(*args)
+    )(*arrays, *args)
+    return results[: len(outs)], results[len(outs) :]
 
 
 def array(shape, dtype=jnp.bfloat16):
     return jax.ShapeDtypeStruct(shape, dtype)
+
+
+def order(count):
+    return [0, *range(count - 1, 0, -1)]
+
+
+def wide_order(count):
+    half = count // 2
+    return [0, half, *range(count - 1, half, -1), *range(half - 1, 0, -1)]
 
 
 def exchange(pieces, axis):
@@ -210,22 +288,28 @@
     query_columns, key_columns = w_query.shape[1], key_weight.shape[1]
     kv_heads = cache_width // HEAD_SIZE
     group = query_columns * down // HEAD_SIZE // kv_heads
-    half = HEAD_SIZE // 2
+
+    used = query_columns + 2 * key_columns
+    width = -(-used // LANES) * LANES + LANES
+    out_rows, out_columns = w_output.shape
+    cuts = [out_rows * cut // 8 for cut in CUTS]
 
     with jax.named_scope("gather_hidden"):
         gathered = exchange([hidden_states] * count, "gy")
-
-    with jax.named_scope("angles"):
-        freqs = 500000.0 ** (-(jnp.arange(half, dtype=jnp.float32) * 2.0 / HEAD_SIZE))
-        angles = filled_lengths.astype(jnp.float32)[:, None] * freqs[None, :]
-        cosine, sine = jnp.cos(angles), jnp.sin(angles)
-        cosine = jnp.concatenate([cosine, cosine], axis=1)
-        sine = jnp.concatenate([-sine, sine], axis=1)
-
-    used = query_columns + 2 * key_columns
-    width = -(-used // LANES) * LANES + LANES
+    with jax.named_scope("fetch_query"):
+        table = array((share * group, HEAD_SIZE), jnp.float32)
+        (cosine, sine, filled), weights = call(
+            functools.partial(rotary_kernel, share),
+            [table, table, array(table.shape, jnp.int32)],
+            [],
+            [filled_lengths],
+            "fetch_query",
+            4,
+            scalars=1,
+            loads=[(w_query, 0, depth)],
+        )
     with jax.named_scope("project"):
-        partial = call(
+        partial, output_weights = call(
             functools.partial(project_kernel, count, width),
             [array((rows, width))] * count,
             [
@@ -233,81 +317,95 @@
                 pltpu.VMEM((count, rows, LANES), jnp.float32),
             ],
             [
-                *gathered,
-                norm_gain[None, :],
-                *(
-                    pltpu.with_memory_space_constraint(w, pltpu.VMEM)
-                    for w in (w_query, key_weight, value_weight)
-                ),
+                *(gathered[k] for k in wide_order(count)),
+                norm_gain,
+                *weights,
+                key_weight,
+                value_weight,
             ],
             "project",
-            40 << 20,
+            8,
+            loads=[(w_output, 0, cuts[0])],
+            flops=2 * count * rows * depth * used,
         )
     with jax.named_scope("sum_gx"):
         received = exchange(partial, "gx")
-        owned = call(
+        owned, _ = call(
             functools.partial(combine_kernel, count),
             [array((share, width))] * count,
             [pltpu.VMEM((count, share, width), jnp.float32)],
-            received,
+            [received[k] for k in wide_order(count)],
             "combine",
+            4,
         )
     with jax.named_scope("to_owner"):
         owned = exchange(owned, "gy")
 
-    if key_columns == HEAD_SIZE:
-        with jax.named_scope("attend"):
-            attended = call(
+    with jax.named_scope("attend"):
+        if key_columns == HEAD_SIZE:
+            attended, _ = call(
                 functools.partial(attend_kernel, count, group, features),
                 [array((share, query_columns))] * count,
                 [],
                 [
-                    *owned,
+                    *(owned[k] for k in order(count)),
                     stored_key_cache,
                     stored_value_cache,
-                    jnp.tile(cosine, (group, 1)),
-                    jnp.tile(sine, (group, 1)),
-                    jnp.tile(filled_lengths, group)[:, None],
+                    cosine,
+                    sine,
+                    filled,
                 ],
                 "attend",
-                24 << 20,
-            )
-    else:
-        with jax.named_scope("attend"):
+                8,
+            )
+        else:
             attended = attend_narrow(
-                owned, used, features, stored_key_cache, stored_value_cache, cosine, sine,
-                filled_lengths, query_columns, key_columns,
+                owned, used, features, stored_key_cache, stored_value_cache, cosine[:share],
+                sine[:share], filled_lengths, query_columns, key_columns,
             )
 
     with jax.named_scope("to_head_rows"):
         attended = exchange(attended, "gy")
-        block = call(
+        (block,), _ = call(
             functools.partial(assemble_kernel, count),
-            array((count * share, query_columns)),
+            [array((count * share, query_columns))],
             [pltpu.VMEM((count, share, query_columns), jnp.float32)],
-            attended,
+            [attended[k] for k in order(count)],
             "assemble",
+            4,
         )
     with jax.named_scope("gather_gx"):
         blocks = exchange([block] * count, "gx")
+        _, loaded = call(
+            lambda *refs: None,
+            [],
+            [],
+            [block],
+            "fetch_output",
+            4,
+            loads=[(w_output, cuts[0], out_rows - cuts[0])],
+        )
     with jax.named_scope("output"):
-        products = call(
+        products, _ = call(
             functools.partial(output_kernel, count),
-            [array((count * share, w_output.shape[1]))] * count,
+            [array((count * share, out_columns))] * count,
             [pltpu.VMEM((count, count * share, query_columns), jnp.bfloat16)],
-            [*blocks, pltpu.with_memory_space_constraint(w_output, pltpu.VMEM)],
+            [*(blocks[k] for k in wide_order(count)), *output_weights, *loaded],
             "output",
-            40 << 20,
+            8,
+            flops=2 * count * count * share * out_rows * out_columns,
         )
     with jax.named_scope("sum_gy"):
         products = exchange(products, "gy")
-        return call(
+        (result,), _ = call(
             functools.partial(add_kernel, count),
-            array((rows, w_output.shape[1])),
+            [array((rows, out_columns))],
             [],
-            products,
+            [products[k] for k in wide_order(count)],
             "add",
-        )
+            8,
+        )
+        return result
 
 
 def attend_narrow(

time: 93.8 us -> 64.4 us (0.69)
  local copies, waits for them, and re-layouts: 20.6 us -> 0.68 us
  waiting for transfers between devices: 33.3 us -> 21.3 us
  Pallas kernels: 16.8 us -> 18.8 us
  starting transfers between devices: 21.6 us -> 23.3 us
    unnamed x48 -> x14, local copies, waits for them, and re-layouts: 19.2 us -> 0.68 us
    ppermute x18, waiting for transfers between devices: 33.3 us -> 21.3 us  [exchange(): lax.ppermute(pieces[offset], axis, [(n, n ^ offset) for n in range(count)])]
    pallas_call x6 -> x8, Pallas kernels: 16.8 us -> 18.8 us  [call(): pl.pallas_call(functools.partial(loading, kernel, parts, (len(args), len(...]
    ppermute x18, starting transfers between devices: 21.6 us -> 23.3 us  [exchange(): lax.ppermute(pieces[offset], axis, [(n, n ^ offset) for n in range(count)])]
    broadcast_in_dim x1 -> x0, local copies, waits for them, and re-layouts: 1.31 us -> none  [per_device(): norm_gain[None, :]]
  transfers between devices with their start and end apart: 18 -> 18, of which waited for: 13 -> 10; matrix products, arithmetic and copies ran while one was open for 2% -> 0% of each run, Pallas kernels for 0% -> 15%
where the time goes in v2:
time: 64.4 us; the launch traced here: 64.2 us
  starting transfers between devices  23.3 us (36%)
  waiting for transfers between devices  21.3 us (33%)
  Pallas kernels  18.8 us (29%)
  local copies, waits for them, and re-layouts  0.68 us (1%)
    ppermute x18, starting transfers between devices, exchange(): lax.ppermute(pieces[offset], axis, [(n, n ^ offset) for n in range(count)])  23.3 us
    ppermute x18, waiting for transfers between devices, exchange(): lax.ppermute(pieces[offset], axis, [(n, n ^ offset) for n in range(count)])  21.3 us
    pallas_call x8, Pallas kernels, call(): pl.pallas_call(functools.partial(loading, kernel, parts, (len(args), len(...  18.8 us
  transfers between devices with their start and end apart: 18, of which 10 were waited for; matrix products, arithmetic and copies ran while one was open for 0% of the time, Pallas kernels for 15%

profile of v2, /device:TPU:0, one launch (start us, length us, event | category | flops | bytes accessed | tf_op | source)
XLA Modules:
  0.0 64.2 jit_solution(16537405441211996681)
XLA Ops:
  0.0 0.0 copy-start.4
  0.0 0.0 copy-start.1
  0.0 0.0 copy-start
  0.0 0.0 copy-start.5
  0.0 5.1 %collective-permute-start.1 = (bf16[16,4096]{1,0:T(8,128)(2,1)}, bf16[16,4096]{1,0:T(8,128)(2,1)S(1)}, u32[]{:S(2)}, u32[]{:S(2)}) collective-permute-start(bf16[16,4096]{1,0:T(8,128)(2,1)} %refs_1_.3), channel_id=1, source_target_pairs={{0,3},{1,2},{2,1},{3,0},{4,7},{5,6},{6,5},{7,4},{8,11},{9,10},{10,... | collective-permute-start | bytes 393224 | tf_op jit(solution)/shard_map/gather_hidden/ppermute | solution.py:265
  5.1 0.0 collective-permute-start
  5.1 0.6 collective-permute-start.2
  5.8 0.0 copy-start.6
  5.8 0.7 %copy-done.6 = s32[4]{0:T(128)S(1)} copy-done((s32[4]{0:T(128)S(1)}, s32[4]{0:T(128)}, u32[]{:S(2)}) %copy-start.6) | copy-done | bytes 40
  6.4 6.3 %fetch_query.1 = (f32[64,128]{1,0:T(8,128)S(1)}, f32[64,128]{1,0:T(8,128)S(1)}, s32[64,128]{1,0:T(8,128)S(1)}, bf16[4096,2048]{1,0:T(8,128)(2,1)S(1)}) custom-call(bf16[4096,2048]{1,0:T(8,128)(2,1)} %refs_0_.3, s32[4]{0:T(128)S(1)} %copy-done.6), custom_call_target="tpu_custom_call" | custom-call | bytes 33619968 | tf_op jit(solution)/shard_map/fetch_query/fetch_query/pallas_call | solution.py:230
  12.8 0.0 collective-permute-done.1.refs_3_
  12.8 3.7 %collective-permute-done.refs_2_ = bf16[16,4096]{1,0:T(8,128)(2,1)S(1)} collective-permute-done((bf16[16,4096]{1,0:T(8,128)(2,1)}, bf16[16,4096]{1,0:T(8,128)(2,1)S(1)}, u32[]{:S(2)}, u32[]{:S(2)}) %collective-permute-start) | collective-permute-done | bytes 131104 | tf_op jit(solution)/shard_map/gather_hidden/ppermute | solution.py:265
  16.4 0.0 collective-permute-done.2.refs_4_
  16.4 0.0 copy-done.4
  16.4 0.0 copy-done.1
  16.4 0.0 copy-done
  16.4 0.0 copy-done.5
  16.5 0.0 copy-start.2
  16.5 0.0 copy-start.3
  16.5 3.6 %project.1 = (bf16[16,2432]{1,0:T(8,128)(2,1)S(1)}, bf16[16,2432]{1,0:T(8,128)(2,1)S(1)}, bf16[16,2432]{1,0:T(8,128)(2,1)S(1)}, bf16[16,2432]{1,0:T(8,128)(2,1)S(1)}, bf16[1024,4096]{1,0:T(8,128)(2,1)S(1)}) custom-call(bf16[2048,4096]{1,0:T(8,128)(2,1)} %refs_0_.5, bf16[16,4096]{1,0:T(8,128)(2,1)S(1)} %copy-done.4, ...), custom_call_target="tpu_custom_call" | custom-call | flops 1207959552 | bytes 16842752 | tf_op jit(solution)/shard_map/project/project/pallas_call | solution.py:230
  20.1 1.6 %collective-permute-start.3 = (bf16[16,2432]{1,0:T(8,128)(2,1)S(1)}, bf16[16,2432]{1,0:T(8,128)(2,1)S(1)}, u32[]{:S(2)}, u32[]{:S(2)}) collective-permute-start(bf16[16,2432]{1,0:T(8,128)(2,1)S(1)} %get-tuple-element.28), channel_id=1, source_target_pairs={{0,8},{4,12},{8,0},{12,4},{1,9},{5,13},{9,1},{13,5},{2,10},{6,14},... | collective-permute-start | bytes 233480 | tf_op jit(solution)/shard_map/sum_gx/ppermute | solution.py:265
  21.6 0.0 collective-permute-start.4
  21.6 0.7 %collective-permute-start.5 = (bf16[16,2432]{1,0:T(8,128)(2,1)S(1)}, bf16[16,2432]{1,0:T(8,128)(2,1)S(1)}, u32[]{:S(2)}, u32[]{:S(2)}) collective-permute-start(bf16[16,2432]{1,0:T(8,128)(2,1)S(1)} %get-tuple-element.30), channel_id=1, source_target_pairs={{0,4},{4,0},{8,12},{12,8},{1,5},{5,1},{9,13},{13,9},{2,6},{6,2},{1... | collective-permute-start | bytes 233480 | tf_op jit(solution)/shard_map/sum_gx/ppermute | solution.py:265
  22.3 2.3 %collective-permute-done.3.refs_1_ = bf16[16,2432]{1,0:T(8,128)(2,1)S(1)} collective-permute-done((bf16[16,2432]{1,0:T(8,128)(2,1)S(1)}, bf16[16,2432]{1,0:T(8,128)(2,1)S(1)}, u32[]{:S(2)}, u32[]{:S(2)}) %collective-permute-start.3) | collective-permute-done | bytes 77856 | tf_op jit(solution)/shard_map/sum_gx/ppermute | solution.py:265
  24.5 1.7 %collective-permute-done.4.refs_2_ = bf16[16,2432]{1,0:T(8,128)(2,1)S(1)} collective-permute-done((bf16[16,2432]{1,0:T(8,128)(2,1)S(1)}, bf16[16,2432]{1,0:T(8,128)(2,1)S(1)}, u32[]{:S(2)}, u32[]{:S(2)}) %collective-permute-start.4) | collective-permute-done | bytes 77856 | tf_op jit(solution)/shard_map/sum_gx/ppermute | solution.py:265
  26.2 0.0 collective-permute-done.5.refs_3_
  26.2 0.1 combine.1
  26.3 2.5 %collective-permute-start.6 = (bf16[4,2432]{1,0:T(4,128)(2,1)S(1)}, bf16[4,2432]{1,0:T(4,128)(2,1)S(1)}, u32[]{:S(2)}, u32[]{:S(2)}) collective-permute-start(bf16[4,2432]{1,0:T(4,128)(2,1)S(1)} %get-tuple-element.32), channel_id=1, source_target_pairs={{0,3},{1,2},{2,1},{3,0},{4,7},{5,6},{6,5},{7,4},{8,11},{9,10},{10,... | collective-permute-start | bytes 58376 | tf_op jit(solution)/shard_map/to_owner/ppermute | solution.py:265
  28.9 0.0 collective-permute-start.7
  28.9 1.9 %collective-permute-start.8 = (bf16[4,2432]{1,0:T(4,128)(2,1)S(1)}, bf16[4,2432]{1,0:T(4,128)(2,1)S(1)}, u32[]{:S(2)}, u32[]{:S(2)}) collective-permute-start(bf16[4,2432]{1,0:T(4,128)(2,1)S(1)} %get-tuple-element.34), channel_id=1, source_target_pairs={{0,1},{1,0},{2,3},{3,2},{4,5},{5,4},{6,7},{7,6},{8,9},{9,8},{10,11... | collective-permute-start | bytes 58376 | tf_op jit(solution)/shard_map/to_owner/ppermute | solution.py:265
  30.8 1.2 %collective-permute-done.6.refs_1_ = bf16[4,2432]{1,0:T(4,128)(2,1)S(1)} collective-permute-done((bf16[4,2432]{1,0:T(4,128)(2,1)S(1)}, bf16[4,2432]{1,0:T(4,128)(2,1)S(1)}, u32[]{:S(2)}, u32[]{:S(2)}) %collective-permute-start.6) | collective-permute-done | bytes 19488 | tf_op jit(solution)/shard_map/to_owner/ppermute | solution.py:265
  32.0 1.6 %collective-permute-done.7.refs_2_ = bf16[4,2432]{1,0:T(4,128)(2,1)S(1)} collective-permute-done((bf16[4,2432]{1,0:T(4,128)(2,1)S(1)}, bf16[4,2432]{1,0:T(4,128)(2,1)S(1)}, u32[]{:S(2)}, u32[]{:S(2)}) %collective-permute-start.7) | collective-permute-done | bytes 19488 | tf_op jit(solution)/shard_map/to_owner/ppermute | solution.py:265
  33.5 0.0 collective-permute-done.8.refs_3_
  33.5 0.0 copy-done.2
  33.5 0.0 copy-done.3
  33.5 1.6 %attend.1 = (bf16[4,2048]{1,0:T(4,128)(2,1)S(1)}, bf16[4,2048]{1,0:T(4,128)(2,1)S(1)}, bf16[4,2048]{1,0:T(4,128)(2,1)S(1)}, bf16[4,2048]{1,0:T(4,128)(2,1)S(1)}) custom-call(bf16[4,2432]{1,0:T(4,128)(2,1)S(1)} %get-tuple-element.31.refs_0_, bf16[4,2432]{1,0:T(4,128)(2,1)S(1)} %collective-permute-done.6.refs_1_, ...), custom_call_target="tpu_custom_call" | custom-call | bytes 65536 | tf_op jit(solution)/shard_map/attend/attend/pallas_call | solution.py:230
  35.2 1.6 %collective-permute-start.9 = (bf16[4,2048]{1,0:T(4,128)(2,1)S(1)}, bf16[4,2048]{1,0:T(4,128)(2,1)S(1)}, u32[]{:S(2)}, u32[]{:S(2)}) collective-permute-start(bf16[4,2048]{1,0:T(4,128)(2,1)S(1)} %get-tuple-element.39), channel_id=1, source_target_pairs={{0,3},{1,2},{2,1},{3,0},{4,7},{5,6},{6,5},{7,4},{8,11},{9,10},{10,... | collective-permute-start | bytes 49160 | tf_op jit(solution)/shard_map/to_head_rows/ppermute | solution.py:265
  36.8 0.9 %collective-permute-start.10 = (bf16[4,2048]{1,0:T(4,128)(2,1)S(1)}, bf16[4,2048]{1,0:T(4,128)(2,1)S(1)}, u32[]{:S(2)}, u32[]{:S(2)}) collective-permute-start(bf16[4,2048]{1,0:T(4,128)(2,1)S(1)} %get-tuple-element.40), channel_id=1, source_target_pairs={{0,2},{1,3},{2,0},{3,1},{4,6},{5,7},{6,4},{7,5},{8,10},{9,11},{10,... | collective-permute-start | bytes 49160 | tf_op jit(solution)/shard_map/to_head_rows/ppermute | solution.py:265
  37.7 1.9 %collective-permute-start.11 = (bf16[4,2048]{1,0:T(4,128)(2,1)S(1)}, bf16[4,2048]{1,0:T(4,128)(2,1)S(1)}, u32[]{:S(2)}, u32[]{:S(2)}) collective-permute-start(bf16[4,2048]{1,0:T(4,128)(2,1)S(1)} %get-tuple-element.41), channel_id=1, source_target_pairs={{0,1},{1,0},{2,3},{3,2},{4,5},{5,4},{6,7},{7,6},{8,9},{9,8},{10,11... | collective-permute-start | bytes 49160 | tf_op jit(solution)/shard_map/to_head_rows/ppermute | solution.py:265
  39.6 1.1 %collective-permute-done.9.refs_1_ = bf16[4,2048]{1,0:T(4,128)(2,1)S(1)} collective-permute-done((bf16[4,2048]{1,0:T(4,128)(2,1)S(1)}, bf16[4,2048]{1,0:T(4,128)(2,1)S(1)}, u32[]{:S(2)}, u32[]{:S(2)}) %collective-permute-start.9) | collective-permute-done | bytes 16416 | tf_op jit(solution)/shard_map/to_head_rows/ppermute | solution.py:265
  40.8 0.7 %collective-permute-done.10.refs_2_ = bf16[4,2048]{1,0:T(4,128)(2,1)S(1)} collective-permute-done((bf16[4,2048]{1,0:T(4,128)(2,1)S(1)}, bf16[4,2048]{1,0:T(4,128)(2,1)S(1)}, u32[]{:S(2)}, u32[]{:S(2)}) %collective-permute-start.10) | collective-permute-done | bytes 16416 | tf_op jit(solution)/shard_map/to_head_rows/ppermute | solution.py:265
  41.5 0.2 collective-permute-done.11.refs_3_
  41.7 0.1 collective-permute-start.14
  41.7 0.8 %collective-permute-start.13 = (bf16[16,2048]{1,0:T(8,128)(2,1)S(1)}, bf16[16,2048]{1,0:T(8,128)(2,1)S(1)}, u32[]{:S(2)}, u32[]{:S(2)}) collective-permute-start(bf16[16,2048]{1,0:T(8,128)(2,1)S(1)} %assemble.1.refs_1_.refs_0_), channel_id=1, source_target_pairs={{0,12},{4,8},{8,4},{12,0},{1,13},{5,9},{9,5},{13,1},{2,14},{6,10},... | collective-permute-start | bytes 196616 | tf_op jit(solution)/shard_map/gather_gx/ppermute | solution.py:265
  42.6 1.3 %collective-permute-start.12 = (bf16[16,2048]{1,0:T(8,128)(2,1)S(1)}, bf16[16,2048]{1,0:T(8,128)(2,1)S(1)}, u32[]{:S(2)}, u32[]{:S(2)}) collective-permute-start(bf16[16,2048]{1,0:T(8,128)(2,1)S(1)} %assemble.1.refs_1_.refs_0_), channel_id=1, source_target_pairs={{0,8},{4,12},{8,0},{12,4},{1,9},{5,13},{9,1},{13,5},{2,10},{6,14},... | collective-permute-start | bytes 196616 | tf_op jit(solution)/shard_map/gather_gx/ppermute | solution.py:265
  43.9 3.4 %fetch_output.1.refs_5_ = bf16[1024,4096]{1,0:T(8,128)(2,1)S(1)} custom-call(bf16[2048,4096]{1,0:T(8,128)(2,1)} %refs_0_.5, bf16[16,2048]{1,0:T(8,128)(2,1)S(1)} %assemble.1.refs_1_.refs_0_), custom_call_target="tpu_custom_call" | custom-call | bytes 16842752 | tf_op jit(solution)/shard_map/gather_gx/fetch_output/pallas_call | solution.py:230
  47.3 0.0 collective-permute-done.14.refs_3_
  47.3 0.0 collective-permute-done.13.refs_2_
  47.3 0.3 collective-permute-done.12.refs_1_
  47.6 3.0 %output.1 = (bf16[16,4096]{1,0:T(8,128)(2,1)S(1)}, bf16[16,4096]{1,0:T(8,128)(2,1)S(1)}, bf16[16,4096]{1,0:T(8,128)(2,1)S(1)}, bf16[16,4096]{1,0:T(8,128)(2,1)S(1)}) custom-call(bf16[16,2048]{1,0:T(8,128)(2,1)S(1)} %assemble.1.refs_1_.refs_0_, bf16[16,2048]{1,0:T(8,128)(2,1)S(1)} %collective-permute-done.12.refs_1_, ...), custom_call_target="tpu_custom_call" | custom-call | flops 1073741824 | bytes 65536 | tf_op jit(solution)/shard_map/output/output/pallas_call | solution.py:230
  50.6 1.9 %collective-permute-start.15 = (bf16[16,4096]{1,0:T(8,128)(2,1)S(1)}, bf16[16,4096]{1,0:T(8,128)(2,1)S(1)}, u32[]{:S(2)}, u32[]{:S(2)}) collective-permute-start(bf16[16,4096]{1,0:T(8,128)(2,1)S(1)} %get-tuple-element.44), channel_id=1, source_target_pairs={{0,2},{1,3},{2,0},{3,1},{4,6},{5,7},{6,4},{7,5},{8,10},{9,11},{10,... | collective-permute-start | bytes 393224 | tf_op jit(solution)/shard_map/sum_gy/ppermute | solution.py:265
  52.5 2.3 %collective-permute-start.16 = (bf16[16,4096]{1,0:T(8,128)(2,1)S(1)}, bf16[16,4096]{1,0:T(8,128)(2,1)S(1)}, u32[]{:S(2)}, u32[]{:S(2)}) collective-permute-start(bf16[16,4096]{1,0:T(8,128)(2,1)S(1)} %get-tuple-element.45), channel_id=1, source_target_pairs={{0,3},{1,2},{2,1},{3,0},{4,7},{5,6},{6,5},{7,4},{8,11},{9,10},{10,... | collective-permute-start | bytes 393224 | tf_op jit(solution)/shard_map/sum_gy/ppermute | solution.py:265
  54.8 0.0 collective-permute-start.17
  54.8 8.7 %collective-permute-done.15.refs_1_ = bf16[16,4096]{1,0:T(8,128)(2,1)S(1)} collective-permute-done((bf16[16,4096]{1,0:T(8,128)(2,1)S(1)}, bf16[16,4096]{1,0:T(8,128)(2,1)S(1)}, u32[]{:S(2)}, u32[]{:S(2)}) %collective-permute-start.15) | collective-permute-done | bytes 131104 | tf_op jit(solution)/shard_map/sum_gy/ppermute | solution.py:265
  63.5 0.0 collective-permute-done.16.refs_2_
  63.5 0.0 collective-permute-done.17.refs_3_
  63.5 0.7 %add.1 = bf16[16,4096]{1,0:T(8,128)(2,1)} custom-call(bf16[16,4096]{1,0:T(8,128)(2,1)S(1)} %get-tuple-element.43.refs_0_, bf16[16,4096]{1,0:T(8,128)(2,1)S(1)} %collective-permute-done.15.refs_1_, bf16[16,4096]{1,0:T(8,128)(2,1)S(1)} %collective-permute-done.16.refs_2_, bf16[16,4096]{1,0:T(8,128)(2,1)S(1)} %collective-permute-done.17.refs_3_), custom_call_target="tpu_custom_call" | custom-call | bytes 65536 | tf_op jit(solution)/shard_map/sum_gy/add/pallas_call | solution.py:230
  (1 shorter events, 0.0 us)
Async XLA Ops:
  0.0 16.4 %copy-start.4 = (bf16[16,4096]{1,0:T(8,128)(2,1)S(1)}, bf16[16,4096]{1,0:T(8,128)(2,1)}, u32[]{:S(2)}) copy-start(bf16[16,4096]{1,0:T(8,128)(2,1)} %refs_1_.3) | copy-start | bytes 393220
  0.0 16.4 %copy-start.1 = (bf16[4096,128]{1,0:T(8,128)(2,1)S(1)}, bf16[4096,128]{1,0:T(8,128)(2,1)}, u32[]{:S(2)}) copy-start(bf16[4096,128]{1,0:T(8,128)(2,1)} %refs_8_.1) | copy-start | bytes 3145732
  0.0 16.4 %copy-start = (bf16[4096,128]{1,0:T(8,128)(2,1)S(1)}, bf16[4096,128]{1,0:T(8,128)(2,1)}, u32[]{:S(2)}) copy-start(bf16[4096,128]{1,0:T(8,128)(2,1)} %refs_7_.1) | copy-start | bytes 3145732
  0.0 16.4 %copy-start.5 = (bf16[4096]{0:T(1024)(128)(2,1)S(1)}, bf16[4096]{0:T(1024)(128)(2,1)}, u32[]{:S(2)}) copy-start(bf16[4096]{0:T(1024)(128)(2,1)} %refs_5_.2) | copy-start | bytes 24580
  0.0 12.8 %collective-permute-start.1 = (bf16[16,4096]{1,0:T(8,128)(2,1)}, bf16[16,4096]{1,0:T(8,128)(2,1)S(1)}, u32[]{:S(2)}, u32[]{:S(2)}) collective-permute-start(bf16[16,4096]{1,0:T(8,128)(2,1)} %refs_1_.3), channel_id=1, source_target_pairs={{0,3},{1,2},{2,1},{3,0},{4,7},{5,6},{6,5},{7,4},{8,11},{9,10},{10,... | collective-permute-start | bytes 393224 | tf_op jit(solution)/shard_map/gather_hidden/ppermute | solution.py:265
  5.1 11.3 %collective-permute-start = (bf16[16,4096]{1,0:T(8,128)(2,1)}, bf16[16,4096]{1,0:T(8,128)(2,1)S(1)}, u32[]{:S(2)}, u32[]{:S(2)}) collective-permute-start(bf16[16,4096]{1,0:T(8,128)(2,1)} %refs_1_.3), channel_id=1, source_target_pairs={{0,2},{1,3},{2,0},{3,1},{4,6},{5,7},{6,4},{7,5},{8,10},{9,11},{10,... | collective-permute-start | bytes 393224 | tf_op jit(solution)/shard_map/gather_hidden/ppermute | solution.py:265
  5.1 11.3 %collective-permute-start.2 = (bf16[16,4096]{1,0:T(8,128)(2,1)}, bf16[16,4096]{1,0:T(8,128)(2,1)S(1)}, u32[]{:S(2)}, u32[]{:S(2)}) collective-permute-start(bf16[16,4096]{1,0:T(8,128)(2,1)} %refs_1_.3), channel_id=1, source_target_pairs={{0,1},{1,0},{2,3},{3,2},{4,5},{5,4},{6,7},{7,6},{8,9},{9,8},{10,11... | collective-permute-start | bytes 393224 | tf_op jit(solution)/shard_map/gather_hidden/ppermute | solution.py:265
  5.8 0.7 %copy-start.6 = (s32[4]{0:T(128)S(1)}, s32[4]{0:T(128)}, u32[]{:S(2)}) copy-start(s32[4]{0:T(128)} %refs_1_.2) | copy-start | bytes 52
  16.5 17.1 %copy-start.2 = (bf16[4,256,512]{2,1,0:T(8,128)(2,1)S(1)}, bf16[4,256,512]{2,1,0:T(8,128)(2,1)}, u32[]{:S(2)}) copy-start(bf16[4,256,512]{2,1,0:T(8,128)(2,1)} %refs_4_.1) | copy-start | bytes 3145732
  16.5 17.1 %copy-start.3 = (bf16[4,256,512]{2,1,0:T(8,128)(2,1)S(1)}, bf16[4,256,512]{2,1,0:T(8,128)(2,1)}, u32[]{:S(2)}) copy-start(bf16[4,256,512]{2,1,0:T(8,128)(2,1)} %refs_5_.3) | copy-start | bytes 3145732
  20.1 4.5 %collective-permute-start.3 = (bf16[16,2432]{1,0:T(8,128)(2,1)S(1)}, bf16[16,2432]{1,0:T(8,128)(2,1)S(1)}, u32[]{:S(2)}, u32[]{:S(2)}) collective-permute-start(bf16[16,2432]{1,0:T(8,128)(2,1)S(1)} %get-tuple-element.28), channel_id=1, source_target_pairs={{0,8},{4,12},{8,0},{12,4},{1,9},{5,13},{9,1},{13,5},{2,10},{6,14},... | collective-permute-start | bytes 233480 | tf_op jit(solution)/shard_map/sum_gx/ppermute | solution.py:265
  21.6 4.6 %collective-permute-start.4 = (bf16[16,2432]{1,0:T(8,128)(2,1)S(1)}, bf16[16,2432]{1,0:T(8,128)(2,1)S(1)}, u32[]{:S(2)}, u32[]{:S(2)}) collective-permute-start(bf16[16,2432]{1,0:T(8,128)(2,1)S(1)} %get-tuple-element.29), channel_id=1, source_target_pairs={{0,12},{4,8},{8,4},{12,0},{1,13},{5,9},{9,5},{13,1},{2,14},{6,10},... | collective-permute-start | bytes 233480 | tf_op jit(solution)/shard_map/sum_gx/ppermute | solution.py:265
  21.6 4.6 %collective-permute-start.5 = (bf16[16,2432]{1,0:T(8,128)(2,1)S(1)}, bf16[16,2432]{1,0:T(8,128)(2,1)S(1)}, u32[]{:S(2)}, u32[]{:S(2)}) collective-permute-start(bf16[16,2432]{1,0:T(8,128)(2,1)S(1)} %get-tuple-element.30), channel_id=1, source_target_pairs={{0,4},{4,0},{8,12},{12,8},{1,5},{5,1},{9,13},{13,9},{2,6},{6,2},{1... | collective-permute-start | bytes 233480 | tf_op jit(solution)/shard_map/sum_gx/ppermute | solution.py:265
  26.3 5.6 %collective-permute-start.6 = (bf16[4,2432]{1,0:T(4,128)(2,1)S(1)}, bf16[4,2432]{1,0:T(4,128)(2,1)S(1)}, u32[]{:S(2)}, u32[]{:S(2)}) collective-permute-start(bf16[4,2432]{1,0:T(4,128)(2,1)S(1)} %get-tuple-element.32), channel_id=1, source_target_pairs={{0,3},{1,2},{2,1},{3,0},{4,7},{5,6},{6,5},{7,4},{8,11},{9,10},{10,... | collective-permute-start | bytes 58376 | tf_op jit(solution)/shard_map/to_owner/ppermute | solution.py:265
  28.9 4.7 %collective-permute-start.7 = (bf16[4,2432]{1,0:T(4,128)(2,1)S(1)}, bf16[4,2432]{1,0:T(4,128)(2,1)S(1)}, u32[]{:S(2)}, u32[]{:S(2)}) collective-permute-start(bf16[4,2432]{1,0:T(4,128)(2,1)S(1)} %get-tuple-element.33), channel_id=1, source_target_pairs={{0,2},{1,3},{2,0},{3,1},{4,6},{5,7},{6,4},{7,5},{8,10},{9,11},{10,... | collective-permute-start | bytes 58376 | tf_op jit(solution)/shard_map/to_owner/ppermute | solution.py:265
  28.9 4.7 %collective-permute-start.8 = (bf16[4,2432]{1,0:T(4,128)(2,1)S(1)}, bf16[4,2432]{1,0:T(4,128)(2,1)S(1)}, u32[]{:S(2)}, u32[]{:S(2)}) collective-permute-start(bf16[4,2432]{1,0:T(4,128)(2,1)S(1)} %get-tuple-element.34), channel_id=1, source_target_pairs={{0,1},{1,0},{2,3},{3,2},{4,5},{5,4},{6,7},{7,6},{8,9},{9,8},{10,11... | collective-permute-start | bytes 58376 | tf_op jit(solution)/shard_map/to_owner/ppermute | solution.py:265
  35.2 5.6 %collective-permute-start.9 = (bf16[4,2048]{1,0:T(4,128)(2,1)S(1)}, bf16[4,2048]{1,0:T(4,128)(2,1)S(1)}, u32[]{:S(2)}, u32[]{:S(2)}) collective-permute-start(bf16[4,2048]{1,0:T(4,128)(2,1)S(1)} %get-tuple-element.39), channel_id=1, source_target_pairs={{0,3},{1,2},{2,1},{3,0},{4,7},{5,6},{6,5},{7,4},{8,11},{9,10},{10,... | collective-permute-start | bytes 49160 | tf_op jit(solution)/shard_map/to_head_rows/ppermute | solution.py:265
  36.8 4.6 %collective-permute-start.10 = (bf16[4,2048]{1,0:T(4,128)(2,1)S(1)}, bf16[4,2048]{1,0:T(4,128)(2,1)S(1)}, u32[]{:S(2)}, u32[]{:S(2)}) collective-permute-start(bf16[4,2048]{1,0:T(4,128)(2,1)S(1)} %get-tuple-element.40), channel_id=1, source_target_pairs={{0,2},{1,3},{2,0},{3,1},{4,6},{5,7},{6,4},{7,5},{8,10},{9,11},{10,... | collective-permute-start | bytes 49160 | tf_op jit(solution)/shard_map/to_head_rows/ppermute | solution.py:265
  37.7 3.9 %collective-permute-start.11 = (bf16[4,2048]{1,0:T(4,128)(2,1)S(1)}, bf16[4,2048]{1,0:T(4,128)(2,1)S(1)}, u32[]{:S(2)}, u32[]{:S(2)}) collective-permute-start(bf16[4,2048]{1,0:T(4,128)(2,1)S(1)} %get-tuple-element.41), channel_id=1, source_target_pairs={{0,1},{1,0},{2,3},{3,2},{4,5},{5,4},{6,7},{7,6},{8,9},{9,8},{10,11... | collective-permute-start | bytes 49160 | tf_op jit(solution)/shard_map/to_head_rows/ppermute | solution.py:265
  41.7 5.6 %collective-permute-start.14 = (bf16[16,2048]{1,0:T(8,128)(2,1)S(1)}, bf16[16,2048]{1,0:T(8,128)(2,1)S(1)}, u32[]{:S(2)}, u32[]{:S(2)}) collective-permute-start(bf16[16,2048]{1,0:T(8,128)(2,1)S(1)} %assemble.1.refs_1_.refs_0_), channel_id=1, source_target_pairs={{0,4},{4,0},{8,12},{12,8},{1,5},{5,1},{9,13},{13,9},{2,6},{6,2},{1... | collective-permute-start | bytes 196616 | tf_op jit(solution)/shard_map/gather_gx/ppermute | solution.py:265
  41.7 5.6 %collective-permute-start.13 = (bf16[16,2048]{1,0:T(8,128)(2,1)S(1)}, bf16[16,2048]{1,0:T(8,128)(2,1)S(1)}, u32[]{:S(2)}, u32[]{:S(2)}) collective-permute-start(bf16[16,2048]{1,0:T(8,128)(2,1)S(1)} %assemble.1.refs_1_.refs_0_), channel_id=1, source_target_pairs={{0,12},{4,8},{8,4},{12,0},{1,13},{5,9},{9,5},{13,1},{2,14},{6,10},... | collective-permute-start | bytes 196616 | tf_op jit(solution)/shard_map/gather_gx/ppermute | solution.py:265
  42.6 5.0 %collective-permute-start.12 = (bf16[16,2048]{1,0:T(8,128)(2,1)S(1)}, bf16[16,2048]{1,0:T(8,128)(2,1)S(1)}, u32[]{:S(2)}, u32[]{:S(2)}) collective-permute-start(bf16[16,2048]{1,0:T(8,128)(2,1)S(1)} %assemble.1.refs_1_.refs_0_), channel_id=1, source_target_pairs={{0,8},{4,12},{8,0},{12,4},{1,9},{5,13},{9,1},{13,5},{2,10},{6,14},... | collective-permute-start | bytes 196616 | tf_op jit(solution)/shard_map/gather_gx/ppermute | solution.py:265
  50.6 12.9 %collective-permute-start.15 = (bf16[16,4096]{1,0:T(8,128)(2,1)S(1)}, bf16[16,4096]{1,0:T(8,128)(2,1)S(1)}, u32[]{:S(2)}, u32[]{:S(2)}) collective-permute-start(bf16[16,4096]{1,0:T(8,128)(2,1)S(1)} %get-tuple-element.44), channel_id=1, source_target_pairs={{0,2},{1,3},{2,0},{3,1},{4,6},{5,7},{6,4},{7,5},{8,10},{9,11},{10,... | collective-permute-start | bytes 393224 | tf_op jit(solution)/shard_map/sum_gy/ppermute | solution.py:265
  52.5 11.0 %collective-permute-start.16 = (bf16[16,4096]{1,0:T(8,128)(2,1)S(1)}, bf16[16,4096]{1,0:T(8,128)(2,1)S(1)}, u32[]{:S(2)}, u32[]{:S(2)}) collective-permute-start(bf16[16,4096]{1,0:T(8,128)(2,1)S(1)} %get-tuple-element.45), channel_id=1, source_target_pairs={{0,3},{1,2},{2,1},{3,0},{4,7},{5,6},{6,5},{7,4},{8,11},{9,10},{10,... | collective-permute-start | bytes 393224 | tf_op jit(solution)/shard_map/sum_gy/ppermute | solution.py:265
  54.8 8.7 %collective-permute-start.17 = (bf16[16,4096]{1,0:T(8,128)(2,1)S(1)}, bf16[16,4096]{1,0:T(8,128)(2,1)S(1)}, u32[]{:S(2)}, u32[]{:S(2)}) collective-permute-start(bf16[16,4096]{1,0:T(8,128)(2,1)S(1)} %get-tuple-element.46), channel_id=1, source_target_pairs={{0,1},{1,0},{2,3},{3,2},{4,5},{5,4},{6,7},{7,6},{8,9},{9,8},{10,11... | collective-permute-start | bytes 393224 | tf_op jit(solution)/shard_map/sum_gy/ppermute | solution.py:265

commit v3 on v2

--- a/solution.py
+++ b/solution.py
@@ -11,8 +11,9 @@
 HEAD_SIZE = 128
 LANES = 128
 EPSILON = 1e-05
-CUTS = (4,)
-LOADS = len(CUTS) + 1
+ORDERS = {"hidden": (2, 3, 1), "sum_gx": (2, 3, 1), "to_owner": (3, 2, 1), "to_head_rows": (3, 2, 1), "gather_gx": (2, 3, 1), "sum_gy": (2, 3, 1)}
+CUTS = (0, 3, 5, 8)
+LOADS = len(CUTS) - 1
 VMEM = pl.BlockSpec(memory_space=pltpu.VMEM)
 
 
@@ -25,18 +26,28 @@
     return jnp.where(lane == 0, high, jnp.where(lane == 1, middle, jnp.where(lane == 2, low, 0.0)))
 
 
+def padded(left):
+    missing = -left.shape[0] % 128
+    if not missing:
+        return left
+    return jnp.concatenate([left, jnp.zeros((missing, left.shape[1]), left.dtype)], axis=0)
+
+
 def project_kernel(count, width, *refs):
-    pieces = [refs[wide_order(count).index(offset)] for offset in range(count)]
+    pieces = [refs[order("hidden", count).index(offset)] for offset in range(count)]
     gain, w_query, key_weight, value_weight = refs[count : count + 4]
-    outs, (scaled, squares) = refs[count + 4 : 2 * count + 4], refs[2 * count + 4 :]
-    flip = lax.axis_index("gx") ^ lax.axis_index("gy")
+    outs, (held,) = refs[count + 4 : 2 * count + 4], refs[2 * count + 4 :]
+    flip = lax.axis_index("gx") ^ lax.axis_index("gy") ^ 1
     gains = gain[...].astype(jnp.float32)[None, :]
+    rows = pieces[0].shape[0]
+    scaled = []
     for offset in range(count):
         states = pieces[offset][...].astype(jnp.float32)
-        scaled[flip ^ offset] = (states * gains).astype(jnp.bfloat16)
-        squares[flip ^ offset] = square_lanes(jnp.sum(states * states, axis=1, keepdims=True))
-    rows = scaled.shape[1]
-    left = scaled[...].reshape(count * rows, scaled.shape[2])
+        scaled.append((states * gains).astype(jnp.bfloat16))
+        held[flip ^ offset, :, width - LANES :] = square_lanes(
+            jnp.sum(states * states, axis=1, keepdims=True)
+        ).astype(jnp.bfloat16)
+    left = padded(jnp.concatenate(scaled, axis=0))
     start = 0
     for weight in (w_query, key_weight, value_weight):
         columns = weight.shape[1]
@@ -46,18 +57,20 @@
                 left, weight[:, first : first + step], preferred_element_type=jnp.float32
             ).astype(jnp.bfloat16)
             for offset in range(count):
-                outs[offset][:, start : start + step] = product[offset * rows : (offset + 1) * rows]
+                held[flip ^ offset, :, start : start + step] = product[
+                    offset * rows : (offset + 1) * rows
+                ]
             start += step
     for offset in range(count):
+        outs[offset][...] = held[offset]
         if start < width - LANES:
             outs[offset][:, start : width - LANES] = jnp.zeros(
                 (rows, width - LANES - start), jnp.bfloat16
             )
-        outs[offset][:, width - LANES :] = squares[offset].astype(jnp.bfloat16)
 
 
 def combine_kernel(count, *refs):
-    pieces = [refs[wide_order(count).index(offset)] for offset in range(count)]
+    pieces = [refs[order("sum_gx", count).index(offset)] for offset in range(count)]
     outs, (held,) = refs[count : 2 * count], refs[2 * count :]
     total = pieces[0][...].astype(jnp.float32)
     for piece in pieces[1:]:
@@ -82,7 +95,7 @@
 
 
 def attend_kernel(count, group, features, *refs):
-    pieces = [refs[order(count).index(offset)] for offset in range(count)]
+    pieces = [refs[order("to_owner", count).index(offset)] for offset in range(count)]
     keys, values, cosines, sines, filled = refs[count : count + 5]
     outs = refs[count + 5 :]
     share, slots = keys.shape[0], keys.shape[1]
@@ -98,6 +111,7 @@
     row_scales = spread(row_scale, group)
     item = lax.broadcasted_iota(jnp.int32, (rows, 1), 0) % share
     valid = lax.broadcasted_iota(jnp.int32, (rows, slots), 1) < filled[:, :1]
+    states, scores = [], []
     for offset in range(count):
         piece = pieces[offset][...].astype(jnp.float32)
         head = me ^ offset
@@ -109,32 +123,41 @@
         query = query * cosine + pltpu.roll(query, HEAD_SIZE // 2, 1) * sine
         query = query.astype(jnp.bfloat16)
         first = group * HEAD_SIZE
-        fresh_key = spread(piece[:, first : first + HEAD_SIZE], group)
-        fresh_key = fresh_key * row_scales
+        fresh_key = spread(piece[:, first : first + HEAD_SIZE], group) * row_scales
         fresh_key = fresh_key * cosine + pltpu.roll(fresh_key, HEAD_SIZE // 2, 1) * sine
         fresh_key = fresh_key.astype(jnp.bfloat16).astype(jnp.float32)
         first = first + HEAD_SIZE
-        fresh_value = spread(piece[:, first : first + HEAD_SIZE], group)
-        fresh_value = (fresh_value * row_scales).astype(jnp.bfloat16).astype(jnp.float32)
+        fresh_value = spread(piece[:, first : first + HEAD_SIZE], group) * row_scales
+        fresh_value = fresh_value.astype(jnp.bfloat16).astype(jnp.float32)
         own = jnp.sum(query.astype(jnp.float32) * fresh_key, axis=1, keepdims=True) * scale
-        scores = jnp.zeros((rows, slots), jnp.float32)
-        for n in range(share):
-            product = lax.dot_general(
+        states.append((lanes, own, fresh_value))
+        products = [
+            lax.dot_general(
                 query,
                 keys[n, :, lanes],
                 (((1,), (1,)), ((), ())),
                 preferred_element_type=jnp.float32,
             )
-            scores = jnp.where(item == n, product, scores)
-        scores = jnp.where(valid, scores * scale, -1e30)
-        top = jnp.maximum(jnp.max(scores, axis=1, keepdims=True), own)
-        weights = jnp.where(valid, jnp.exp(scores - top), 0.0)
-        own_weight = jnp.exp(own - top)
-        total = jnp.sum(weights, axis=1, keepdims=True) + own_weight
+            for n in range(share)
+        ]
+        score = products[0]
+        for n in range(1, share):
+            score = jnp.where(item == n, products[n], score)
+        scores.append(jnp.where(valid, score * scale, -1e30))
+    tops = [
+        jnp.maximum(jnp.max(score, axis=1, keepdims=True), own)
+        for score, (_, own, _) in zip(scores, states)
+    ]
+    weights = [
+        jnp.where(valid, jnp.exp(score - top), 0.0) for score, top in zip(scores, tops)
+    ]
+    for offset, (lanes, own, fresh_value) in enumerate(states):
+        own_weight = jnp.exp(own - tops[offset])
+        total = jnp.sum(weights[offset], axis=1, keepdims=True) + own_weight
         mixed = own_weight.astype(jnp.bfloat16).astype(jnp.float32) * fresh_value
         for n in range(share):
             mixed = mixed + jnp.dot(
-                jnp.where(item == n, weights, 0.0).astype(jnp.bfloat16),
+                jnp.where(item == n, weights[offset], 0.0).astype(jnp.bfloat16),
                 values[n, :, lanes],
                 preferred_element_type=jnp.float32,
             )
@@ -145,7 +168,7 @@
 
 
 def assemble_kernel(count, *refs):
-    pieces = [refs[order(count).index(offset)] for offset in range(count)]
+    pieces = [refs[order("to_head_rows", count).index(offset)] for offset in range(count)]
     out, held = refs[count], refs[count + 1]
     me = lax.axis_index("gy")
     for offset in range(count):
@@ -154,14 +177,14 @@
 
 
 def output_kernel(count, *refs):
-    pieces = [refs[wide_order(count).index(offset)] for offset in range(count)]
+    pieces = [refs[order("gather_gx", count).index(offset)] for offset in range(count)]
     weights = refs[count : count + LOADS]
     outs, (held,) = refs[count + LOADS : 2 * count + LOADS], refs[2 * count + LOADS :]
-    flip = lax.axis_index("gx") ^ lax.axis_index("gy")
+    flip = lax.axis_index("gx") ^ lax.axis_index("gy") ^ 1
     for offset in range(count):
         held[flip ^ offset] = pieces[offset][...]
     rows = held.shape[1]
-    left = held[...].reshape(count * rows, held.shape[2])
+    left = padded(held[...].reshape(count * rows, held.shape[2]))
     columns = weights[0].shape[1]
     step = min(columns, 512)
     for first in range(0, columns, step):
@@ -203,9 +226,9 @@
 
 
 def loading(kernel, loads, counts, *refs):
-    inputs, outputs = counts
+    skip, inputs, outputs = counts
     many = len(loads)
-    sources, refs = refs[:many], refs[many:]
+    sources, refs = refs[:many], refs[many + skip :]
     if many:
         targets, sems = refs[inputs + outputs : inputs + outputs + many], refs[-1]
         refs = refs[: inputs + outputs] + refs[inputs + outputs + many : -1]
@@ -223,14 +246,15 @@
         copy.wait()
 
 
-def call(kernel, outs, scratch, args, name, limit, scalars=0, loads=(), flops=0):
+def call(kernel, outs, scratch, args, name, limit, scalars=0, loads=(), flops=0, after=()):
     arrays = [pltpu.with_memory_space_constraint(load[0], pltpu.HBM) for load in loads]
     parts = [load[1:] for load in loads]
     size = sum(2 * rows * array.shape[1] for array, _, rows in loads)
     results = pl.pallas_call(
-        functools.partial(loading, kernel, parts, (len(args), len(outs))),
+        functools.partial(loading, kernel, parts, (len(after), len(args), len(outs))),
         out_shape=[*outs, *(pltpu.VMEM((rows, a.shape[1]), a.dtype) for a, _, rows in loads)],
         in_specs=[pl.BlockSpec(memory_space=pltpu.HBM)] * len(loads)
+        + [pl.BlockSpec(memory_space=pl.ANY)] * len(after)
         + [VMEM] * (len(args) - scalars)
         + [pl.BlockSpec(memory_space=pltpu.SMEM)] * scalars,
         out_specs=[VMEM] * (len(outs) + len(loads)),
@@ -241,7 +265,7 @@
         ),
         compiler_params=pltpu.CompilerParams(vmem_limit_bytes=limit << 20),
         name=name,
-    )(*arrays, *args)
+    )(*arrays, *after, *args)
     return results[: len(outs)], results[len(outs) :]
 
 
@@ -249,21 +273,30 @@
     return jax.ShapeDtypeStruct(shape, dtype)
 
 
-def order(count):
-    return [0, *range(count - 1, 0, -1)]
-
-
-def wide_order(count):
-    half = count // 2
-    return [0, half, *range(count - 1, half, -1), *range(half - 1, 0, -1)]
-
-
-def exchange(pieces, axis):
+def order(name, count):
+    if count == len(ORDERS[name]) + 1:
+        return (0, *ORDERS[name])
+    return (0, *range(count - 1, 0, -1))
+
+
+def exchange(pieces, axis, name):
     count = len(pieces)
     result = list(pieces)
-    for offset in range(count - 1, 0, -1):
+    for offset in order(name, count)[1:]:
         result[offset] = lax.ppermute(
             pieces[offset], axis, [(n, n ^ offset) for n in range(count)]
+        )
+    return result
+
+
+def crossing_exchange(pieces, name):
+    count = len(pieces)
+    result = list(pieces)
+    for offset in (*order(name, count)[1:], 0):
+        result[offset] = lax.ppermute(
+            pieces[offset],
+            ("gx", "gy"),
+            [(n, (n ^ count) ^ offset) for n in range(lax.axis_size("gx") * count)],
         )
     return result
 
@@ -294,8 +327,12 @@
     out_rows, out_columns = w_output.shape
     cuts = [out_rows * cut // 8 for cut in CUTS]
 
+    def fetch(name, index, after):
+        first, last = cuts[index : index + 2]
+        return call(None, [], [], [], name, 4, loads=[(w_output, first, last - first)], after=[after])[1]
+
     with jax.named_scope("gather_hidden"):
-        gathered = exchange([hidden_states] * count, "gy")
+        gathered = exchange([hidden_states] * count, "gy", "hidden")
     with jax.named_scope("fetch_query"):
         table = array((share * group, HEAD_SIZE), jnp.float32)
         (cosine, sine, filled), weights = call(
@@ -312,12 +349,9 @@
         partial, output_weights = call(
             functools.partial(project_kernel, count, width),
             [array((rows, width))] * count,
+            [pltpu.VMEM((count, rows, width), jnp.bfloat16)],
             [
-                pltpu.VMEM((count, rows, depth), jnp.bfloat16),
-                pltpu.VMEM((count, rows, LANES), jnp.float32),
-            ],
-            [
-                *(gathered[k] for k in wide_order(count)),
+                *(gathered[k] for k in order("hidden", count)),
                 norm_gain,
                 *weights,
                 key_weight,
@@ -325,21 +359,23 @@
             ],
             "project",
             8,
-            loads=[(w_output, 0, cuts[0])],
+            loads=[(w_output, cuts[0], cuts[1] - cuts[0])],
             flops=2 * count * rows * depth * used,
         )
     with jax.named_scope("sum_gx"):
-        received = exchange(partial, "gx")
+        received = exchange(partial, "gx", "sum_gx")
+        output_weights += fetch("fetch_output", 1, partial[0])
         owned, _ = call(
             functools.partial(combine_kernel, count),
             [array((share, width))] * count,
             [pltpu.VMEM((count, share, width), jnp.float32)],
-            [received[k] for k in wide_order(count)],
+            [received[k] for k in order("sum_gx", count)],
             "combine",
             4,
+            after=output_weights[1:],
         )
     with jax.named_scope("to_owner"):
-        owned = exchange(owned, "gy")
+        owned = crossing_exchange(owned, "to_owner")
 
     with jax.named_scope("attend"):
         if key_columns == HEAD_SIZE:
@@ -348,7 +384,7 @@
                 [array((share, query_columns))] * count,
                 [],
                 [
-                    *(owned[k] for k in order(count)),
+                    *(owned[k] for k in order("to_owner", count)),
                     stored_key_cache,
                     stored_value_cache,
                     cosine,
@@ -365,43 +401,35 @@
             )
 
     with jax.named_scope("to_head_rows"):
-        attended = exchange(attended, "gy")
+        attended = crossing_exchange(attended, "to_head_rows")
         (block,), _ = call(
             functools.partial(assemble_kernel, count),
             [array((count * share, query_columns))],
             [pltpu.VMEM((count, share, query_columns), jnp.float32)],
-            [attended[k] for k in order(count)],
+            [attended[k] for k in order("to_head_rows", count)],
             "assemble",
             4,
         )
     with jax.named_scope("gather_gx"):
-        blocks = exchange([block] * count, "gx")
-        _, loaded = call(
-            lambda *refs: None,
-            [],
-            [],
-            [block],
-            "fetch_output",
-            4,
-            loads=[(w_output, cuts[0], out_rows - cuts[0])],
-        )
+        blocks = exchange([block] * count, "gx", "gather_gx")
+        output_weights += fetch("fetch_output", 2, block)
     with jax.named_scope("output"):
         products, _ = call(
             functools.partial(output_kernel, count),
             [array((count * share, out_columns))] * count,
             [pltpu.VMEM((count, count * share, query_columns), jnp.bfloat16)],
-            [*(blocks[k] for k in wide_order(count)), *output_weights, *loaded],
+            [*(blocks[k] for k in order("gather_gx", count)), *output_weights],
             "output",
             8,
             flops=2 * count * count * share * out_rows * out_columns,
         )
     with jax.named_scope("sum_gy"):
-        products = exchange(products, "gy")
+        products = exchange(products, "gy", "sum_gy")
         (result,), _ = call(
             functools.partial(add_kernel, count),
             [array((rows, out_columns))],
             [],
-            [products[k] for k in wide_order(count)],
+            [products[k] for k in order("sum_gy", count)],
             "add",
             8,
         )

time: 64.4 us -> 62.3 us (0.967)
  waiting for transfers between devices: 21.3 us -> 20.3 us
  starting transfers between devices: 23.3 us -> 22.5 us
    ppermute x18 -> x12, starting transfers between devices: 23.3 us -> 13.9 us  [exchange(): lax.ppermute(pieces[offset], axis, [(n, n ^ offset) for n in range(count)])]
    ppermute x0 -> x8, starting transfers between devices: none -> 8.59 us  [crossing_exchange(): lax.ppermute(pieces[offset], ('gx', 'gy'), [(n, n ^ count ^ offset) for n...]
    ppermute x18 -> x12, waiting for transfers between devices: 21.3 us -> 15.7 us  [exchange(): lax.ppermute(pieces[offset], axis, [(n, n ^ offset) for n in range(count)])]
    ppermute x0 -> x8, waiting for transfers between devices: none -> 4.58 us  [crossing_exchange(): lax.ppermute(pieces[offset], ('gx', 'gy'), [(n, n ^ count ^ offset) for n...]
    pallas_call x8 -> x9, Pallas kernels: 18.8 us -> 18.5 us  [call(): pl.pallas_call(functools.partial(loading, kernel, parts, (len(after), len...]
  transfers between devices with their start and end apart: 18 -> 20, of which waited for: 10 -> 10; matrix products, arithmetic and copies ran while one was open for 0% -> 0% of each run, Pallas kernels for 15% -> 18%
where the time goes in v3:
time: 62.3 us; the launch traced here: 62.1 us
  starting transfers between devices  22.5 us (36%)
  waiting for transfers between devices  20.3 us (33%)
  Pallas kernels  18.5 us (30%)
  local copies, waits for them, and re-layouts  0.68 us (1%)
    pallas_call x9, Pallas kernels, call(): pl.pallas_call(functools.partial(loading, kernel, parts, (len(after), len...  18.5 us
    ppermute x12, waiting for transfers between devices, exchange(): lax.ppermute(pieces[offset], axis, [(n, n ^ offset) for n in range(count)])  15.7 us
    ppermute x12, starting transfers between devices, exchange(): lax.ppermute(pieces[offset], axis, [(n, n ^ offset) for n in range(count)])  13.9 us
    ppermute x8, starting transfers between devices, crossing_exchange(): lax.ppermute(pieces[offset], ('gx', 'gy'), [(n, n ^ count ^ offset) for n...  8.59 us
    ppermute x8, waiting for transfers between devices, crossing_exchange(): lax.ppermute(pieces[offset], ('gx', 'gy'), [(n, n ^ count ^ offset) for n...  4.58 us
  transfers between devices with their start and end apart: 20, of which 10 were waited for; matrix products, arithmetic and copies ran while one was open for 0% of the time, Pallas kernels for 18%

profile of v3, /device:TPU:0, one launch (start us, length us, event | category | flops | bytes accessed | tf_op | source)
XLA Modules:
  0.0 62.1 jit_solution(12753534337910078751)
XLA Ops:
  0.0 0.0 copy-start.4
  0.0 0.0 copy-start.1
  0.0 0.0 copy-start
  0.0 0.0 copy-start.5
  0.0 5.1 %collective-permute-start.1 = (bf16[16,4096]{1,0:T(8,128)(2,1)}, bf16[16,4096]{1,0:T(8,128)(2,1)S(1)}, u32[]{:S(2)}, u32[]{:S(2)}) collective-permute-start(bf16[16,4096]{1,0:T(8,128)(2,1)} %refs_1_.3), channel_id=1, source_target_pairs={{0,3},{1,2},{2,1},{3,0},{4,7},{5,6},{6,5},{7,4},{8,11},{9,10},{10,... | collective-permute-start | bytes 393224 | tf_op jit(solution)/shard_map/gather_hidden/ppermute | solution.py:286
  5.1 0.0 collective-permute-start
  5.1 0.6 %collective-permute-start.2 = (bf16[16,4096]{1,0:T(8,128)(2,1)}, bf16[16,4096]{1,0:T(8,128)(2,1)S(1)}, u32[]{:S(2)}, u32[]{:S(2)}) collective-permute-start(bf16[16,4096]{1,0:T(8,128)(2,1)} %refs_1_.3), channel_id=1, source_target_pairs={{0,1},{1,0},{2,3},{3,2},{4,5},{5,4},{6,7},{7,6},{8,9},{9,8},{10,11... | collective-permute-start | bytes 393224 | tf_op jit(solution)/shard_map/gather_hidden/ppermute | solution.py:286
  5.8 0.0 copy-start.6
  5.8 0.7 %copy-done.6 = s32[4]{0:T(128)S(1)} copy-done((s32[4]{0:T(128)S(1)}, s32[4]{0:T(128)}, u32[]{:S(2)}) %copy-start.6) | copy-done | bytes 40
  6.4 6.3 %fetch_query.1 = (f32[64,128]{1,0:T(8,128)S(1)}, f32[64,128]{1,0:T(8,128)S(1)}, s32[64,128]{1,0:T(8,128)S(1)}, bf16[4096,2048]{1,0:T(8,128)(2,1)S(1)}) custom-call(bf16[4096,2048]{1,0:T(8,128)(2,1)} %refs_0_.4, s32[4]{0:T(128)S(1)} %copy-done.6), custom_call_target="tpu_custom_call" | custom-call | bytes 33619968 | tf_op jit(solution)/shard_map/fetch_query/fetch_query/pallas_call | solution.py:253
  12.8 0.0 collective-permute-done.1.refs_3_
  12.8 3.7 %collective-permute-done.refs_2_ = bf16[16,4096]{1,0:T(8,128)(2,1)S(1)} collective-permute-done((bf16[16,4096]{1,0:T(8,128)(2,1)}, bf16[16,4096]{1,0:T(8,128)(2,1)S(1)}, u32[]{:S(2)}, u32[]{:S(2)}) %collective-permute-start) | collective-permute-done | bytes 131104 | tf_op jit(solution)/shard_map/gather_hidden/ppermute | solution.py:286
  16.4 0.0 collective-permute-done.2.refs_4_
  16.4 0.0 copy-done.4
  16.4 0.0 copy-done.1
  16.4 0.0 copy-done
  16.4 0.0 copy-done.5
  16.5 3.0 %project.1 = (bf16[16,2432]{1,0:T(8,128)(2,1)S(1)}, bf16[16,2432]{1,0:T(8,128)(2,1)S(1)}, bf16[16,2432]{1,0:T(8,128)(2,1)S(1)}, bf16[16,2432]{1,0:T(8,128)(2,1)S(1)}, bf16[768,4096]{1,0:T(8,128)(2,1)S(1)}) custom-call(bf16[2048,4096]{1,0:T(8,128)(2,1)} %refs_0_.7, bf16[16,4096]{1,0:T(8,128)(2,1)S(1)} %copy-done.4, ...), custom_call_target="tpu_custom_call" | custom-call | flops 1207959552 | bytes 12648448 | tf_op jit(solution)/shard_map/project/project/pallas_call | solution.py:253
  19.5 0.0 copy-start.2
  19.5 0.0 copy-start.3
  19.5 1.6 %collective-permute-start.3 = (bf16[16,2432]{1,0:T(8,128)(2,1)S(1)}, bf16[16,2432]{1,0:T(8,128)(2,1)S(1)}, u32[]{:S(2)}, u32[]{:S(2)}) collective-permute-start(bf16[16,2432]{1,0:T(8,128)(2,1)S(1)} %get-tuple-element.28), channel_id=1, source_target_pairs={{0,8},{4,12},{8,0},{12,4},{1,9},{5,13},{9,1},{13,5},{2,10},{6,14},... | collective-permute-start | bytes 233480 | tf_op jit(solution)/shard_map/sum_gx/ppermute | solution.py:286
  21.0 0.0 collective-permute-start.4
  21.0 0.7 %collective-permute-start.5 = (bf16[16,2432]{1,0:T(8,128)(2,1)S(1)}, bf16[16,2432]{1,0:T(8,128)(2,1)S(1)}, u32[]{:S(2)}, u32[]{:S(2)}) collective-permute-start(bf16[16,2432]{1,0:T(8,128)(2,1)S(1)} %get-tuple-element.30), channel_id=1, source_target_pairs={{0,4},{4,0},{8,12},{12,8},{1,5},{5,1},{9,13},{13,9},{2,6},{6,2},{1... | collective-permute-start | bytes 233480 | tf_op jit(solution)/shard_map/sum_gx/ppermute | solution.py:286
  21.7 2.2 %fetch_output.2.refs_0_.refs_5_ = bf16[512,4096]{1,0:T(8,128)(2,1)S(1)} custom-call(bf16[2048,4096]{1,0:T(8,128)(2,1)} %refs_0_.7, bf16[16,2432]{1,0:T(8,128)(2,1)S(1)} %get-tuple-element.27.refs_1_), custom_call_target="tpu_custom_call" | custom-call | bytes 8454144 | tf_op jit(solution)/shard_map/sum_gx/fetch_output/pallas_call | solution.py:253
  23.9 0.1 collective-permute-done.3.refs_2_
  24.0 1.7 %collective-permute-done.4.refs_3_ = bf16[16,2432]{1,0:T(8,128)(2,1)S(1)} collective-permute-done((bf16[16,2432]{1,0:T(8,128)(2,1)S(1)}, bf16[16,2432]{1,0:T(8,128)(2,1)S(1)}, u32[]{:S(2)}, u32[]{:S(2)}) %collective-permute-start.4) | collective-permute-done | bytes 77856 | tf_op jit(solution)/shard_map/sum_gx/ppermute | solution.py:286
  25.6 0.0 collective-permute-done.5.refs_4_
  25.6 0.1 combine.1
  25.7 0.1 collective-permute-start.6
  25.9 2.5 %collective-permute-start.7 = (bf16[4,2432]{1,0:T(4,128)(2,1)S(1)}, bf16[4,2432]{1,0:T(4,128)(2,1)S(1)}, u32[]{:S(2)}, u32[]{:S(2)}) collective-permute-start(bf16[4,2432]{1,0:T(4,128)(2,1)S(1)} %get-tuple-element.32), channel_id=1, source_target_pairs={{0,7},{1,6},{2,5},{3,4},{4,3},{5,2},{6,1},{7,0},{8,15},{9,14},{10,... | collective-permute-start | bytes 58376 | tf_op jit(solution)/shard_map/to_owner/ppermute | solution.py:296
  28.4 0.0 collective-permute-start.8
  28.4 1.6 %collective-permute-start.9 = (bf16[4,2432]{1,0:T(4,128)(2,1)S(1)}, bf16[4,2432]{1,0:T(4,128)(2,1)S(1)}, u32[]{:S(2)}, u32[]{:S(2)}) collective-permute-start(bf16[4,2432]{1,0:T(4,128)(2,1)S(1)} %get-tuple-element.34), channel_id=1, source_target_pairs={{0,5},{1,4},{2,7},{3,6},{4,1},{5,0},{6,3},{7,2},{8,13},{9,12},{10,... | collective-permute-start | bytes 58376 | tf_op jit(solution)/shard_map/to_owner/ppermute | solution.py:296
  30.0 0.0 collective-permute-done.6.refs_0_
  30.1 0.8 %collective-permute-done.7.refs_1_ = bf16[4,2432]{1,0:T(4,128)(2,1)S(1)} collective-permute-done((bf16[4,2432]{1,0:T(4,128)(2,1)S(1)}, bf16[4,2432]{1,0:T(4,128)(2,1)S(1)}, u32[]{:S(2)}, u32[]{:S(2)}) %collective-permute-start.7) | collective-permute-done | bytes 19488 | tf_op jit(solution)/shard_map/to_owner/ppermute | solution.py:296
  30.9 1.6 %collective-permute-done.8.refs_2_ = bf16[4,2432]{1,0:T(4,128)(2,1)S(1)} collective-permute-done((bf16[4,2432]{1,0:T(4,128)(2,1)S(1)}, bf16[4,2432]{1,0:T(4,128)(2,1)S(1)}, u32[]{:S(2)}, u32[]{:S(2)}) %collective-permute-start.8) | collective-permute-done | bytes 19488 | tf_op jit(solution)/shard_map/to_owner/ppermute | solution.py:296
  32.5 0.0 collective-permute-done.9.refs_3_
  32.5 0.0 copy-done.2
  32.5 0.0 copy-done.3
  32.5 1.0 %attend.1 = (bf16[4,2048]{1,0:T(4,128)(2,1)S(1)}, bf16[4,2048]{1,0:T(4,128)(2,1)S(1)}, bf16[4,2048]{1,0:T(4,128)(2,1)S(1)}, bf16[4,2048]{1,0:T(4,128)(2,1)S(1)}) custom-call(bf16[4,2432]{1,0:T(4,128)(2,1)S(1)} %collective-permute-done.6.refs_0_, bf16[4,2432]{1,0:T(4,128)(2,1)S(1)} %collective-permute-done.7.refs_1_, ...), custom_call_target="tpu_custom_call" | custom-call | bytes 65536 | tf_op jit(solution)/shard_map/attend/attend/pallas_call | solution.py:253
  33.5 0.2 collective-permute-start.10
  33.7 2.2 %collective-permute-start.11 = (bf16[4,2048]{1,0:T(4,128)(2,1)S(1)}, bf16[4,2048]{1,0:T(4,128)(2,1)S(1)}, u32[]{:S(2)}, u32[]{:S(2)}) collective-permute-start(bf16[4,2048]{1,0:T(4,128)(2,1)S(1)} %get-tuple-element.39), channel_id=1, source_target_pairs={{0,7},{1,6},{2,5},{3,4},{4,3},{5,2},{6,1},{7,0},{8,15},{9,14},{10,... | collective-permute-start | bytes 49160 | tf_op jit(solution)/shard_map/to_head_rows/ppermute | solution.py:296
  35.9 0.0 collective-permute-start.12
  35.9 1.9 %collective-permute-start.13 = (bf16[4,2048]{1,0:T(4,128)(2,1)S(1)}, bf16[4,2048]{1,0:T(4,128)(2,1)S(1)}, u32[]{:S(2)}, u32[]{:S(2)}) collective-permute-start(bf16[4,2048]{1,0:T(4,128)(2,1)S(1)} %get-tuple-element.41), channel_id=1, source_target_pairs={{0,5},{1,4},{2,7},{3,6},{4,1},{5,0},{6,3},{7,2},{8,13},{9,12},{10,... | collective-permute-start | bytes 49160 | tf_op jit(solution)/shard_map/to_head_rows/ppermute | solution.py:296
  37.8 0.0 collective-permute-done.10.refs_0_
  37.8 0.9 %collective-permute-done.11.refs_1_ = bf16[4,2048]{1,0:T(4,128)(2,1)S(1)} collective-permute-done((bf16[4,2048]{1,0:T(4,128)(2,1)S(1)}, bf16[4,2048]{1,0:T(4,128)(2,1)S(1)}, u32[]{:S(2)}, u32[]{:S(2)}) %collective-permute-start.11) | collective-permute-done | bytes 16416 | tf_op jit(solution)/shard_map/to_head_rows/ppermute | solution.py:296
  38.7 1.2 %collective-permute-done.12.refs_2_ = bf16[4,2048]{1,0:T(4,128)(2,1)S(1)} collective-permute-done((bf16[4,2048]{1,0:T(4,128)(2,1)S(1)}, bf16[4,2048]{1,0:T(4,128)(2,1)S(1)}, u32[]{:S(2)}, u32[]{:S(2)}) %collective-permute-start.12) | collective-permute-done | bytes 16416 | tf_op jit(solution)/shard_map/to_head_rows/ppermute | solution.py:296
  39.9 0.0 collective-permute-done.13.refs_3_
  40.0 0.2 collective-permute-start.16
  40.2 0.9 %collective-permute-start.15 = (bf16[16,2048]{1,0:T(8,128)(2,1)S(1)}, bf16[16,2048]{1,0:T(8,128)(2,1)S(1)}, u32[]{:S(2)}, u32[]{:S(2)}) collective-permute-start(bf16[16,2048]{1,0:T(8,128)(2,1)S(1)} %assemble.1.refs_1_.refs_0_), channel_id=1, source_target_pairs={{0,12},{4,8},{8,4},{12,0},{1,13},{5,9},{9,5},{13,1},{2,14},{6,10},... | collective-permute-start | bytes 196616 | tf_op jit(solution)/shard_map/gather_gx/ppermute | solution.py:286
  41.1 1.1 %collective-permute-start.14 = (bf16[16,2048]{1,0:T(8,128)(2,1)S(1)}, bf16[16,2048]{1,0:T(8,128)(2,1)S(1)}, u32[]{:S(2)}, u32[]{:S(2)}) collective-permute-start(bf16[16,2048]{1,0:T(8,128)(2,1)S(1)} %assemble.1.refs_1_.refs_0_), channel_id=1, source_target_pairs={{0,8},{4,12},{8,0},{12,4},{1,9},{5,13},{9,1},{13,5},{2,10},{6,14},... | collective-permute-start | bytes 196616 | tf_op jit(solution)/shard_map/gather_gx/ppermute | solution.py:286
  42.2 2.8 %fetch_output.3.refs_6_ = bf16[768,4096]{1,0:T(8,128)(2,1)S(1)} custom-call(bf16[2048,4096]{1,0:T(8,128)(2,1)} %refs_0_.7, bf16[16,2048]{1,0:T(8,128)(2,1)S(1)} %assemble.1.refs_1_.refs_0_), custom_call_target="tpu_custom_call" | custom-call | bytes 12648448 | tf_op jit(solution)/shard_map/gather_gx/fetch_output/pallas_call | solution.py:253
  45.0 0.0 collective-permute-done.16.refs_3_
  45.0 0.0 collective-permute-done.15.refs_2_
  45.0 1.0 %collective-permute-done.14.refs_1_ = bf16[16,2048]{1,0:T(8,128)(2,1)S(1)} collective-permute-done((bf16[16,2048]{1,0:T(8,128)(2,1)S(1)}, bf16[16,2048]{1,0:T(8,128)(2,1)S(1)}, u32[]{:S(2)}, u32[]{:S(2)}) %collective-permute-start.14) | collective-permute-done | bytes 65568 | tf_op jit(solution)/shard_map/gather_gx/ppermute | solution.py:286
  46.0 2.4 %output.1 = (bf16[16,4096]{1,0:T(8,128)(2,1)S(1)}, bf16[16,4096]{1,0:T(8,128)(2,1)S(1)}, bf16[16,4096]{1,0:T(8,128)(2,1)S(1)}, bf16[16,4096]{1,0:T(8,128)(2,1)S(1)}) custom-call(bf16[16,2048]{1,0:T(8,128)(2,1)S(1)} %assemble.1.refs_1_.refs_0_, bf16[16,2048]{1,0:T(8,128)(2,1)S(1)} %collective-permute-done.14.refs_1_, ...), custom_call_target="tpu_custom_call" | custom-call | flops 1073741824 | bytes 65536 | tf_op jit(solution)/shard_map/output/output/pallas_call | solution.py:253
  48.4 2.0 %collective-permute-start.17 = (bf16[16,4096]{1,0:T(8,128)(2,1)S(1)}, bf16[16,4096]{1,0:T(8,128)(2,1)S(1)}, u32[]{:S(2)}, u32[]{:S(2)}) collective-permute-start(bf16[16,4096]{1,0:T(8,128)(2,1)S(1)} %get-tuple-element.44), channel_id=1, source_target_pairs={{0,2},{1,3},{2,0},{3,1},{4,6},{5,7},{6,4},{7,5},{8,10},{9,11},{10,... | collective-permute-start | bytes 393224 | tf_op jit(solution)/shard_map/sum_gy/ppermute | solution.py:286
  50.4 1.7 %collective-permute-start.18 = (bf16[16,4096]{1,0:T(8,128)(2,1)S(1)}, bf16[16,4096]{1,0:T(8,128)(2,1)S(1)}, u32[]{:S(2)}, u32[]{:S(2)}) collective-permute-start(bf16[16,4096]{1,0:T(8,128)(2,1)S(1)} %get-tuple-element.45), channel_id=1, source_target_pairs={{0,3},{1,2},{2,1},{3,0},{4,7},{5,6},{6,5},{7,4},{8,11},{9,10},{10,... | collective-permute-start | bytes 393224 | tf_op jit(solution)/shard_map/sum_gy/ppermute | solution.py:286
  52.1 0.0 collective-permute-start.19
  52.1 8.9 %collective-permute-done.17.refs_1_ = bf16[16,4096]{1,0:T(8,128)(2,1)S(1)} collective-permute-done((bf16[16,4096]{1,0:T(8,128)(2,1)S(1)}, bf16[16,4096]{1,0:T(8,128)(2,1)S(1)}, u32[]{:S(2)}, u32[]{:S(2)}) %collective-permute-start.17) | collective-permute-done | bytes 131104 | tf_op jit(solution)/shard_map/sum_gy/ppermute | solution.py:286
  61.0 0.0 collective-permute-done.18.refs_2_
  61.0 0.4 collective-permute-done.19.refs_3_
  61.4 0.7 %add.1 = bf16[16,4096]{1,0:T(8,128)(2,1)} custom-call(bf16[16,4096]{1,0:T(8,128)(2,1)S(1)} %get-tuple-element.43.refs_0_, bf16[16,4096]{1,0:T(8,128)(2,1)S(1)} %collective-permute-done.17.refs_1_, bf16[16,4096]{1,0:T(8,128)(2,1)S(1)} %collective-permute-done.18.refs_2_, bf16[16,4096]{1,0:T(8,128)(2,1)S(1)} %collective-permute-done.19.refs_3_), custom_call_target="tpu_custom_call" | custom-call | bytes 65536 | tf_op jit(solution)/shard_map/sum_gy/add/pallas_call | solution.py:253
  (1 shorter events, 0.0 us)
Async XLA Ops:
  0.0 16.4 %copy-start.4 = (bf16[16,4096]{1,0:T(8,128)(2,1)S(1)}, bf16[16,4096]{1,0:T(8,128)(2,1)}, u32[]{:S(2)}) copy-start(bf16[16,4096]{1,0:T(8,128)(2,1)} %refs_1_.3) | copy-start | bytes 393220
  0.0 16.4 %copy-start.1 = (bf16[4096,128]{1,0:T(8,128)(2,1)S(1)}, bf16[4096,128]{1,0:T(8,128)(2,1)}, u32[]{:S(2)}) copy-start(bf16[4096,128]{1,0:T(8,128)(2,1)} %refs_8_.1) | copy-start | bytes 3145732
  0.0 16.4 %copy-start = (bf16[4096,128]{1,0:T(8,128)(2,1)S(1)}, bf16[4096,128]{1,0:T(8,128)(2,1)}, u32[]{:S(2)}) copy-start(bf16[4096,128]{1,0:T(8,128)(2,1)} %refs_7_.1) | copy-start | bytes 3145732
  0.0 16.4 %copy-start.5 = (bf16[4096]{0:T(1024)(128)(2,1)S(1)}, bf16[4096]{0:T(1024)(128)(2,1)}, u32[]{:S(2)}) copy-start(bf16[4096]{0:T(1024)(128)(2,1)} %refs_5_.2) | copy-start | bytes 24580
  0.0 12.8 %collective-permute-start.1 = (bf16[16,4096]{1,0:T(8,128)(2,1)}, bf16[16,4096]{1,0:T(8,128)(2,1)S(1)}, u32[]{:S(2)}, u32[]{:S(2)}) collective-permute-start(bf16[16,4096]{1,0:T(8,128)(2,1)} %refs_1_.3), channel_id=1, source_target_pairs={{0,3},{1,2},{2,1},{3,0},{4,7},{5,6},{6,5},{7,4},{8,11},{9,10},{10,... | collective-permute-start | bytes 393224 | tf_op jit(solution)/shard_map/gather_hidden/ppermute | solution.py:286
  5.1 11.3 %collective-permute-start = (bf16[16,4096]{1,0:T(8,128)(2,1)}, bf16[16,4096]{1,0:T(8,128)(2,1)S(1)}, u32[]{:S(2)}, u32[]{:S(2)}) collective-permute-start(bf16[16,4096]{1,0:T(8,128)(2,1)} %refs_1_.3), channel_id=1, source_target_pairs={{0,2},{1,3},{2,0},{3,1},{4,6},{5,7},{6,4},{7,5},{8,10},{9,11},{10,... | collective-permute-start | bytes 393224 | tf_op jit(solution)/shard_map/gather_hidden/ppermute | solution.py:286
  5.1 11.3 %collective-permute-start.2 = (bf16[16,4096]{1,0:T(8,128)(2,1)}, bf16[16,4096]{1,0:T(8,128)(2,1)S(1)}, u32[]{:S(2)}, u32[]{:S(2)}) collective-permute-start(bf16[16,4096]{1,0:T(8,128)(2,1)} %refs_1_.3), channel_id=1, source_target_pairs={{0,1},{1,0},{2,3},{3,2},{4,5},{5,4},{6,7},{7,6},{8,9},{9,8},{10,11... | collective-permute-start | bytes 393224 | tf_op jit(solution)/shard_map/gather_hidden/ppermute | solution.py:286
  5.8 0.7 %copy-start.6 = (s32[4]{0:T(128)S(1)}, s32[4]{0:T(128)}, u32[]{:S(2)}) copy-start(s32[4]{0:T(128)} %refs_1_.2) | copy-start | bytes 52
  19.5 13.1 %copy-start.2 = (bf16[4,256,512]{2,1,0:T(8,128)(2,1)S(1)}, bf16[4,256,512]{2,1,0:T(8,128)(2,1)}, u32[]{:S(2)}) copy-start(bf16[4,256,512]{2,1,0:T(8,128)(2,1)} %refs_4_.1) | copy-start | bytes 3145732
  19.5 13.0 %copy-start.3 = (bf16[4,256,512]{2,1,0:T(8,128)(2,1)S(1)}, bf16[4,256,512]{2,1,0:T(8,128)(2,1)}, u32[]{:S(2)}) copy-start(bf16[4,256,512]{2,1,0:T(8,128)(2,1)} %refs_5_.3) | copy-start | bytes 3145732
  19.5 4.5 %collective-permute-start.3 = (bf16[16,2432]{1,0:T(8,128)(2,1)S(1)}, bf16[16,2432]{1,0:T(8,128)(2,1)S(1)}, u32[]{:S(2)}, u32[]{:S(2)}) collective-permute-start(bf16[16,2432]{1,0:T(8,128)(2,1)S(1)} %get-tuple-element.28), channel_id=1, source_target_pairs={{0,8},{4,12},{8,0},{12,4},{1,9},{5,13},{9,1},{13,5},{2,10},{6,14},... | collective-permute-start | bytes 233480 | tf_op jit(solution)/shard_map/sum_gx/ppermute | solution.py:286
  21.0 4.6 %collective-permute-start.4 = (bf16[16,2432]{1,0:T(8,128)(2,1)S(1)}, bf16[16,2432]{1,0:T(8,128)(2,1)S(1)}, u32[]{:S(2)}, u32[]{:S(2)}) collective-permute-start(bf16[16,2432]{1,0:T(8,128)(2,1)S(1)} %get-tuple-element.29), channel_id=1, source_target_pairs={{0,12},{4,8},{8,4},{12,0},{1,13},{5,9},{9,5},{13,1},{2,14},{6,10},... | collective-permute-start | bytes 233480 | tf_op jit(solution)/shard_map/sum_gx/ppermute | solution.py:286
  21.0 4.6 %collective-permute-start.5 = (bf16[16,2432]{1,0:T(8,128)(2,1)S(1)}, bf16[16,2432]{1,0:T(8,128)(2,1)S(1)}, u32[]{:S(2)}, u32[]{:S(2)}) collective-permute-start(bf16[16,2432]{1,0:T(8,128)(2,1)S(1)} %get-tuple-element.30), channel_id=1, source_target_pairs={{0,4},{4,0},{8,12},{12,8},{1,5},{5,1},{9,13},{13,9},{2,6},{6,2},{1... | collective-permute-start | bytes 233480 | tf_op jit(solution)/shard_map/sum_gx/ppermute | solution.py:286
  25.7 4.3 %collective-permute-start.6 = (bf16[4,2432]{1,0:T(4,128)(2,1)S(1)}, bf16[4,2432]{1,0:T(4,128)(2,1)S(1)}, u32[]{:S(2)}, u32[]{:S(2)}) collective-permute-start(bf16[4,2432]{1,0:T(4,128)(2,1)S(1)} %get-tuple-element.31), channel_id=1, source_target_pairs={{0,4},{1,5},{2,6},{3,7},{4,0},{5,1},{6,2},{7,3},{8,12},{9,13},{10,... | collective-permute-start | bytes 58376 | tf_op jit(solution)/shard_map/to_owner/ppermute | solution.py:296
  25.9 5.0 %collective-permute-start.7 = (bf16[4,2432]{1,0:T(4,128)(2,1)S(1)}, bf16[4,2432]{1,0:T(4,128)(2,1)S(1)}, u32[]{:S(2)}, u32[]{:S(2)}) collective-permute-start(bf16[4,2432]{1,0:T(4,128)(2,1)S(1)} %get-tuple-element.32), channel_id=1, source_target_pairs={{0,7},{1,6},{2,5},{3,4},{4,3},{5,2},{6,1},{7,0},{8,15},{9,14},{10,... | collective-permute-start | bytes 58376 | tf_op jit(solution)/shard_map/to_owner/ppermute | solution.py:296
  28.4 4.1 %collective-permute-start.8 = (bf16[4,2432]{1,0:T(4,128)(2,1)S(1)}, bf16[4,2432]{1,0:T(4,128)(2,1)S(1)}, u32[]{:S(2)}, u32[]{:S(2)}) collective-permute-start(bf16[4,2432]{1,0:T(4,128)(2,1)S(1)} %get-tuple-element.33), channel_id=1, source_target_pairs={{0,6},{1,7},{2,4},{3,5},{4,2},{5,3},{6,0},{7,1},{8,14},{9,15},{10,... | collective-permute-start | bytes 58376 | tf_op jit(solution)/shard_map/to_owner/ppermute | solution.py:296
  28.4 4.1 %collective-permute-start.9 = (bf16[4,2432]{1,0:T(4,128)(2,1)S(1)}, bf16[4,2432]{1,0:T(4,128)(2,1)S(1)}, u32[]{:S(2)}, u32[]{:S(2)}) collective-permute-start(bf16[4,2432]{1,0:T(4,128)(2,1)S(1)} %get-tuple-element.34), channel_id=1, source_target_pairs={{0,5},{1,4},{2,7},{3,6},{4,1},{5,0},{6,3},{7,2},{8,13},{9,12},{10,... | collective-permute-start | bytes 58376 | tf_op jit(solution)/shard_map/to_owner/ppermute | solution.py:296
  33.5 4.3 %collective-permute-start.10 = (bf16[4,2048]{1,0:T(4,128)(2,1)S(1)}, bf16[4,2048]{1,0:T(4,128)(2,1)S(1)}, u32[]{:S(2)}, u32[]{:S(2)}) collective-permute-start(bf16[4,2048]{1,0:T(4,128)(2,1)S(1)} %get-tuple-element.38), channel_id=1, source_target_pairs={{0,4},{1,5},{2,6},{3,7},{4,0},{5,1},{6,2},{7,3},{8,12},{9,13},{10,... | collective-permute-start | bytes 49160 | tf_op jit(solution)/shard_map/to_head_rows/ppermute | solution.py:296
  33.7 5.0 %collective-permute-start.11 = (bf16[4,2048]{1,0:T(4,128)(2,1)S(1)}, bf16[4,2048]{1,0:T(4,128)(2,1)S(1)}, u32[]{:S(2)}, u32[]{:S(2)}) collective-permute-start(bf16[4,2048]{1,0:T(4,128)(2,1)S(1)} %get-tuple-element.39), channel_id=1, source_target_pairs={{0,7},{1,6},{2,5},{3,4},{4,3},{5,2},{6,1},{7,0},{8,15},{9,14},{10,... | collective-permute-start | bytes 49160 | tf_op jit(solution)/shard_map/to_head_rows/ppermute | solution.py:296
  35.9 4.1 %collective-permute-start.12 = (bf16[4,2048]{1,0:T(4,128)(2,1)S(1)}, bf16[4,2048]{1,0:T(4,128)(2,1)S(1)}, u32[]{:S(2)}, u32[]{:S(2)}) collective-permute-start(bf16[4,2048]{1,0:T(4,128)(2,1)S(1)} %get-tuple-element.40), channel_id=1, source_target_pairs={{0,6},{1,7},{2,4},{3,5},{4,2},{5,3},{6,0},{7,1},{8,14},{9,15},{10,... | collective-permute-start | bytes 49160 | tf_op jit(solution)/shard_map/to_head_rows/ppermute | solution.py:296
  35.9 4.0 %collective-permute-start.13 = (bf16[4,2048]{1,0:T(4,128)(2,1)S(1)}, bf16[4,2048]{1,0:T(4,128)(2,1)S(1)}, u32[]{:S(2)}, u32[]{:S(2)}) collective-permute-start(bf16[4,2048]{1,0:T(4,128)(2,1)S(1)} %get-tuple-element.41), channel_id=1, source_target_pairs={{0,5},{1,4},{2,7},{3,6},{4,1},{5,0},{6,3},{7,2},{8,13},{9,12},{10,... | collective-permute-start | bytes 49160 | tf_op jit(solution)/shard_map/to_head_rows/ppermute | solution.py:296
  40.0 5.0 %collective-permute-start.16 = (bf16[16,2048]{1,0:T(8,128)(2,1)S(1)}, bf16[16,2048]{1,0:T(8,128)(2,1)S(1)}, u32[]{:S(2)}, u32[]{:S(2)}) collective-permute-start(bf16[16,2048]{1,0:T(8,128)(2,1)S(1)} %assemble.1.refs_1_.refs_0_), channel_id=1, source_target_pairs={{0,4},{4,0},{8,12},{12,8},{1,5},{5,1},{9,13},{13,9},{2,6},{6,2},{1... | collective-permute-start | bytes 196616 | tf_op jit(solution)/shard_map/gather_gx/ppermute | solution.py:286
  40.2 4.8 %collective-permute-start.15 = (bf16[16,2048]{1,0:T(8,128)(2,1)S(1)}, bf16[16,2048]{1,0:T(8,128)(2,1)S(1)}, u32[]{:S(2)}, u32[]{:S(2)}) collective-permute-start(bf16[16,2048]{1,0:T(8,128)(2,1)S(1)} %assemble.1.refs_1_.refs_0_), channel_id=1, source_target_pairs={{0,12},{4,8},{8,4},{12,0},{1,13},{5,9},{9,5},{13,1},{2,14},{6,10},... | collective-permute-start | bytes 196616 | tf_op jit(solution)/shard_map/gather_gx/ppermute | solution.py:286
  41.1 4.9 %collective-permute-start.14 = (bf16[16,2048]{1,0:T(8,128)(2,1)S(1)}, bf16[16,2048]{1,0:T(8,128)(2,1)S(1)}, u32[]{:S(2)}, u32[]{:S(2)}) collective-permute-start(bf16[16,2048]{1,0:T(8,128)(2,1)S(1)} %assemble.1.refs_1_.refs_0_), channel_id=1, source_target_pairs={{0,8},{4,12},{8,0},{12,4},{1,9},{5,13},{9,1},{13,5},{2,10},{6,14},... | collective-permute-start | bytes 196616 | tf_op jit(solution)/shard_map/gather_gx/ppermute | solution.py:286
  48.4 12.6 %collective-permute-start.17 = (bf16[16,4096]{1,0:T(8,128)(2,1)S(1)}, bf16[16,4096]{1,0:T(8,128)(2,1)S(1)}, u32[]{:S(2)}, u32[]{:S(2)}) collective-permute-start(bf16[16,4096]{1,0:T(8,128)(2,1)S(1)} %get-tuple-element.44), channel_id=1, source_target_pairs={{0,2},{1,3},{2,0},{3,1},{4,6},{5,7},{6,4},{7,5},{8,10},{9,11},{10,... | collective-permute-start | bytes 393224 | tf_op jit(solution)/shard_map/sum_gy/ppermute | solution.py:286
  50.4 10.6 %collective-permute-start.18 = (bf16[16,4096]{1,0:T(8,128)(2,1)S(1)}, bf16[16,4096]{1,0:T(8,128)(2,1)S(1)}, u32[]{:S(2)}, u32[]{:S(2)}) collective-permute-start(bf16[16,4096]{1,0:T(8,128)(2,1)S(1)} %get-tuple-element.45), channel_id=1, source_target_pairs={{0,3},{1,2},{2,1},{3,0},{4,7},{5,6},{6,5},{7,4},{8,11},{9,10},{10,... | collective-permute-start | bytes 393224 | tf_op jit(solution)/shard_map/sum_gy/ppermute | solution.py:286
  52.1 9.3 %collective-permute-start.19 = (bf16[16,4096]{1,0:T(8,128)(2,1)S(1)}, bf16[16,4096]{1,0:T(8,128)(2,1)S(1)}, u32[]{:S(2)}, u32[]{:S(2)}) collective-permute-start(bf16[16,4096]{1,0:T(8,128)(2,1)S(1)} %get-tuple-element.46), channel_id=1, source_target_pairs={{0,1},{1,0},{2,3},{3,2},{4,5},{5,4},{6,7},{7,6},{8,9},{9,8},{10,11... | collective-permute-start | bytes 393224 | tf_op jit(solution)/shard_map/sum_gy/ppermute | solution.py:286

commit v4 on v3

--- a/solution.py
+++ b/solution.py
@@ -11,7 +11,14 @@
 HEAD_SIZE = 128
 LANES = 128
 EPSILON = 1e-05
-ORDERS = {"hidden": (2, 3, 1), "sum_gx": (2, 3, 1), "to_owner": (3, 2, 1), "to_head_rows": (3, 2, 1), "gather_gx": (2, 3, 1), "sum_gy": (2, 3, 1)}
+ORDERS = {
+    "hidden": (2, 3, 1),
+    "sum_gx": (2, 1, 3),
+    "to_owner": (2, 3, 1),
+    "to_head_rows": (2, 3, 1),
+    "gather_gx": (2, 1, 3),
+    "sum_gy": (2, 1, 3),
+}
 CUTS = (0, 3, 5, 8)
 LOADS = len(CUTS) - 1
 VMEM = pl.BlockSpec(memory_space=pltpu.VMEM)
@@ -327,24 +334,13 @@
     out_rows, out_columns = w_output.shape
     cuts = [out_rows * cut // 8 for cut in CUTS]
 
-    def fetch(name, index, after):
-        first, last = cuts[index : index + 2]
-        return call(None, [], [], [], name, 4, loads=[(w_output, first, last - first)], after=[after])[1]
+    def load(index):
+        return w_output, cuts[index], cuts[index + 1] - cuts[index]
 
     with jax.named_scope("gather_hidden"):
         gathered = exchange([hidden_states] * count, "gy", "hidden")
     with jax.named_scope("fetch_query"):
-        table = array((share * group, HEAD_SIZE), jnp.float32)
-        (cosine, sine, filled), weights = call(
-            functools.partial(rotary_kernel, share),
-            [table, table, array(table.shape, jnp.int32)],
-            [],
-            [filled_lengths],
-            "fetch_query",
-            4,
-            scalars=1,
-            loads=[(w_query, 0, depth)],
-        )
+        _, weights = call(None, [], [], [], "fetch_query", 4, loads=[(w_query, 0, depth)])
     with jax.named_scope("project"):
         partial, output_weights = call(
             functools.partial(project_kernel, count, width),
@@ -359,12 +355,24 @@
             ],
             "project",
             8,
-            loads=[(w_output, cuts[0], cuts[1] - cuts[0])],
+            loads=[load(0)],
             flops=2 * count * rows * depth * used,
         )
     with jax.named_scope("sum_gx"):
         received = exchange(partial, "gx", "sum_gx")
-        output_weights += fetch("fetch_output", 1, partial[0])
+        table = array((share * group, HEAD_SIZE), jnp.float32)
+        (cosine, sine, filled), loaded = call(
+            functools.partial(rotary_kernel, share),
+            [table, table, array(table.shape, jnp.int32)],
+            [],
+            [filled_lengths],
+            "fetch_output",
+            4,
+            scalars=1,
+            loads=[load(1)],
+            after=partial[:1],
+        )
+        output_weights += loaded
         owned, _ = call(
             functools.partial(combine_kernel, count),
             [array((share, width))] * count,
@@ -412,7 +420,9 @@
         )
     with jax.named_scope("gather_gx"):
         blocks = exchange([block] * count, "gx", "gather_gx")
-        output_weights += fetch("fetch_output", 2, block)
+        output_weights += call(
+            None, [], [], [], "fetch_output", 4, loads=[load(2)], after=[block]
+        )[1]
     with jax.named_scope("output"):
         products, _ = call(
             functools.partial(output_kernel, count),

time: 62.3 us -> 60 us (0.963)
  starting transfers between devices: 22.5 us -> 21.4 us
  waiting for transfers between devices: 20.3 us -> 19.4 us
  local copies, waits for them, and re-layouts: 0.68 us -> 0.03 us
    ppermute x12, waiting for transfers between devices: 15.7 us -> 13.1 us  [exchange(): lax.ppermute(pieces[offset], axis, [(n, n ^ offset) for n in range(count)])]
    ppermute x8, starting transfers between devices: 8.59 us -> 6.81 us  [crossing_exchange(): lax.ppermute(pieces[offset], ('gx', 'gy'), [(n, n ^ count ^ offset) for n...]
    ppermute x8, waiting for transfers between devices: 4.58 us -> 6.32 us  [crossing_exchange(): lax.ppermute(pieces[offset], ('gx', 'gy'), [(n, n ^ count ^ offset) for n...]
    ppermute x12, starting transfers between devices: 13.9 us -> 14.6 us  [exchange(): lax.ppermute(pieces[offset], axis, [(n, n ^ offset) for n in range(count)])]
    unnamed x14, local copies, waits for them, and re-layouts: 0.68 us -> 0.03 us
  transfers between devices with their start and end apart: 20 -> 20, of which waited for: 10 -> 10; matrix products, arithmetic and copies ran while one was open for 0% -> 0% of each run, Pallas kernels for 18% -> 19%
where the time goes in v4:
time: 60 us; the launch traced here: 59.6 us
  starting transfers between devices  21.4 us (36%)
  waiting for transfers between devices  19.4 us (32%)
  Pallas kernels  18.5 us (31%)
    pallas_call x9, Pallas kernels, call(): pl.pallas_call(functools.partial(loading, kernel, parts, (len(after), len...  18.5 us
    ppermute x12, starting transfers between devices, exchange(): lax.ppermute(pieces[offset], axis, [(n, n ^ offset) for n in range(count)])  14.6 us
    ppermute x12, waiting for transfers between devices, exchange(): lax.ppermute(pieces[offset], axis, [(n, n ^ offset) for n in range(count)])  13.1 us
    ppermute x8, starting transfers between devices, crossing_exchange(): lax.ppermute(pieces[offset], ('gx', 'gy'), [(n, n ^ count ^ offset) for n...  6.81 us
    ppermute x8, waiting for transfers between devices, crossing_exchange(): lax.ppermute(pieces[offset], ('gx', 'gy'), [(n, n ^ count ^ offset) for n...  6.32 us
  transfers between devices with their start and end apart: 20, of which 10 were waited for; matrix products, arithmetic and copies ran while one was open for 0% of the time, Pallas kernels for 19%

profile of v4, /device:TPU:0, one launch (start us, length us, event | category | flops | bytes accessed | tf_op | source)
XLA Modules:
  0.0 59.6 jit_solution(3012195231003234948)
XLA Ops:
  0.0 0.0 copy-start.4
  0.0 0.0 copy-start.1
  0.0 0.0 copy-start
  0.0 0.0 copy-start.5
  0.0 5.1 %collective-permute-start.1 = (bf16[16,4096]{1,0:T(8,128)(2,1)}, bf16[16,4096]{1,0:T(8,128)(2,1)S(1)}, u32[]{:S(2)}, u32[]{:S(2)}) collective-permute-start(bf16[16,4096]{1,0:T(8,128)(2,1)} %refs_1_.1), channel_id=1, source_target_pairs={{0,3},{1,2},{2,1},{3,0},{4,7},{5,6},{6,5},{7,4},{8,11},{9,10},{10,... | collective-permute-start | bytes 393224 | tf_op jit(solution)/shard_map/gather_hidden/ppermute | solution.py:293
  5.1 0.0 collective-permute-start
  5.1 0.6 %collective-permute-start.2 = (bf16[16,4096]{1,0:T(8,128)(2,1)}, bf16[16,4096]{1,0:T(8,128)(2,1)S(1)}, u32[]{:S(2)}, u32[]{:S(2)}) collective-permute-start(bf16[16,4096]{1,0:T(8,128)(2,1)} %refs_1_.1), channel_id=1, source_target_pairs={{0,1},{1,0},{2,3},{3,2},{4,5},{5,4},{6,7},{7,6},{8,9},{9,8},{10,11... | collective-permute-start | bytes 393224 | tf_op jit(solution)/shard_map/gather_hidden/ppermute | solution.py:293
  5.8 5.8 %fetch_query.1.refs_6_ = bf16[4096,2048]{1,0:T(8,128)(2,1)S(1)} custom-call(bf16[4096,2048]{1,0:T(8,128)(2,1)} %refs_0_.4), custom_call_target="tpu_custom_call" | custom-call | bytes 33619968 | tf_op jit(solution)/shard_map/fetch_query/fetch_query/pallas_call | solution.py:260
  11.6 0.0 copy-start.6
  11.6 0.0 collective-permute-done.1.refs_3_
  11.6 4.8 %collective-permute-done.refs_2_ = bf16[16,4096]{1,0:T(8,128)(2,1)S(1)} collective-permute-done((bf16[16,4096]{1,0:T(8,128)(2,1)}, bf16[16,4096]{1,0:T(8,128)(2,1)S(1)}, u32[]{:S(2)}, u32[]{:S(2)}) %collective-permute-start) | collective-permute-done | bytes 131104 | tf_op jit(solution)/shard_map/gather_hidden/ppermute | solution.py:293
  16.4 0.0 collective-permute-done.2.refs_4_
  16.4 0.0 copy-done.4
  16.4 0.0 copy-done.1
  16.4 0.0 copy-done
  16.4 0.0 copy-done.5
  16.5 3.0 %project.1 = (bf16[16,2432]{1,0:T(8,128)(2,1)S(1)}, bf16[16,2432]{1,0:T(8,128)(2,1)S(1)}, bf16[16,2432]{1,0:T(8,128)(2,1)S(1)}, bf16[16,2432]{1,0:T(8,128)(2,1)S(1)}, bf16[768,4096]{1,0:T(8,128)(2,1)S(1)}) custom-call(bf16[2048,4096]{1,0:T(8,128)(2,1)} %refs_0_.7, bf16[16,4096]{1,0:T(8,128)(2,1)S(1)} %copy-done.4, ...), custom_call_target="tpu_custom_call" | custom-call | flops 1207959552 | bytes 12648448 | tf_op jit(solution)/shard_map/project/project/pallas_call | solution.py:260
  19.5 0.0 copy-start.2
  19.5 0.0 copy-start.3
  19.5 1.6 %collective-permute-start.3 = (bf16[16,2432]{1,0:T(8,128)(2,1)S(1)}, bf16[16,2432]{1,0:T(8,128)(2,1)S(1)}, u32[]{:S(2)}, u32[]{:S(2)}) collective-permute-start(bf16[16,2432]{1,0:T(8,128)(2,1)S(1)} %get-tuple-element.28), channel_id=1, source_target_pairs={{0,8},{4,12},{8,0},{12,4},{1,9},{5,13},{9,1},{13,5},{2,10},{6,14},... | collective-permute-start | bytes 233480 | tf_op jit(solution)/shard_map/sum_gx/ppermute | solution.py:293
  21.0 0.0 collective-permute-start.4
  21.0 0.6 %collective-permute-start.5 = (bf16[16,2432]{1,0:T(8,128)(2,1)S(1)}, bf16[16,2432]{1,0:T(8,128)(2,1)S(1)}, u32[]{:S(2)}, u32[]{:S(2)}) collective-permute-start(bf16[16,2432]{1,0:T(8,128)(2,1)S(1)} %get-tuple-element.30), channel_id=1, source_target_pairs={{0,12},{4,8},{8,4},{12,0},{1,13},{5,9},{9,5},{13,1},{2,14},{6,10},... | collective-permute-start | bytes 233480 | tf_op jit(solution)/shard_map/sum_gx/ppermute | solution.py:293
  21.7 0.0 copy-done.6
  21.7 2.7 %fetch_output.2 = (f32[64,128]{1,0:T(8,128)S(1)}, f32[64,128]{1,0:T(8,128)S(1)}, s32[64,128]{1,0:T(8,128)S(1)}, bf16[512,4096]{1,0:T(8,128)(2,1)S(1)}) custom-call(bf16[2048,4096]{1,0:T(8,128)(2,1)} %refs_0_.7, bf16[16,2432]{1,0:T(8,128)(2,1)S(1)} %get-tuple-element.26.refs_1_, s32[4]{0:T(128)S(1)} %copy-done.6), custom_call_target="tpu_custom_call" | custom-call | bytes 8454144 | tf_op jit(solution)/shard_map/sum_gx/fetch_output/pallas_call | solution.py:260
  24.4 0.0 collective-permute-done.3.refs_2_
  24.4 0.0 collective-permute-done.4.refs_3_
  24.5 0.6 collective-permute-done.5.refs_4_
  25.0 0.1 combine.1
  25.2 0.5 collective-permute-start.6
  25.7 0.0 collective-permute-start.7
  25.7 2.2 %collective-permute-start.8 = (bf16[4,2432]{1,0:T(4,128)(2,1)S(1)}, bf16[4,2432]{1,0:T(4,128)(2,1)S(1)}, u32[]{:S(2)}, u32[]{:S(2)}) collective-permute-start(bf16[4,2432]{1,0:T(4,128)(2,1)S(1)} %get-tuple-element.33), channel_id=1, source_target_pairs={{0,7},{1,6},{2,5},{3,4},{4,3},{5,2},{6,1},{7,0},{8,15},{9,14},{10,... | collective-permute-start | bytes 58376 | tf_op jit(solution)/shard_map/to_owner/ppermute | solution.py:303
  27.9 0.7 %collective-permute-start.9 = (bf16[4,2432]{1,0:T(4,128)(2,1)S(1)}, bf16[4,2432]{1,0:T(4,128)(2,1)S(1)}, u32[]{:S(2)}, u32[]{:S(2)}) collective-permute-start(bf16[4,2432]{1,0:T(4,128)(2,1)S(1)} %get-tuple-element.34), channel_id=1, source_target_pairs={{0,5},{1,4},{2,7},{3,6},{4,1},{5,0},{6,3},{7,2},{8,13},{9,12},{10,... | collective-permute-start | bytes 58376 | tf_op jit(solution)/shard_map/to_owner/ppermute | solution.py:303
  28.6 0.0 collective-permute-done.6.refs_0_
  28.6 1.2 %collective-permute-done.7.refs_1_ = bf16[4,2432]{1,0:T(4,128)(2,1)S(1)} collective-permute-done((bf16[4,2432]{1,0:T(4,128)(2,1)S(1)}, bf16[4,2432]{1,0:T(4,128)(2,1)S(1)}, u32[]{:S(2)}, u32[]{:S(2)}) %collective-permute-start.7) | collective-permute-done | bytes 19488 | tf_op jit(solution)/shard_map/to_owner/ppermute | solution.py:303
  29.8 0.9 %collective-permute-done.8.refs_2_ = bf16[4,2432]{1,0:T(4,128)(2,1)S(1)} collective-permute-done((bf16[4,2432]{1,0:T(4,128)(2,1)S(1)}, bf16[4,2432]{1,0:T(4,128)(2,1)S(1)}, u32[]{:S(2)}, u32[]{:S(2)}) %collective-permute-start.8) | collective-permute-done | bytes 19488 | tf_op jit(solution)/shard_map/to_owner/ppermute | solution.py:303
  30.7 0.5 collective-permute-done.9.refs_3_
  31.2 0.0 copy-done.2
  31.2 0.0 copy-done.3
  31.2 1.0 %attend.1 = (bf16[4,2048]{1,0:T(4,128)(2,1)S(1)}, bf16[4,2048]{1,0:T(4,128)(2,1)S(1)}, bf16[4,2048]{1,0:T(4,128)(2,1)S(1)}, bf16[4,2048]{1,0:T(4,128)(2,1)S(1)}) custom-call(bf16[4,2432]{1,0:T(4,128)(2,1)S(1)} %collective-permute-done.6.refs_0_, bf16[4,2432]{1,0:T(4,128)(2,1)S(1)} %collective-permute-done.7.refs_1_, ...), custom_call_target="tpu_custom_call" | custom-call | bytes 65536 | tf_op jit(solution)/shard_map/attend/attend/pallas_call | solution.py:260
  32.3 0.3 collective-permute-start.10
  32.6 1.8 %collective-permute-start.11 = (bf16[4,2048]{1,0:T(4,128)(2,1)S(1)}, bf16[4,2048]{1,0:T(4,128)(2,1)S(1)}, u32[]{:S(2)}, u32[]{:S(2)}) collective-permute-start(bf16[4,2048]{1,0:T(4,128)(2,1)S(1)} %get-tuple-element.39), channel_id=1, source_target_pairs={{0,6},{1,7},{2,4},{3,5},{4,2},{5,3},{6,0},{7,1},{8,14},{9,15},{10,... | collective-permute-start | bytes 49160 | tf_op jit(solution)/shard_map/to_head_rows/ppermute | solution.py:303
  34.3 1.1 %collective-permute-start.12 = (bf16[4,2048]{1,0:T(4,128)(2,1)S(1)}, bf16[4,2048]{1,0:T(4,128)(2,1)S(1)}, u32[]{:S(2)}, u32[]{:S(2)}) collective-permute-start(bf16[4,2048]{1,0:T(4,128)(2,1)S(1)} %get-tuple-element.40), channel_id=1, source_target_pairs={{0,7},{1,6},{2,5},{3,4},{4,3},{5,2},{6,1},{7,0},{8,15},{9,14},{10,... | collective-permute-start | bytes 49160 | tf_op jit(solution)/shard_map/to_head_rows/ppermute | solution.py:303
  35.4 0.2 collective-permute-start.13
  35.6 0.0 collective-permute-done.10.refs_0_
  35.6 1.0 %collective-permute-done.11.refs_1_ = bf16[4,2048]{1,0:T(4,128)(2,1)S(1)} collective-permute-done((bf16[4,2048]{1,0:T(4,128)(2,1)S(1)}, bf16[4,2048]{1,0:T(4,128)(2,1)S(1)}, u32[]{:S(2)}, u32[]{:S(2)}) %collective-permute-start.11) | collective-permute-done | bytes 16416 | tf_op jit(solution)/shard_map/to_head_rows/ppermute | solution.py:303
  36.6 2.7 %collective-permute-done.12.refs_2_ = bf16[4,2048]{1,0:T(4,128)(2,1)S(1)} collective-permute-done((bf16[4,2048]{1,0:T(4,128)(2,1)S(1)}, bf16[4,2048]{1,0:T(4,128)(2,1)S(1)}, u32[]{:S(2)}, u32[]{:S(2)}) %collective-permute-start.12) | collective-permute-done | bytes 16416 | tf_op jit(solution)/shard_map/to_head_rows/ppermute | solution.py:303
  39.3 0.0 collective-permute-done.13.refs_3_
  39.4 1.2 %collective-permute-start.16 = (bf16[16,2048]{1,0:T(8,128)(2,1)S(1)}, bf16[16,2048]{1,0:T(8,128)(2,1)S(1)}, u32[]{:S(2)}, u32[]{:S(2)}) collective-permute-start(bf16[16,2048]{1,0:T(8,128)(2,1)S(1)} %assemble.1.refs_1_.refs_0_), channel_id=1, source_target_pairs={{0,12},{4,8},{8,4},{12,0},{1,13},{5,9},{9,5},{13,1},{2,14},{6,10},... | collective-permute-start | bytes 196616 | tf_op jit(solution)/shard_map/gather_gx/ppermute | solution.py:293
  40.5 0.3 collective-permute-start.15
  40.9 0.7 %collective-permute-start.14 = (bf16[16,2048]{1,0:T(8,128)(2,1)S(1)}, bf16[16,2048]{1,0:T(8,128)(2,1)S(1)}, u32[]{:S(2)}, u32[]{:S(2)}) collective-permute-start(bf16[16,2048]{1,0:T(8,128)(2,1)S(1)} %assemble.1.refs_1_.refs_0_), channel_id=1, source_target_pairs={{0,8},{4,12},{8,0},{12,4},{1,9},{5,13},{9,1},{13,5},{2,10},{6,14},... | collective-permute-start | bytes 196616 | tf_op jit(solution)/shard_map/gather_gx/ppermute | solution.py:293
  41.6 2.8 %fetch_output.3.refs_6_ = bf16[768,4096]{1,0:T(8,128)(2,1)S(1)} custom-call(bf16[2048,4096]{1,0:T(8,128)(2,1)} %refs_0_.7, bf16[16,2048]{1,0:T(8,128)(2,1)S(1)} %assemble.1.refs_1_.refs_0_), custom_call_target="tpu_custom_call" | custom-call | bytes 12648448 | tf_op jit(solution)/shard_map/gather_gx/fetch_output/pallas_call | solution.py:260
  44.4 0.0 collective-permute-done.16.refs_3_
  44.4 0.0 collective-permute-done.15.refs_2_
  44.4 0.8 %collective-permute-done.14.refs_1_ = bf16[16,2048]{1,0:T(8,128)(2,1)S(1)} collective-permute-done((bf16[16,2048]{1,0:T(8,128)(2,1)S(1)}, bf16[16,2048]{1,0:T(8,128)(2,1)S(1)}, u32[]{:S(2)}, u32[]{:S(2)}) %collective-permute-start.14) | collective-permute-done | bytes 65568 | tf_op jit(solution)/shard_map/gather_gx/ppermute | solution.py:293
  45.2 2.4 %output.1 = (bf16[16,4096]{1,0:T(8,128)(2,1)S(1)}, bf16[16,4096]{1,0:T(8,128)(2,1)S(1)}, bf16[16,4096]{1,0:T(8,128)(2,1)S(1)}, bf16[16,4096]{1,0:T(8,128)(2,1)S(1)}) custom-call(bf16[16,2048]{1,0:T(8,128)(2,1)S(1)} %assemble.1.refs_1_.refs_0_, bf16[16,2048]{1,0:T(8,128)(2,1)S(1)} %collective-permute-done.14.refs_1_, ...), custom_call_target="tpu_custom_call" | custom-call | flops 1073741824 | bytes 65536 | tf_op jit(solution)/shard_map/output/output/pallas_call | solution.py:260
  47.6 0.8 %collective-permute-start.17 = (bf16[16,4096]{1,0:T(8,128)(2,1)S(1)}, bf16[16,4096]{1,0:T(8,128)(2,1)S(1)}, u32[]{:S(2)}, u32[]{:S(2)}) collective-permute-start(bf16[16,4096]{1,0:T(8,128)(2,1)S(1)} %get-tuple-element.44), channel_id=1, source_target_pairs={{0,2},{1,3},{2,0},{3,1},{4,6},{5,7},{6,4},{7,5},{8,10},{9,11},{10,... | collective-permute-start | bytes 393224 | tf_op jit(solution)/shard_map/sum_gy/ppermute | solution.py:293
  48.4 1.7 %collective-permute-start.18 = (bf16[16,4096]{1,0:T(8,128)(2,1)S(1)}, bf16[16,4096]{1,0:T(8,128)(2,1)S(1)}, u32[]{:S(2)}, u32[]{:S(2)}) collective-permute-start(bf16[16,4096]{1,0:T(8,128)(2,1)S(1)} %get-tuple-element.45), channel_id=1, source_target_pairs={{0,1},{1,0},{2,3},{3,2},{4,5},{5,4},{6,7},{7,6},{8,9},{9,8},{10,11... | collective-permute-start | bytes 393224 | tf_op jit(solution)/shard_map/sum_gy/ppermute | solution.py:293
  50.1 2.0 %collective-permute-start.19 = (bf16[16,4096]{1,0:T(8,128)(2,1)S(1)}, bf16[16,4096]{1,0:T(8,128)(2,1)S(1)}, u32[]{:S(2)}, u32[]{:S(2)}) collective-permute-start(bf16[16,4096]{1,0:T(8,128)(2,1)S(1)} %get-tuple-element.46), channel_id=1, source_target_pairs={{0,3},{1,2},{2,1},{3,0},{4,7},{5,6},{6,5},{7,4},{8,11},{9,10},{10,... | collective-permute-start | bytes 393224 | tf_op jit(solution)/shard_map/sum_gy/ppermute | solution.py:293
  52.0 6.5 %collective-permute-done.17.refs_1_ = bf16[16,4096]{1,0:T(8,128)(2,1)S(1)} collective-permute-done((bf16[16,4096]{1,0:T(8,128)(2,1)S(1)}, bf16[16,4096]{1,0:T(8,128)(2,1)S(1)}, u32[]{:S(2)}, u32[]{:S(2)}) %collective-permute-start.17) | collective-permute-done | bytes 131104 | tf_op jit(solution)/shard_map/sum_gy/ppermute | solution.py:293
  58.5 0.4 collective-permute-done.18.refs_2_
  58.9 0.0 collective-permute-done.19.refs_3_
  58.9 0.7 %add.1 = bf16[16,4096]{1,0:T(8,128)(2,1)} custom-call(bf16[16,4096]{1,0:T(8,128)(2,1)S(1)} %get-tuple-element.43.refs_0_, bf16[16,4096]{1,0:T(8,128)(2,1)S(1)} %collective-permute-done.17.refs_1_, bf16[16,4096]{1,0:T(8,128)(2,1)S(1)} %collective-permute-done.18.refs_2_, bf16[16,4096]{1,0:T(8,128)(2,1)S(1)} %collective-permute-done.19.refs_3_), custom_call_target="tpu_custom_call" | custom-call | bytes 65536 | tf_op jit(solution)/shard_map/sum_gy/add/pallas_call | solution.py:260
  (1 shorter events, 0.0 us)
Async XLA Ops:
  0.0 16.4 %copy-start.4 = (bf16[16,4096]{1,0:T(8,128)(2,1)S(1)}, bf16[16,4096]{1,0:T(8,128)(2,1)}, u32[]{:S(2)}) copy-start(bf16[16,4096]{1,0:T(8,128)(2,1)} %refs_1_.1) | copy-start | bytes 393220
  0.0 16.4 %copy-start.1 = (bf16[4096,128]{1,0:T(8,128)(2,1)S(1)}, bf16[4096,128]{1,0:T(8,128)(2,1)}, u32[]{:S(2)}) copy-start(bf16[4096,128]{1,0:T(8,128)(2,1)} %refs_8_.1) | copy-start | bytes 3145732
  0.0 16.4 %copy-start = (bf16[4096,128]{1,0:T(8,128)(2,1)S(1)}, bf16[4096,128]{1,0:T(8,128)(2,1)}, u32[]{:S(2)}) copy-start(bf16[4096,128]{1,0:T(8,128)(2,1)} %refs_7_.1) | copy-start | bytes 3145732
  0.0 16.4 %copy-start.5 = (bf16[4096]{0:T(1024)(128)(2,1)S(1)}, bf16[4096]{0:T(1024)(128)(2,1)}, u32[]{:S(2)}) copy-start(bf16[4096]{0:T(1024)(128)(2,1)} %refs_5_.2) | copy-start | bytes 24580
  0.0 11.6 %collective-permute-start.1 = (bf16[16,4096]{1,0:T(8,128)(2,1)}, bf16[16,4096]{1,0:T(8,128)(2,1)S(1)}, u32[]{:S(2)}, u32[]{:S(2)}) collective-permute-start(bf16[16,4096]{1,0:T(8,128)(2,1)} %refs_1_.1), channel_id=1, source_target_pairs={{0,3},{1,2},{2,1},{3,0},{4,7},{5,6},{6,5},{7,4},{8,11},{9,10},{10,... | collective-permute-start | bytes 393224 | tf_op jit(solution)/shard_map/gather_hidden/ppermute | solution.py:293
  5.1 11.3 %collective-permute-start = (bf16[16,4096]{1,0:T(8,128)(2,1)}, bf16[16,4096]{1,0:T(8,128)(2,1)S(1)}, u32[]{:S(2)}, u32[]{:S(2)}) collective-permute-start(bf16[16,4096]{1,0:T(8,128)(2,1)} %refs_1_.1), channel_id=1, source_target_pairs={{0,2},{1,3},{2,0},{3,1},{4,6},{5,7},{6,4},{7,5},{8,10},{9,11},{10,... | collective-permute-start | bytes 393224 | tf_op jit(solution)/shard_map/gather_hidden/ppermute | solution.py:293
  5.1 11.3 %collective-permute-start.2 = (bf16[16,4096]{1,0:T(8,128)(2,1)}, bf16[16,4096]{1,0:T(8,128)(2,1)S(1)}, u32[]{:S(2)}, u32[]{:S(2)}) collective-permute-start(bf16[16,4096]{1,0:T(8,128)(2,1)} %refs_1_.1), channel_id=1, source_target_pairs={{0,1},{1,0},{2,3},{3,2},{4,5},{5,4},{6,7},{7,6},{8,9},{9,8},{10,11... | collective-permute-start | bytes 393224 | tf_op jit(solution)/shard_map/gather_hidden/ppermute | solution.py:293
  11.6 10.1 %copy-start.6 = (s32[4]{0:T(128)S(1)}, s32[4]{0:T(128)}, u32[]{:S(2)}) copy-start(s32[4]{0:T(128)} %refs_2_.1) | copy-start | bytes 52
  19.5 11.8 %copy-start.2 = (bf16[4,256,512]{2,1,0:T(8,128)(2,1)S(1)}, bf16[4,256,512]{2,1,0:T(8,128)(2,1)}, u32[]{:S(2)}) copy-start(bf16[4,256,512]{2,1,0:T(8,128)(2,1)} %refs_4_.1) | copy-start | bytes 3145732
  19.5 11.8 %copy-start.3 = (bf16[4,256,512]{2,1,0:T(8,128)(2,1)S(1)}, bf16[4,256,512]{2,1,0:T(8,128)(2,1)}, u32[]{:S(2)}) copy-start(bf16[4,256,512]{2,1,0:T(8,128)(2,1)} %refs_5_.3) | copy-start | bytes 3145732
  19.5 5.0 %collective-permute-start.3 = (bf16[16,2432]{1,0:T(8,128)(2,1)S(1)}, bf16[16,2432]{1,0:T(8,128)(2,1)S(1)}, u32[]{:S(2)}, u32[]{:S(2)}) collective-permute-start(bf16[16,2432]{1,0:T(8,128)(2,1)S(1)} %get-tuple-element.28), channel_id=1, source_target_pairs={{0,8},{4,12},{8,0},{12,4},{1,9},{5,13},{9,1},{13,5},{2,10},{6,14},... | collective-permute-start | bytes 233480 | tf_op jit(solution)/shard_map/sum_gx/ppermute | solution.py:293
  21.0 3.4 %collective-permute-start.4 = (bf16[16,2432]{1,0:T(8,128)(2,1)S(1)}, bf16[16,2432]{1,0:T(8,128)(2,1)S(1)}, u32[]{:S(2)}, u32[]{:S(2)}) collective-permute-start(bf16[16,2432]{1,0:T(8,128)(2,1)S(1)} %get-tuple-element.29), channel_id=1, source_target_pairs={{0,4},{4,0},{8,12},{12,8},{1,5},{5,1},{9,13},{13,9},{2,6},{6,2},{1... | collective-permute-start | bytes 233480 | tf_op jit(solution)/shard_map/sum_gx/ppermute | solution.py:293
  21.0 4.0 %collective-permute-start.5 = (bf16[16,2432]{1,0:T(8,128)(2,1)S(1)}, bf16[16,2432]{1,0:T(8,128)(2,1)S(1)}, u32[]{:S(2)}, u32[]{:S(2)}) collective-permute-start(bf16[16,2432]{1,0:T(8,128)(2,1)S(1)} %get-tuple-element.30), channel_id=1, source_target_pairs={{0,12},{4,8},{8,4},{12,0},{1,13},{5,9},{9,5},{13,1},{2,14},{6,10},... | collective-permute-start | bytes 233480 | tf_op jit(solution)/shard_map/sum_gx/ppermute | solution.py:293
  25.2 3.4 %collective-permute-start.6 = (bf16[4,2432]{1,0:T(4,128)(2,1)S(1)}, bf16[4,2432]{1,0:T(4,128)(2,1)S(1)}, u32[]{:S(2)}, u32[]{:S(2)}) collective-permute-start(bf16[4,2432]{1,0:T(4,128)(2,1)S(1)} %get-tuple-element.31), channel_id=1, source_target_pairs={{0,4},{1,5},{2,6},{3,7},{4,0},{5,1},{6,2},{7,3},{8,12},{9,13},{10,... | collective-permute-start | bytes 58376 | tf_op jit(solution)/shard_map/to_owner/ppermute | solution.py:303
  25.7 4.1 %collective-permute-start.7 = (bf16[4,2432]{1,0:T(4,128)(2,1)S(1)}, bf16[4,2432]{1,0:T(4,128)(2,1)S(1)}, u32[]{:S(2)}, u32[]{:S(2)}) collective-permute-start(bf16[4,2432]{1,0:T(4,128)(2,1)S(1)} %get-tuple-element.32), channel_id=1, source_target_pairs={{0,6},{1,7},{2,4},{3,5},{4,2},{5,3},{6,0},{7,1},{8,14},{9,15},{10,... | collective-permute-start | bytes 58376 | tf_op jit(solution)/shard_map/to_owner/ppermute | solution.py:303
  25.7 5.0 %collective-permute-start.8 = (bf16[4,2432]{1,0:T(4,128)(2,1)S(1)}, bf16[4,2432]{1,0:T(4,128)(2,1)S(1)}, u32[]{:S(2)}, u32[]{:S(2)}) collective-permute-start(bf16[4,2432]{1,0:T(4,128)(2,1)S(1)} %get-tuple-element.33), channel_id=1, source_target_pairs={{0,7},{1,6},{2,5},{3,4},{4,3},{5,2},{6,1},{7,0},{8,15},{9,14},{10,... | collective-permute-start | bytes 58376 | tf_op jit(solution)/shard_map/to_owner/ppermute | solution.py:303
  27.9 3.3 %collective-permute-start.9 = (bf16[4,2432]{1,0:T(4,128)(2,1)S(1)}, bf16[4,2432]{1,0:T(4,128)(2,1)S(1)}, u32[]{:S(2)}, u32[]{:S(2)}) collective-permute-start(bf16[4,2432]{1,0:T(4,128)(2,1)S(1)} %get-tuple-element.34), channel_id=1, source_target_pairs={{0,5},{1,4},{2,7},{3,6},{4,1},{5,0},{6,3},{7,2},{8,13},{9,12},{10,... | collective-permute-start | bytes 58376 | tf_op jit(solution)/shard_map/to_owner/ppermute | solution.py:303
  32.3 3.4 %collective-permute-start.10 = (bf16[4,2048]{1,0:T(4,128)(2,1)S(1)}, bf16[4,2048]{1,0:T(4,128)(2,1)S(1)}, u32[]{:S(2)}, u32[]{:S(2)}) collective-permute-start(bf16[4,2048]{1,0:T(4,128)(2,1)S(1)} %get-tuple-element.38), channel_id=1, source_target_pairs={{0,4},{1,5},{2,6},{3,7},{4,0},{5,1},{6,2},{7,3},{8,12},{9,13},{10,... | collective-permute-start | bytes 49160 | tf_op jit(solution)/shard_map/to_head_rows/ppermute | solution.py:303
  32.6 4.1 %collective-permute-start.11 = (bf16[4,2048]{1,0:T(4,128)(2,1)S(1)}, bf16[4,2048]{1,0:T(4,128)(2,1)S(1)}, u32[]{:S(2)}, u32[]{:S(2)}) collective-permute-start(bf16[4,2048]{1,0:T(4,128)(2,1)S(1)} %get-tuple-element.39), channel_id=1, source_target_pairs={{0,6},{1,7},{2,4},{3,5},{4,2},{5,3},{6,0},{7,1},{8,14},{9,15},{10,... | collective-permute-start | bytes 49160 | tf_op jit(solution)/shard_map/to_head_rows/ppermute | solution.py:303
  34.3 5.0 %collective-permute-start.12 = (bf16[4,2048]{1,0:T(4,128)(2,1)S(1)}, bf16[4,2048]{1,0:T(4,128)(2,1)S(1)}, u32[]{:S(2)}, u32[]{:S(2)}) collective-permute-start(bf16[4,2048]{1,0:T(4,128)(2,1)S(1)} %get-tuple-element.40), channel_id=1, source_target_pairs={{0,7},{1,6},{2,5},{3,4},{4,3},{5,2},{6,1},{7,0},{8,15},{9,14},{10,... | collective-permute-start | bytes 49160 | tf_op jit(solution)/shard_map/to_head_rows/ppermute | solution.py:303
  35.4 3.9 %collective-permute-start.13 = (bf16[4,2048]{1,0:T(4,128)(2,1)S(1)}, bf16[4,2048]{1,0:T(4,128)(2,1)S(1)}, u32[]{:S(2)}, u32[]{:S(2)}) collective-permute-start(bf16[4,2048]{1,0:T(4,128)(2,1)S(1)} %get-tuple-element.41), channel_id=1, source_target_pairs={{0,5},{1,4},{2,7},{3,6},{4,1},{5,0},{6,3},{7,2},{8,13},{9,12},{10,... | collective-permute-start | bytes 49160 | tf_op jit(solution)/shard_map/to_head_rows/ppermute | solution.py:303
  39.4 5.0 %collective-permute-start.16 = (bf16[16,2048]{1,0:T(8,128)(2,1)S(1)}, bf16[16,2048]{1,0:T(8,128)(2,1)S(1)}, u32[]{:S(2)}, u32[]{:S(2)}) collective-permute-start(bf16[16,2048]{1,0:T(8,128)(2,1)S(1)} %assemble.1.refs_1_.refs_0_), channel_id=1, source_target_pairs={{0,12},{4,8},{8,4},{12,0},{1,13},{5,9},{9,5},{13,1},{2,14},{6,10},... | collective-permute-start | bytes 196616 | tf_op jit(solution)/shard_map/gather_gx/ppermute | solution.py:293
  40.5 3.8 %collective-permute-start.15 = (bf16[16,2048]{1,0:T(8,128)(2,1)S(1)}, bf16[16,2048]{1,0:T(8,128)(2,1)S(1)}, u32[]{:S(2)}, u32[]{:S(2)}) collective-permute-start(bf16[16,2048]{1,0:T(8,128)(2,1)S(1)} %assemble.1.refs_1_.refs_0_), channel_id=1, source_target_pairs={{0,4},{4,0},{8,12},{12,8},{1,5},{5,1},{9,13},{13,9},{2,6},{6,2},{1... | collective-permute-start | bytes 196616 | tf_op jit(solution)/shard_map/gather_gx/ppermute | solution.py:293
  40.9 4.3 %collective-permute-start.14 = (bf16[16,2048]{1,0:T(8,128)(2,1)S(1)}, bf16[16,2048]{1,0:T(8,128)(2,1)S(1)}, u32[]{:S(2)}, u32[]{:S(2)}) collective-permute-start(bf16[16,2048]{1,0:T(8,128)(2,1)S(1)} %assemble.1.refs_1_.refs_0_), channel_id=1, source_target_pairs={{0,8},{4,12},{8,0},{12,4},{1,9},{5,13},{9,1},{13,5},{2,10},{6,14},... | collective-permute-start | bytes 196616 | tf_op jit(solution)/shard_map/gather_gx/ppermute | solution.py:293
  47.6 10.9 %collective-permute-start.17 = (bf16[16,4096]{1,0:T(8,128)(2,1)S(1)}, bf16[16,4096]{1,0:T(8,128)(2,1)S(1)}, u32[]{:S(2)}, u32[]{:S(2)}) collective-permute-start(bf16[16,4096]{1,0:T(8,128)(2,1)S(1)} %get-tuple-element.44), channel_id=1, source_target_pairs={{0,2},{1,3},{2,0},{3,1},{4,6},{5,7},{6,4},{7,5},{8,10},{9,11},{10,... | collective-permute-start | bytes 393224 | tf_op jit(solution)/shard_map/sum_gy/ppermute | solution.py:293
  48.4 10.5 %collective-permute-start.18 = (bf16[16,4096]{1,0:T(8,128)(2,1)S(1)}, bf16[16,4096]{1,0:T(8,128)(2,1)S(1)}, u32[]{:S(2)}, u32[]{:S(2)}) collective-permute-start(bf16[16,4096]{1,0:T(8,128)(2,1)S(1)} %get-tuple-element.45), channel_id=1, source_target_pairs={{0,1},{1,0},{2,3},{3,2},{4,5},{5,4},{6,7},{7,6},{8,9},{9,8},{10,11... | collective-permute-start | bytes 393224 | tf_op jit(solution)/shard_map/sum_gy/ppermute | solution.py:293
  50.1 8.8 %collective-permute-start.19 = (bf16[16,4096]{1,0:T(8,128)(2,1)S(1)}, bf16[16,4096]{1,0:T(8,128)(2,1)S(1)}, u32[]{:S(2)}, u32[]{:S(2)}) collective-permute-start(bf16[16,4096]{1,0:T(8,128)(2,1)S(1)} %get-tuple-element.46), channel_id=1, source_target_pairs={{0,3},{1,2},{2,1},{3,0},{4,7},{5,6},{6,5},{7,4},{8,11},{9,10},{10,... | collective-permute-start | bytes 393224 | tf_op jit(solution)/shard_map/sum_gy/ppermute | solution.py:293

commit v5 on v4

--- a/solution.py
+++ b/solution.py
@@ -21,6 +21,7 @@
 }
 CUTS = (0, 3, 5, 8)
 LOADS = len(CUTS) - 1
+FIRST = 4
 VMEM = pl.BlockSpec(memory_space=pltpu.VMEM)
 
 
@@ -183,16 +184,20 @@
     out[...] = jnp.concatenate([held[n] for n in range(count)], axis=0).astype(jnp.bfloat16)
 
 
-def output_kernel(count, *refs):
+def output_kernel(count, begin, earlier, *refs):
     pieces = [refs[order("gather_gx", count).index(offset)] for offset in range(count)]
     weights = refs[count : count + LOADS]
-    outs, (held,) = refs[count + LOADS : 2 * count + LOADS], refs[2 * count + LOADS :]
+    before = refs[count + LOADS : count + LOADS + earlier]
+    refs = refs[count + LOADS + earlier :]
+    outs, (held,) = refs[:count], refs[count:]
     flip = lax.axis_index("gx") ^ lax.axis_index("gy") ^ 1
     for offset in range(count):
         held[flip ^ offset] = pieces[offset][...]
+    if earlier:
+        outs[1][:, :begin] = before[0][...]
     rows = held.shape[1]
     left = padded(held[...].reshape(count * rows, held.shape[2]))
-    columns = weights[0].shape[1]
+    columns = outs[0].shape[1]
     step = min(columns, 512)
     for first in range(0, columns, step):
         product, start = 0.0, 0
@@ -200,20 +205,34 @@
             depth = weight.shape[0]
             product = product + jnp.dot(
                 left[:, start : start + depth],
-                weight[:, first : first + step],
+                weight[:, begin + first : begin + first + step],
                 preferred_element_type=jnp.float32,
             )
             start += depth
         product = product.astype(jnp.bfloat16)
         for offset in range(count):
-            outs[offset][:, first : first + step] = product[offset * rows : (offset + 1) * rows]
-
-
-def add_kernel(count, *refs):
-    total = refs[0][...].astype(jnp.float32)
-    for piece in refs[1:count]:
-        total = total + piece[...].astype(jnp.float32)
-    refs[count][...] = total.astype(jnp.bfloat16)
+            shift = begin if earlier and offset == 1 else 0
+            outs[offset][:, shift + first : shift + first + step] = product[
+                offset * rows : (offset + 1) * rows
+            ]
+
+
+def relay_kernel(mine, relayed, out):
+    out[...] = (mine[...].astype(jnp.float32) + relayed[...].astype(jnp.float32)).astype(
+        jnp.bfloat16
+    )
+
+
+def add_kernel(terms, *refs):
+    whole, out = refs[-2], refs[-1]
+    start = 0
+    for first in range(0, len(refs) - 2, terms):
+        end = start + refs[first].shape[1]
+        total = whole[:, start:end].astype(jnp.float32)
+        for piece in refs[first : first + terms]:
+            total = total + piece[...].astype(jnp.float32)
+        out[:, start:end] = total.astype(jnp.bfloat16)
+        start = end
 
 
 def rotary_kernel(share, lengths, cosines, sines, filled):
@@ -256,7 +275,8 @@
 def call(kernel, outs, scratch, args, name, limit, scalars=0, loads=(), flops=0, after=()):
     arrays = [pltpu.with_memory_space_constraint(load[0], pltpu.HBM) for load in loads]
     parts = [load[1:] for load in loads]
-    size = sum(2 * rows * array.shape[1] for array, _, rows in loads)
+    size = sum(4 * rows * array.shape[1] for array, _, rows in loads)
+    size += sum(a.size * a.dtype.itemsize for a in (*args, *outs))
     results = pl.pallas_call(
         functools.partial(loading, kernel, parts, (len(after), len(args), len(outs))),
         out_shape=[*outs, *(pltpu.VMEM((rows, a.shape[1]), a.dtype) for a, _, rows in loads)],
@@ -268,7 +288,7 @@
         scratch_shapes=scratch
         + ([pltpu.SemaphoreType.DMA((len(loads),))] if loads else []),
         cost_estimate=pl.CostEstimate(
-            flops=flops, bytes_accessed=2 * size + (1 << 16), transcendentals=0
+            flops=flops, bytes_accessed=size, transcendentals=0
         ),
         compiler_params=pltpu.CompilerParams(vmem_limit_bytes=limit << 20),
         name=name,
@@ -423,23 +443,49 @@
         output_weights += call(
             None, [], [], [], "fetch_output", 4, loads=[load(2)], after=[block]
         )[1]
-    with jax.named_scope("output"):
-        products, _ = call(
-            functools.partial(output_kernel, count),
-            [array((count * share, out_columns))] * count,
-            [pltpu.VMEM((count, count * share, query_columns), jnp.bfloat16)],
-            [*(blocks[k] for k in order("gather_gx", count)), *output_weights],
-            "output",
-            8,
-            flops=2 * count * count * share * out_rows * out_columns,
-        )
+    cut = out_columns * FIRST // 8
+    pair = [(n, n ^ 1) for n in range(count)]
+    terms, before = [], []
+    for begin, end in ((0, cut), (cut, out_columns)):
+        shapes = [(count * share, end - begin)] * count
+        if begin:
+            shapes[1] = (count * share, end)
+        with jax.named_scope("output"):
+            parts, _ = call(
+                functools.partial(output_kernel, count, begin, len(before)),
+                [array(shape) for shape in shapes],
+                [pltpu.VMEM((count, count * share, query_columns), jnp.bfloat16)],
+                [
+                    *(blocks[k] for k in order("gather_gx", count)),
+                    *output_weights,
+                    *before,
+                ],
+                "output",
+                8,
+                flops=2 * count * count * share * out_rows * (end - begin),
+            )
+        before = [parts[1]]
+        terms.append(parts[0])
+        with jax.named_scope("sum_gy"):
+            for offset in range(2, count, 2):
+                relayed = lax.ppermute(parts[offset + 1], "gy", pair)
+                (both,), _ = call(
+                    relay_kernel,
+                    [array(shapes[offset])],
+                    [],
+                    [parts[offset], relayed],
+                    "relay",
+                    4,
+                )
+                terms.append(
+                    lax.ppermute(both, "gy", [(n, n ^ offset) for n in range(count)])
+                )
     with jax.named_scope("sum_gy"):
-        products = exchange(products, "gy", "sum_gy")
         (result,), _ = call(
-            functools.partial(add_kernel, count),
+            functools.partial(add_kernel, len(terms) // 2),
             [array((rows, out_columns))],
             [],
-            [products[k] for k in order("sum_gy", count)],
+            [*terms, lax.ppermute(before[0], "gy", pair)],
             "add",
             8,
         )

time: 60 us -> 59.7 us (level)
  waiting for transfers between devices: 19.4 us -> 18.5 us
  starting transfers between devices: 21.4 us -> 22.1 us
    ppermute x12 -> x9, waiting for transfers between devices: 13.1 us -> 6.28 us  [exchange(): lax.ppermute(pieces[offset], axis, [(n, n ^ offset) for n in range(count)])]
    ppermute x0 -> x5, waiting for transfers between devices: none -> 5.94 us  [the longest x2 3.4 us: per_device(): lax.ppermute(both, 'gy', [(n, n ^ offset) for n in range(count)])]
    ppermute x0 -> x5, starting transfers between devices: none -> 5.07 us  [the longest x2 2.84 us: per_device(): lax.ppermute(both, 'gy', [(n, n ^ offset) for n in range(count)])]
    ppermute x12 -> x9, starting transfers between devices: 14.6 us -> 10.2 us  [exchange(): lax.ppermute(pieces[offset], axis, [(n, n ^ offset) for n in range(count)])]
    pallas_call x9 -> x12, Pallas kernels: 18.5 us -> 18.7 us  [call(): pl.pallas_call(functools.partial(loading, kernel, parts, (len(after), len...]
  transfers between devices with their start and end apart: 20 -> 22, of which waited for: 10 -> 12; matrix products, arithmetic and copies ran while one was open for 0% -> 0% of each run, Pallas kernels for 19% -> 21%
where the time goes in v5:
time: 59.7 us; the launch traced here: 59.5 us
  starting transfers between devices  22.1 us (37%)
  Pallas kernels  18.7 us (31%)
  waiting for transfers between devices  18.5 us (31%)
    pallas_call x12, Pallas kernels, call(): pl.pallas_call(functools.partial(loading, kernel, parts, (len(after), len...  18.7 us
    ppermute x9, starting transfers between devices, exchange(): lax.ppermute(pieces[offset], axis, [(n, n ^ offset) for n in range(count)])  10.2 us
    ppermute x8, starting transfers between devices, crossing_exchange(): lax.ppermute(pieces[offset], ('gx', 'gy'), [(n, n ^ count ^ offset) for n...  6.81 us
    ppermute x8, waiting for transfers between devices, crossing_exchange(): lax.ppermute(pieces[offset], ('gx', 'gy'), [(n, n ^ count ^ offset) for n...  6.31 us
    ppermute x9, waiting for transfers between devices, exchange(): lax.ppermute(pieces[offset], axis, [(n, n ^ offset) for n in range(count)])  6.28 us
    ppermute x2, waiting for transfers between devices, per_device(): lax.ppermute(both, 'gy', [(n, n ^ offset) for n in range(count)])  3.4 us
    ppermute x2, starting transfers between devices, per_device(): lax.ppermute(both, 'gy', [(n, n ^ offset) for n in range(count)])  2.84 us
    ppermute x2, waiting for transfers between devices, per_device(): relayed = lax.ppermute(parts[offset + 1], 'gy', pair)  2.54 us
  transfers between devices with their start and end apart: 22, of which 12 were waited for; matrix products, arithmetic and copies ran while one was open for 0% of the time, Pallas kernels for 21%

profile of v5, /device:TPU:0, one launch (start us, length us, event | category | flops | bytes accessed | tf_op | source)
XLA Modules:
  0.0 59.5 jit_solution(16917506238319013225)
XLA Ops:
  0.0 0.0 copy-start.4
  0.0 5.1 %collective-permute-start.1 = (bf16[16,4096]{1,0:T(8,128)(2,1)}, bf16[16,4096]{1,0:T(8,128)(2,1)S(1)}, u32[]{:S(2)}, u32[]{:S(2)}) collective-permute-start(bf16[16,4096]{1,0:T(8,128)(2,1)} %refs_1_.1), channel_id=1, source_target_pairs={{0,3},{1,2},{2,1},{3,0},{4,7},{5,6},{6,5},{7,4},{8,11},{9,10},{10,... | collective-permute-start | bytes 393224 | tf_op jit(solution)/shard_map/gather_hidden/ppermute | solution.py:313
  5.1 0.0 collective-permute-start
  5.1 0.6 %collective-permute-start.2 = (bf16[16,4096]{1,0:T(8,128)(2,1)}, bf16[16,4096]{1,0:T(8,128)(2,1)S(1)}, u32[]{:S(2)}, u32[]{:S(2)}) collective-permute-start(bf16[16,4096]{1,0:T(8,128)(2,1)} %refs_1_.1), channel_id=1, source_target_pairs={{0,1},{1,0},{2,3},{3,2},{4,5},{5,4},{6,7},{7,6},{8,9},{9,8},{10,11... | collective-permute-start | bytes 393224 | tf_op jit(solution)/shard_map/gather_hidden/ppermute | solution.py:313
  5.8 5.8 %fetch_query.1.refs_6_ = bf16[4096,2048]{1,0:T(8,128)(2,1)S(1)} custom-call(bf16[4096,2048]{1,0:T(8,128)(2,1)} %refs_0_.4), custom_call_target="tpu_custom_call" | custom-call | bytes 33554432 | tf_op jit(solution)/shard_map/fetch_query/fetch_query/pallas_call | solution.py:280
  11.6 0.0 copy-start.6
  11.6 0.0 collective-permute-done.1.refs_3_
  11.6 4.8 %collective-permute-done.refs_2_ = bf16[16,4096]{1,0:T(8,128)(2,1)S(1)} collective-permute-done((bf16[16,4096]{1,0:T(8,128)(2,1)}, bf16[16,4096]{1,0:T(8,128)(2,1)S(1)}, u32[]{:S(2)}, u32[]{:S(2)}) %collective-permute-start) | collective-permute-done | bytes 131104 | tf_op jit(solution)/shard_map/gather_hidden/ppermute | solution.py:313
  16.4 0.0 collective-permute-done.2.refs_4_
  16.4 0.0 copy-done.4
  16.4 0.0 copy-done.1
  16.4 0.0 copy-done
  16.4 0.0 copy-done.5
  16.5 3.0 %project.1 = (bf16[16,2432]{1,0:T(8,128)(2,1)S(1)}, bf16[16,2432]{1,0:T(8,128)(2,1)S(1)}, bf16[16,2432]{1,0:T(8,128)(2,1)S(1)}, bf16[16,2432]{1,0:T(8,128)(2,1)S(1)}, bf16[768,4096]{1,0:T(8,128)(2,1)S(1)}) custom-call(bf16[2048,4096]{1,0:T(8,128)(2,1)} %refs_0_.7, bf16[16,4096]{1,0:T(8,128)(2,1)S(1)} %copy-done.4, ...), custom_call_target="tpu_custom_call" | custom-call | flops 1207959552 | bytes 32301056 | tf_op jit(solution)/shard_map/project/project/pallas_call | solution.py:280
  19.5 0.0 copy-start.2
  19.5 0.0 copy-start.3
  19.5 1.6 %collective-permute-start.3 = (bf16[16,2432]{1,0:T(8,128)(2,1)S(1)}, bf16[16,2432]{1,0:T(8,128)(2,1)S(1)}, u32[]{:S(2)}, u32[]{:S(2)}) collective-permute-start(bf16[16,2432]{1,0:T(8,128)(2,1)S(1)} %get-tuple-element.32), channel_id=1, source_target_pairs={{0,8},{4,12},{8,0},{12,4},{1,9},{5,13},{9,1},{13,5},{2,10},{6,14},... | collective-permute-start | bytes 233480 | tf_op jit(solution)/shard_map/sum_gx/ppermute | solution.py:313
  21.0 0.0 collective-permute-start.4
  21.0 0.6 %collective-permute-start.5 = (bf16[16,2432]{1,0:T(8,128)(2,1)S(1)}, bf16[16,2432]{1,0:T(8,128)(2,1)S(1)}, u32[]{:S(2)}, u32[]{:S(2)}) collective-permute-start(bf16[16,2432]{1,0:T(8,128)(2,1)S(1)} %get-tuple-element.34), channel_id=1, source_target_pairs={{0,12},{4,8},{8,4},{12,0},{1,13},{5,9},{9,5},{13,1},{2,14},{6,10},... | collective-permute-start | bytes 233480 | tf_op jit(solution)/shard_map/sum_gx/ppermute | solution.py:313
  21.7 0.0 copy-done.6
  21.7 2.7 %fetch_output.2 = (f32[64,128]{1,0:T(8,128)S(1)}, f32[64,128]{1,0:T(8,128)S(1)}, s32[64,128]{1,0:T(8,128)S(1)}, bf16[512,4096]{1,0:T(8,128)(2,1)S(1)}) custom-call(bf16[2048,4096]{1,0:T(8,128)(2,1)} %refs_0_.7, bf16[16,2432]{1,0:T(8,128)(2,1)S(1)} %get-tuple-element.30.refs_1_, s32[4]{0:T(128)S(1)} %copy-done.6), custom_call_target="tpu_custom_call" | custom-call | bytes 8486928 | tf_op jit(solution)/shard_map/sum_gx/fetch_output/pallas_call | solution.py:280
  24.4 0.0 collective-permute-done.3.refs_2_
  24.4 0.0 collective-permute-done.4.refs_3_
  24.5 0.6 collective-permute-done.5.refs_4_
  25.0 0.1 combine.1
  25.2 0.5 collective-permute-start.6
  25.7 0.0 collective-permute-start.7
  25.7 2.2 %collective-permute-start.8 = (bf16[4,2432]{1,0:T(4,128)(2,1)S(1)}, bf16[4,2432]{1,0:T(4,128)(2,1)S(1)}, u32[]{:S(2)}, u32[]{:S(2)}) collective-permute-start(bf16[4,2432]{1,0:T(4,128)(2,1)S(1)} %get-tuple-element.37), channel_id=1, source_target_pairs={{0,7},{1,6},{2,5},{3,4},{4,3},{5,2},{6,1},{7,0},{8,15},{9,14},{10,... | collective-permute-start | bytes 58376 | tf_op jit(solution)/shard_map/to_owner/ppermute | solution.py:323
  27.9 0.7 %collective-permute-start.9 = (bf16[4,2432]{1,0:T(4,128)(2,1)S(1)}, bf16[4,2432]{1,0:T(4,128)(2,1)S(1)}, u32[]{:S(2)}, u32[]{:S(2)}) collective-permute-start(bf16[4,2432]{1,0:T(4,128)(2,1)S(1)} %get-tuple-element.38), channel_id=1, source_target_pairs={{0,5},{1,4},{2,7},{3,6},{4,1},{5,0},{6,3},{7,2},{8,13},{9,12},{10,... | collective-permute-start | bytes 58376 | tf_op jit(solution)/shard_map/to_owner/ppermute | solution.py:323
  28.6 0.0 collective-permute-done.6.refs_0_
  28.6 1.2 %collective-permute-done.7.refs_1_ = bf16[4,2432]{1,0:T(4,128)(2,1)S(1)} collective-permute-done((bf16[4,2432]{1,0:T(4,128)(2,1)S(1)}, bf16[4,2432]{1,0:T(4,128)(2,1)S(1)}, u32[]{:S(2)}, u32[]{:S(2)}) %collective-permute-start.7) | collective-permute-done | bytes 19488 | tf_op jit(solution)/shard_map/to_owner/ppermute | solution.py:323
  29.8 0.9 %collective-permute-done.8.refs_2_ = bf16[4,2432]{1,0:T(4,128)(2,1)S(1)} collective-permute-done((bf16[4,2432]{1,0:T(4,128)(2,1)S(1)}, bf16[4,2432]{1,0:T(4,128)(2,1)S(1)}, u32[]{:S(2)}, u32[]{:S(2)}) %collective-permute-start.8) | collective-permute-done | bytes 19488 | tf_op jit(solution)/shard_map/to_owner/ppermute | solution.py:323
  30.7 0.5 collective-permute-done.9.refs_3_
  31.2 0.0 copy-done.2
  31.2 0.0 copy-done.3
  31.2 1.0 %attend.1 = (bf16[4,2048]{1,0:T(4,128)(2,1)S(1)}, bf16[4,2048]{1,0:T(4,128)(2,1)S(1)}, bf16[4,2048]{1,0:T(4,128)(2,1)S(1)}, bf16[4,2048]{1,0:T(4,128)(2,1)S(1)}) custom-call(bf16[4,2432]{1,0:T(4,128)(2,1)S(1)} %collective-permute-done.6.refs_0_, bf16[4,2432]{1,0:T(4,128)(2,1)S(1)} %collective-permute-done.7.refs_1_, ...), custom_call_target="tpu_custom_call" | custom-call | bytes 2338816 | tf_op jit(solution)/shard_map/attend/attend/pallas_call | solution.py:280
  32.3 0.3 collective-permute-start.10
  32.6 1.8 %collective-permute-start.11 = (bf16[4,2048]{1,0:T(4,128)(2,1)S(1)}, bf16[4,2048]{1,0:T(4,128)(2,1)S(1)}, u32[]{:S(2)}, u32[]{:S(2)}) collective-permute-start(bf16[4,2048]{1,0:T(4,128)(2,1)S(1)} %get-tuple-element.43), channel_id=1, source_target_pairs={{0,6},{1,7},{2,4},{3,5},{4,2},{5,3},{6,0},{7,1},{8,14},{9,15},{10,... | collective-permute-start | bytes 49160 | tf_op jit(solution)/shard_map/to_head_rows/ppermute | solution.py:323
  34.3 1.1 %collective-permute-start.12 = (bf16[4,2048]{1,0:T(4,128)(2,1)S(1)}, bf16[4,2048]{1,0:T(4,128)(2,1)S(1)}, u32[]{:S(2)}, u32[]{:S(2)}) collective-permute-start(bf16[4,2048]{1,0:T(4,128)(2,1)S(1)} %get-tuple-element.44), channel_id=1, source_target_pairs={{0,7},{1,6},{2,5},{3,4},{4,3},{5,2},{6,1},{7,0},{8,15},{9,14},{10,... | collective-permute-start | bytes 49160 | tf_op jit(solution)/shard_map/to_head_rows/ppermute | solution.py:323
  35.4 0.2 collective-permute-start.13
  35.6 0.0 collective-permute-done.10.refs_0_
  35.6 1.0 %collective-permute-done.11.refs_1_ = bf16[4,2048]{1,0:T(4,128)(2,1)S(1)} collective-permute-done((bf16[4,2048]{1,0:T(4,128)(2,1)S(1)}, bf16[4,2048]{1,0:T(4,128)(2,1)S(1)}, u32[]{:S(2)}, u32[]{:S(2)}) %collective-permute-start.11) | collective-permute-done | bytes 16416 | tf_op jit(solution)/shard_map/to_head_rows/ppermute | solution.py:323
  36.6 2.7 %collective-permute-done.12.refs_2_ = bf16[4,2048]{1,0:T(4,128)(2,1)S(1)} collective-permute-done((bf16[4,2048]{1,0:T(4,128)(2,1)S(1)}, bf16[4,2048]{1,0:T(4,128)(2,1)S(1)}, u32[]{:S(2)}, u32[]{:S(2)}) %collective-permute-start.12) | collective-permute-done | bytes 16416 | tf_op jit(solution)/shard_map/to_head_rows/ppermute | solution.py:323
  39.3 0.0 collective-permute-done.13.refs_3_
  39.3 1.2 %collective-permute-start.16 = (bf16[16,2048]{1,0:T(8,128)(2,1)S(1)}, bf16[16,2048]{1,0:T(8,128)(2,1)S(1)}, u32[]{:S(2)}, u32[]{:S(2)}) collective-permute-start(bf16[16,2048]{1,0:T(8,128)(2,1)S(1)} %assemble.1.refs_1_.refs_0_), channel_id=1, source_target_pairs={{0,12},{4,8},{8,4},{12,0},{1,13},{5,9},{9,5},{13,1},{2,14},{6,10},... | collective-permute-start | bytes 196616 | tf_op jit(solution)/shard_map/gather_gx/ppermute | solution.py:313
  40.5 0.3 collective-permute-start.15
  40.9 0.7 %collective-permute-start.14 = (bf16[16,2048]{1,0:T(8,128)(2,1)S(1)}, bf16[16,2048]{1,0:T(8,128)(2,1)S(1)}, u32[]{:S(2)}, u32[]{:S(2)}) collective-permute-start(bf16[16,2048]{1,0:T(8,128)(2,1)S(1)} %assemble.1.refs_1_.refs_0_), channel_id=1, source_target_pairs={{0,8},{4,12},{8,0},{12,4},{1,9},{5,13},{9,1},{13,5},{2,10},{6,14},... | collective-permute-start | bytes 196616 | tf_op jit(solution)/shard_map/gather_gx/ppermute | solution.py:313
  41.6 2.8 %fetch_output.3.refs_6_ = bf16[768,4096]{1,0:T(8,128)(2,1)S(1)} custom-call(bf16[2048,4096]{1,0:T(8,128)(2,1)} %refs_0_.7, bf16[16,2048]{1,0:T(8,128)(2,1)S(1)} %assemble.1.refs_1_.refs_0_), custom_call_target="tpu_custom_call" | custom-call | bytes 12582912 | tf_op jit(solution)/shard_map/gather_gx/fetch_output/pallas_call | solution.py:280
  44.4 0.0 collective-permute-done.16.refs_3_
  44.4 0.0 collective-permute-done.15.refs_2_
  44.4 0.8 %collective-permute-done.14.refs_1_ = bf16[16,2048]{1,0:T(8,128)(2,1)S(1)} collective-permute-done((bf16[16,2048]{1,0:T(8,128)(2,1)S(1)}, bf16[16,2048]{1,0:T(8,128)(2,1)S(1)}, u32[]{:S(2)}, u32[]{:S(2)}) %collective-permute-start.14) | collective-permute-done | bytes 65568 | tf_op jit(solution)/shard_map/gather_gx/ppermute | solution.py:313
  45.2 1.3 %output.2 = (bf16[16,2048]{1,0:T(8,128)(2,1)S(1)}, bf16[16,2048]{1,0:T(8,128)(2,1)S(1)}, bf16[16,2048]{1,0:T(8,128)(2,1)S(1)}, bf16[16,2048]{1,0:T(8,128)(2,1)S(1)}) custom-call(bf16[16,2048]{1,0:T(8,128)(2,1)S(1)} %assemble.1.refs_1_.refs_0_, bf16[16,2048]{1,0:T(8,128)(2,1)S(1)} %collective-permute-done.14.refs_1_, ...), custom_call_target="tpu_custom_call" | custom-call | flops 536870912 | bytes 17301504 | tf_op jit(solution)/shard_map/output/output/pallas_call | solution.py:280
  46.5 0.1 collective-permute-start.17
  46.6 1.3 %output.3 = (bf16[16,2048]{1,0:T(8,128)(2,1)S(1)}, bf16[16,4096]{1,0:T(8,128)(2,1)S(1)}, bf16[16,2048]{1,0:T(8,128)(2,1)S(1)}, bf16[16,2048]{1,0:T(8,128)(2,1)S(1)}) custom-call(bf16[16,2048]{1,0:T(8,128)(2,1)S(1)} %assemble.1.refs_1_.refs_0_, bf16[16,2048]{1,0:T(8,128)(2,1)S(1)} %collective-permute-done.14.refs_1_, ...), custom_call_target="tpu_custom_call" | custom-call | flops 536870912 | bytes 17432576 | tf_op jit(solution)/shard_map/output/output/pallas_call | solution.py:280
  47.8 2.1 %collective-permute-start.19 = (bf16[16,2048]{1,0:T(8,128)(2,1)S(1)}, bf16[16,2048]{1,0:T(8,128)(2,1)S(1)}, u32[]{:S(2)}, u32[]{:S(2)}) collective-permute-start(bf16[16,2048]{1,0:T(8,128)(2,1)S(1)} %get-tuple-element.53), channel_id=1, source_target_pairs={{0,1},{1,0},{2,3},{3,2},{4,5},{5,4},{6,7},{7,6},{8,9},{9,8},{10,11... | collective-permute-start | bytes 196616 | tf_op jit(solution)/shard_map/sum_gy/ppermute | solution.py:471
  49.9 0.1 collective-permute-start.21
  50.0 1.4 %collective-permute-done.17.refs_1_ = bf16[16,2048]{1,0:T(8,128)(2,1)S(1)} collective-permute-done((bf16[16,2048]{1,0:T(8,128)(2,1)S(1)}, bf16[16,2048]{1,0:T(8,128)(2,1)S(1)}, u32[]{:S(2)}, u32[]{:S(2)}) %collective-permute-start.17) | collective-permute-done | bytes 65568 | tf_op jit(solution)/shard_map/sum_gy/ppermute | solution.py:471
  51.4 1.0 %collective-permute-start.18 = (bf16[16,2048]{1,0:T(8,128)(2,1)S(1)}, bf16[16,2048]{1,0:T(8,128)(2,1)S(1)}, u32[]{:S(2)}, u32[]{:S(2)}) collective-permute-start(bf16[16,2048]{1,0:T(8,128)(2,1)S(1)} %relay.2), channel_id=1, source_target_pairs={{0,2},{1,3},{2,0},{3,1},{4,6},{5,7},{6,4},{7,5},{8,10},{9,11},{10,... | collective-permute-start | bytes 196616 | tf_op jit(solution)/shard_map/sum_gy/ppermute | solution.py:481
  52.4 1.1 %collective-permute-done.19.refs_1_ = bf16[16,2048]{1,0:T(8,128)(2,1)S(1)} collective-permute-done((bf16[16,2048]{1,0:T(8,128)(2,1)S(1)}, bf16[16,2048]{1,0:T(8,128)(2,1)S(1)}, u32[]{:S(2)}, u32[]{:S(2)}) %collective-permute-start.19) | collective-permute-done | bytes 65568 | tf_op jit(solution)/shard_map/sum_gy/ppermute | solution.py:471
  53.6 1.8 %collective-permute-start.20 = (bf16[16,2048]{1,0:T(8,128)(2,1)S(1)}, bf16[16,2048]{1,0:T(8,128)(2,1)S(1)}, u32[]{:S(2)}, u32[]{:S(2)}) collective-permute-start(bf16[16,2048]{1,0:T(8,128)(2,1)S(1)} %relay.3), channel_id=1, source_target_pairs={{0,2},{1,3},{2,0},{3,1},{4,6},{5,7},{6,4},{7,5},{8,10},{9,11},{10,... | collective-permute-start | bytes 196616 | tf_op jit(solution)/shard_map/sum_gy/ppermute | solution.py:481
  55.4 1.8 %collective-permute-done.18.refs_1_ = bf16[16,2048]{1,0:T(8,128)(2,1)S(1)} collective-permute-done((bf16[16,2048]{1,0:T(8,128)(2,1)S(1)}, bf16[16,2048]{1,0:T(8,128)(2,1)S(1)}, u32[]{:S(2)}, u32[]{:S(2)}) %collective-permute-start.18) | collective-permute-done | bytes 65568 | tf_op jit(solution)/shard_map/sum_gy/ppermute | solution.py:481
  57.3 1.5 %collective-permute-done.20.refs_3_ = bf16[16,2048]{1,0:T(8,128)(2,1)S(1)} collective-permute-done((bf16[16,2048]{1,0:T(8,128)(2,1)S(1)}, bf16[16,2048]{1,0:T(8,128)(2,1)S(1)}, u32[]{:S(2)}, u32[]{:S(2)}) %collective-permute-start.20) | collective-permute-done | bytes 65568 | tf_op jit(solution)/shard_map/sum_gy/ppermute | solution.py:481
  58.8 0.0 collective-permute-done.21.refs_4_
  58.8 0.7 %add.1 = bf16[16,4096]{1,0:T(8,128)(2,1)} custom-call(bf16[16,2048]{1,0:T(8,128)(2,1)S(1)} %get-tuple-element.47.refs_0_, bf16[16,2048]{1,0:T(8,128)(2,1)S(1)} %collective-permute-done.18.refs_1_, bf16[16,2048]{1,0:T(8,128)(2,1)S(1)} %get-tuple-element.51.refs_2_, bf16[16,2048]{1,0:T(8,128)(2,1)S(1)} %collective-permute-done.20.refs_3_, ...), custom_call_target="tpu_custom_call" | custom-call | bytes 524288 | tf_op jit(solution)/shard_map/sum_gy/add/pallas_call | solution.py:280
  (6 shorter events, 0.1 us)
Async XLA Ops:
  0.0 16.4 %copy-start.4 = (bf16[16,4096]{1,0:T(8,128)(2,1)S(1)}, bf16[16,4096]{1,0:T(8,128)(2,1)}, u32[]{:S(2)}) copy-start(bf16[16,4096]{1,0:T(8,128)(2,1)} %refs_1_.1) | copy-start | bytes 393220
  0.0 16.4 %copy-start.1 = (bf16[4096,128]{1,0:T(8,128)(2,1)S(1)}, bf16[4096,128]{1,0:T(8,128)(2,1)}, u32[]{:S(2)}) copy-start(bf16[4096,128]{1,0:T(8,128)(2,1)} %refs_8_.1) | copy-start | bytes 3145732
  0.0 16.4 %copy-start = (bf16[4096,128]{1,0:T(8,128)(2,1)S(1)}, bf16[4096,128]{1,0:T(8,128)(2,1)}, u32[]{:S(2)}) copy-start(bf16[4096,128]{1,0:T(8,128)(2,1)} %refs_7_.1) | copy-start | bytes 3145732
  0.0 16.4 %copy-start.5 = (bf16[4096]{0:T(1024)(128)(2,1)S(1)}, bf16[4096]{0:T(1024)(128)(2,1)}, u32[]{:S(2)}) copy-start(bf16[4096]{0:T(1024)(128)(2,1)} %refs_5_.2) | copy-start | bytes 24580
  0.0 11.6 %collective-permute-start.1 = (bf16[16,4096]{1,0:T(8,128)(2,1)}, bf16[16,4096]{1,0:T(8,128)(2,1)S(1)}, u32[]{:S(2)}, u32[]{:S(2)}) collective-permute-start(bf16[16,4096]{1,0:T(8,128)(2,1)} %refs_1_.1), channel_id=1, source_target_pairs={{0,3},{1,2},{2,1},{3,0},{4,7},{5,6},{6,5},{7,4},{8,11},{9,10},{10,... | collective-permute-start | bytes 393224 | tf_op jit(solution)/shard_map/gather_hidden/ppermute | solution.py:313
  5.1 11.3 %collective-permute-start = (bf16[16,4096]{1,0:T(8,128)(2,1)}, bf16[16,4096]{1,0:T(8,128)(2,1)S(1)}, u32[]{:S(2)}, u32[]{:S(2)}) collective-permute-start(bf16[16,4096]{1,0:T(8,128)(2,1)} %refs_1_.1), channel_id=1, source_target_pairs={{0,2},{1,3},{2,0},{3,1},{4,6},{5,7},{6,4},{7,5},{8,10},{9,11},{10,... | collective-permute-start | bytes 393224 | tf_op jit(solution)/shard_map/gather_hidden/ppermute | solution.py:313
  5.1 11.3 %collective-permute-start.2 = (bf16[16,4096]{1,0:T(8,128)(2,1)}, bf16[16,4096]{1,0:T(8,128)(2,1)S(1)}, u32[]{:S(2)}, u32[]{:S(2)}) collective-permute-start(bf16[16,4096]{1,0:T(8,128)(2,1)} %refs_1_.1), channel_id=1, source_target_pairs={{0,1},{1,0},{2,3},{3,2},{4,5},{5,4},{6,7},{7,6},{8,9},{9,8},{10,11... | collective-permute-start | bytes 393224 | tf_op jit(solution)/shard_map/gather_hidden/ppermute | solution.py:313
  11.6 10.1 %copy-start.6 = (s32[4]{0:T(128)S(1)}, s32[4]{0:T(128)}, u32[]{:S(2)}) copy-start(s32[4]{0:T(128)} %refs_2_.1) | copy-start | bytes 52
  19.5 11.8 %copy-start.2 = (bf16[4,256,512]{2,1,0:T(8,128)(2,1)S(1)}, bf16[4,256,512]{2,1,0:T(8,128)(2,1)}, u32[]{:S(2)}) copy-start(bf16[4,256,512]{2,1,0:T(8,128)(2,1)} %refs_4_.1) | copy-start | bytes 3145732
  19.5 11.8 %copy-start.3 = (bf16[4,256,512]{2,1,0:T(8,128)(2,1)S(1)}, bf16[4,256,512]{2,1,0:T(8,128)(2,1)}, u32[]{:S(2)}) copy-start(bf16[4,256,512]{2,1,0:T(8,128)(2,1)} %refs_5_.3) | copy-start | bytes 3145732
  19.5 5.0 %collective-permute-start.3 = (bf16[16,2432]{1,0:T(8,128)(2,1)S(1)}, bf16[16,2432]{1,0:T(8,128)(2,1)S(1)}, u32[]{:S(2)}, u32[]{:S(2)}) collective-permute-start(bf16[16,2432]{1,0:T(8,128)(2,1)S(1)} %get-tuple-element.32), channel_id=1, source_target_pairs={{0,8},{4,12},{8,0},{12,4},{1,9},{5,13},{9,1},{13,5},{2,10},{6,14},... | collective-permute-start | bytes 233480 | tf_op jit(solution)/shard_map/sum_gx/ppermute | solution.py:313
  21.0 3.4 %collective-permute-start.4 = (bf16[16,2432]{1,0:T(8,128)(2,1)S(1)}, bf16[16,2432]{1,0:T(8,128)(2,1)S(1)}, u32[]{:S(2)}, u32[]{:S(2)}) collective-permute-start(bf16[16,2432]{1,0:T(8,128)(2,1)S(1)} %get-tuple-element.33), channel_id=1, source_target_pairs={{0,4},{4,0},{8,12},{12,8},{1,5},{5,1},{9,13},{13,9},{2,6},{6,2},{1... | collective-permute-start | bytes 233480 | tf_op jit(solution)/shard_map/sum_gx/ppermute | solution.py:313
  21.0 4.0 %collective-permute-start.5 = (bf16[16,2432]{1,0:T(8,128)(2,1)S(1)}, bf16[16,2432]{1,0:T(8,128)(2,1)S(1)}, u32[]{:S(2)}, u32[]{:S(2)}) collective-permute-start(bf16[16,2432]{1,0:T(8,128)(2,1)S(1)} %get-tuple-element.34), channel_id=1, source_target_pairs={{0,12},{4,8},{8,4},{12,0},{1,13},{5,9},{9,5},{13,1},{2,14},{6,10},... | collective-permute-start | bytes 233480 | tf_op jit(solution)/shard_map/sum_gx/ppermute | solution.py:313
  25.2 3.4 %collective-permute-start.6 = (bf16[4,2432]{1,0:T(4,128)(2,1)S(1)}, bf16[4,2432]{1,0:T(4,128)(2,1)S(1)}, u32[]{:S(2)}, u32[]{:S(2)}) collective-permute-start(bf16[4,2432]{1,0:T(4,128)(2,1)S(1)} %get-tuple-element.35), channel_id=1, source_target_pairs={{0,4},{1,5},{2,6},{3,7},{4,0},{5,1},{6,2},{7,3},{8,12},{9,13},{10,... | collective-permute-start | bytes 58376 | tf_op jit(solution)/shard_map/to_owner/ppermute | solution.py:323
  25.7 4.1 %collective-permute-start.7 = (bf16[4,2432]{1,0:T(4,128)(2,1)S(1)}, bf16[4,2432]{1,0:T(4,128)(2,1)S(1)}, u32[]{:S(2)}, u32[]{:S(2)}) collective-permute-start(bf16[4,2432]{1,0:T(4,128)(2,1)S(1)} %get-tuple-element.36), channel_id=1, source_target_pairs={{0,6},{1,7},{2,4},{3,5},{4,2},{5,3},{6,0},{7,1},{8,14},{9,15},{10,... | collective-permute-start | bytes 58376 | tf_op jit(solution)/shard_map/to_owner/ppermute | solution.py:323
  25.7 5.0 %collective-permute-start.8 = (bf16[4,2432]{1,0:T(4,128)(2,1)S(1)}, bf16[4,2432]{1,0:T(4,128)(2,1)S(1)}, u32[]{:S(2)}, u32[]{:S(2)}) collective-permute-start(bf16[4,2432]{1,0:T(4,128)(2,1)S(1)} %get-tuple-element.37), channel_id=1, source_target_pairs={{0,7},{1,6},{2,5},{3,4},{4,3},{5,2},{6,1},{7,0},{8,15},{9,14},{10,... | collective-permute-start | bytes 58376 | tf_op jit(solution)/shard_map/to_owner/ppermute | solution.py:323
  27.9 3.3 %collective-permute-start.9 = (bf16[4,2432]{1,0:T(4,128)(2,1)S(1)}, bf16[4,2432]{1,0:T(4,128)(2,1)S(1)}, u32[]{:S(2)}, u32[]{:S(2)}) collective-permute-start(bf16[4,2432]{1,0:T(4,128)(2,1)S(1)} %get-tuple-element.38), channel_id=1, source_target_pairs={{0,5},{1,4},{2,7},{3,6},{4,1},{5,0},{6,3},{7,2},{8,13},{9,12},{10,... | collective-permute-start | bytes 58376 | tf_op jit(solution)/shard_map/to_owner/ppermute | solution.py:323
  32.3 3.4 %collective-permute-start.10 = (bf16[4,2048]{1,0:T(4,128)(2,1)S(1)}, bf16[4,2048]{1,0:T(4,128)(2,1)S(1)}, u32[]{:S(2)}, u32[]{:S(2)}) collective-permute-start(bf16[4,2048]{1,0:T(4,128)(2,1)S(1)} %get-tuple-element.42), channel_id=1, source_target_pairs={{0,4},{1,5},{2,6},{3,7},{4,0},{5,1},{6,2},{7,3},{8,12},{9,13},{10,... | collective-permute-start | bytes 49160 | tf_op jit(solution)/shard_map/to_head_rows/ppermute | solution.py:323
  32.6 4.1 %collective-permute-start.11 = (bf16[4,2048]{1,0:T(4,128)(2,1)S(1)}, bf16[4,2048]{1,0:T(4,128)(2,1)S(1)}, u32[]{:S(2)}, u32[]{:S(2)}) collective-permute-start(bf16[4,2048]{1,0:T(4,128)(2,1)S(1)} %get-tuple-element.43), channel_id=1, source_target_pairs={{0,6},{1,7},{2,4},{3,5},{4,2},{5,3},{6,0},{7,1},{8,14},{9,15},{10,... | collective-permute-start | bytes 49160 | tf_op jit(solution)/shard_map/to_head_rows/ppermute | solution.py:323
  34.3 5.0 %collective-permute-start.12 = (bf16[4,2048]{1,0:T(4,128)(2,1)S(1)}, bf16[4,2048]{1,0:T(4,128)(2,1)S(1)}, u32[]{:S(2)}, u32[]{:S(2)}) collective-permute-start(bf16[4,2048]{1,0:T(4,128)(2,1)S(1)} %get-tuple-element.44), channel_id=1, source_target_pairs={{0,7},{1,6},{2,5},{3,4},{4,3},{5,2},{6,1},{7,0},{8,15},{9,14},{10,... | collective-permute-start | bytes 49160 | tf_op jit(solution)/shard_map/to_head_rows/ppermute | solution.py:323
  35.4 3.9 %collective-permute-start.13 = (bf16[4,2048]{1,0:T(4,128)(2,1)S(1)}, bf16[4,2048]{1,0:T(4,128)(2,1)S(1)}, u32[]{:S(2)}, u32[]{:S(2)}) collective-permute-start(bf16[4,2048]{1,0:T(4,128)(2,1)S(1)} %get-tuple-element.45), channel_id=1, source_target_pairs={{0,5},{1,4},{2,7},{3,6},{4,1},{5,0},{6,3},{7,2},{8,13},{9,12},{10,... | collective-permute-start | bytes 49160 | tf_op jit(solution)/shard_map/to_head_rows/ppermute | solution.py:323
  39.3 5.0 %collective-permute-start.16 = (bf16[16,2048]{1,0:T(8,128)(2,1)S(1)}, bf16[16,2048]{1,0:T(8,128)(2,1)S(1)}, u32[]{:S(2)}, u32[]{:S(2)}) collective-permute-start(bf16[16,2048]{1,0:T(8,128)(2,1)S(1)} %assemble.1.refs_1_.refs_0_), channel_id=1, source_target_pairs={{0,12},{4,8},{8,4},{12,0},{1,13},{5,9},{9,5},{13,1},{2,14},{6,10},... | collective-permute-start | bytes 196616 | tf_op jit(solution)/shard_map/gather_gx/ppermute | solution.py:313
  40.5 3.8 %collective-permute-start.15 = (bf16[16,2048]{1,0:T(8,128)(2,1)S(1)}, bf16[16,2048]{1,0:T(8,128)(2,1)S(1)}, u32[]{:S(2)}, u32[]{:S(2)}) collective-permute-start(bf16[16,2048]{1,0:T(8,128)(2,1)S(1)} %assemble.1.refs_1_.refs_0_), channel_id=1, source_target_pairs={{0,4},{4,0},{8,12},{12,8},{1,5},{5,1},{9,13},{13,9},{2,6},{6,2},{1... | collective-permute-start | bytes 196616 | tf_op jit(solution)/shard_map/gather_gx/ppermute | solution.py:313
  40.9 4.3 %collective-permute-start.14 = (bf16[16,2048]{1,0:T(8,128)(2,1)S(1)}, bf16[16,2048]{1,0:T(8,128)(2,1)S(1)}, u32[]{:S(2)}, u32[]{:S(2)}) collective-permute-start(bf16[16,2048]{1,0:T(8,128)(2,1)S(1)} %assemble.1.refs_1_.refs_0_), channel_id=1, source_target_pairs={{0,8},{4,12},{8,0},{12,4},{1,9},{5,13},{9,1},{13,5},{2,10},{6,14},... | collective-permute-start | bytes 196616 | tf_op jit(solution)/shard_map/gather_gx/ppermute | solution.py:313
  46.5 4.9 %collective-permute-start.17 = (bf16[16,2048]{1,0:T(8,128)(2,1)S(1)}, bf16[16,2048]{1,0:T(8,128)(2,1)S(1)}, u32[]{:S(2)}, u32[]{:S(2)}) collective-permute-start(bf16[16,2048]{1,0:T(8,128)(2,1)S(1)} %get-tuple-element.49), channel_id=1, source_target_pairs={{0,1},{1,0},{2,3},{3,2},{4,5},{5,4},{6,7},{7,6},{8,9},{9,8},{10,11... | collective-permute-start | bytes 196616 | tf_op jit(solution)/shard_map/sum_gy/ppermute | solution.py:471
  47.8 5.7 %collective-permute-start.19 = (bf16[16,2048]{1,0:T(8,128)(2,1)S(1)}, bf16[16,2048]{1,0:T(8,128)(2,1)S(1)}, u32[]{:S(2)}, u32[]{:S(2)}) collective-permute-start(bf16[16,2048]{1,0:T(8,128)(2,1)S(1)} %get-tuple-element.53), channel_id=1, source_target_pairs={{0,1},{1,0},{2,3},{3,2},{4,5},{5,4},{6,7},{7,6},{8,9},{9,8},{10,11... | collective-permute-start | bytes 196616 | tf_op jit(solution)/shard_map/sum_gy/ppermute | solution.py:471
  49.9 8.9 %collective-permute-start.21 = (bf16[16,4096]{1,0:T(8,128)(2,1)S(1)}, bf16[16,4096]{1,0:T(8,128)(2,1)S(1)}, u32[]{:S(2)}, u32[]{:S(2)}) collective-permute-start(bf16[16,4096]{1,0:T(8,128)(2,1)S(1)} %get-tuple-element.54), channel_id=1, source_target_pairs={{0,1},{1,0},{2,3},{3,2},{4,5},{5,4},{6,7},{7,6},{8,9},{9,8},{10,11... | collective-permute-start | bytes 393224 | tf_op jit(solution)/shard_map/sum_gy/ppermute | solution.py:488
  51.4 5.9 %collective-permute-start.18 = (bf16[16,2048]{1,0:T(8,128)(2,1)S(1)}, bf16[16,2048]{1,0:T(8,128)(2,1)S(1)}, u32[]{:S(2)}, u32[]{:S(2)}) collective-permute-start(bf16[16,2048]{1,0:T(8,128)(2,1)S(1)} %relay.2), channel_id=1, source_target_pairs={{0,2},{1,3},{2,0},{3,1},{4,6},{5,7},{6,4},{7,5},{8,10},{9,11},{10,... | collective-permute-start | bytes 196616 | tf_op jit(solution)/shard_map/sum_gy/ppermute | solution.py:481
  53.6 5.2 %collective-permute-start.20 = (bf16[16,2048]{1,0:T(8,128)(2,1)S(1)}, bf16[16,2048]{1,0:T(8,128)(2,1)S(1)}, u32[]{:S(2)}, u32[]{:S(2)}) collective-permute-start(bf16[16,2048]{1,0:T(8,128)(2,1)S(1)} %relay.3), channel_id=1, source_target_pairs={{0,2},{1,3},{2,0},{3,1},{4,6},{5,7},{6,4},{7,5},{8,10},{9,11},{10,... | collective-permute-start | bytes 196616 | tf_op jit(solution)/shard_map/sum_gy/ppermute | solution.py:481

commit v6 on v4

--- a/solution.py
+++ b/solution.py
@@ -101,8 +101,9 @@
     return wide.reshape(group * rows.shape[0], rows.shape[1])
 
 
-def attend_kernel(count, group, features, *refs):
-    pieces = [refs[order("to_owner", count).index(offset)] for offset in range(count)]
+def attend_kernel(offsets, group, features, *refs):
+    count = len(offsets)
+    pieces = refs[:count]
     keys, values, cosines, sines, filled = refs[count : count + 5]
     outs = refs[count + 5 :]
     share, slots = keys.shape[0], keys.shape[1]
@@ -119,8 +120,8 @@
     item = lax.broadcasted_iota(jnp.int32, (rows, 1), 0) % share
     valid = lax.broadcasted_iota(jnp.int32, (rows, slots), 1) < filled[:, :1]
     states, scores = [], []
-    for offset in range(count):
-        piece = pieces[offset][...].astype(jnp.float32)
+    for piece, offset in zip(pieces, offsets):
+        piece = piece[...].astype(jnp.float32)
         head = me ^ offset
         lanes = pl.ds(pl.multiple_of(head * HEAD_SIZE, HEAD_SIZE), HEAD_SIZE)
         query = jnp.concatenate(
@@ -387,21 +388,27 @@
 
     with jax.named_scope("attend"):
         if key_columns == HEAD_SIZE:
-            attended, _ = call(
-                functools.partial(attend_kernel, count, group, features),
-                [array((share, query_columns))] * count,
-                [],
-                [
-                    *(owned[k] for k in order("to_owner", count)),
-                    stored_key_cache,
-                    stored_value_cache,
-                    cosine,
-                    sine,
-                    filled,
-                ],
-                "attend",
-                8,
-            )
+            attended = [None] * count
+            taken = order("to_owner", count)
+            early = len(taken) // 2
+            for offsets in (taken[:early], taken[early:]):
+                results, _ = call(
+                    functools.partial(attend_kernel, offsets, group, features),
+                    [array((share, query_columns))] * len(offsets),
+                    [],
+                    [
+                        *(owned[k] for k in offsets),
+                        stored_key_cache,
+                        stored_value_cache,
+                        cosine,
+                        sine,
+                        filled,
+                    ],
+                    "attend",
+                    8,
+                )
+                for offset, result in zip(offsets, results):
+                    attended[offset] = result
         else:
             attended = attend_narrow(
                 owned, used, features, stored_key_cache, stored_value_cache, cosine[:share],

time: 60 us -> 58.8 us (0.980)
  waiting for transfers between devices: 19.4 us -> 17.7 us
    ppermute x8, waiting for transfers between devices: 6.32 us -> 4.07 us  [crossing_exchange(): lax.ppermute(pieces[offset], ('gx', 'gy'), [(n, n ^ count ^ offset) for n...]
    pallas_call x9 -> x10, Pallas kernels: 18.5 us -> 19 us  [call(): pl.pallas_call(functools.partial(loading, kernel, parts, (len(after), len...]
  transfers between devices with their start and end apart: 20 -> 20, of which waited for: 10 -> 9; matrix products, arithmetic and copies ran while one was open for 0% -> 0% of each run, Pallas kernels for 19% -> 22%
where the time goes in v6:
time: 58.8 us; the launch traced here: 58.1 us
  starting transfers between devices  21.2 us (36%)
  Pallas kernels  19 us (32%)
  waiting for transfers between devices  17.7 us (30%)
    pallas_call x10, Pallas kernels, call(): pl.pallas_call(functools.partial(loading, kernel, parts, (len(after), len...  19 us
    ppermute x12, starting transfers between devices, exchange(): lax.ppermute(pieces[offset], axis, [(n, n ^ offset) for n in range(count)])  14.6 us
    ppermute x12, waiting for transfers between devices, exchange(): lax.ppermute(pieces[offset], axis, [(n, n ^ offset) for n in range(count)])  13.6 us
    ppermute x8, starting transfers between devices, crossing_exchange(): lax.ppermute(pieces[offset], ('gx', 'gy'), [(n, n ^ count ^ offset) for n...  6.56 us
    ppermute x8, waiting for transfers between devices, crossing_exchange(): lax.ppermute(pieces[offset], ('gx', 'gy'), [(n, n ^ count ^ offset) for n...  4.07 us
  transfers between devices with their start and end apart: 20, of which 9 were waited for; matrix products, arithmetic and copies ran while one was open for 0% of the time, Pallas kernels for 22%

profile of v6, /device:TPU:0, one launch (start us, length us, event | category | flops | bytes accessed | tf_op | source)
XLA Modules:
  0.0 58.1 jit_solution(10684379304375159051)
XLA Ops:
  0.0 0.0 copy-start.4
  0.0 0.0 copy-start.3
  0.0 0.0 copy-start.2
  0.0 0.0 copy-start.5
  0.0 5.1 %collective-permute-start.1 = (bf16[16,4096]{1,0:T(8,128)(2,1)}, bf16[16,4096]{1,0:T(8,128)(2,1)S(1)}, u32[]{:S(2)}, u32[]{:S(2)}) collective-permute-start(bf16[16,4096]{1,0:T(8,128)(2,1)} %refs_1_.1), channel_id=1, source_target_pairs={{0,3},{1,2},{2,1},{3,0},{4,7},{5,6},{6,5},{7,4},{8,11},{9,10},{10,... | collective-permute-start | bytes 393224 | tf_op jit(solution)/shard_map/gather_hidden/ppermute | solution.py:294
  5.1 0.0 collective-permute-start
  5.1 0.6 %collective-permute-start.2 = (bf16[16,4096]{1,0:T(8,128)(2,1)}, bf16[16,4096]{1,0:T(8,128)(2,1)S(1)}, u32[]{:S(2)}, u32[]{:S(2)}) collective-permute-start(bf16[16,4096]{1,0:T(8,128)(2,1)} %refs_1_.1), channel_id=1, source_target_pairs={{0,1},{1,0},{2,3},{3,2},{4,5},{5,4},{6,7},{7,6},{8,9},{9,8},{10,11... | collective-permute-start | bytes 393224 | tf_op jit(solution)/shard_map/gather_hidden/ppermute | solution.py:294
  5.8 5.8 %fetch_query.1.refs_6_ = bf16[4096,2048]{1,0:T(8,128)(2,1)S(1)} custom-call(bf16[4096,2048]{1,0:T(8,128)(2,1)} %refs_0_.4), custom_call_target="tpu_custom_call" | custom-call | bytes 33619968 | tf_op jit(solution)/shard_map/fetch_query/fetch_query/pallas_call | solution.py:261
  11.6 0.0 copy-start.6
  11.6 0.0 collective-permute-done.1.refs_3_
  11.6 4.8 %collective-permute-done.refs_2_ = bf16[16,4096]{1,0:T(8,128)(2,1)S(1)} collective-permute-done((bf16[16,4096]{1,0:T(8,128)(2,1)}, bf16[16,4096]{1,0:T(8,128)(2,1)S(1)}, u32[]{:S(2)}, u32[]{:S(2)}) %collective-permute-start) | collective-permute-done | bytes 131104 | tf_op jit(solution)/shard_map/gather_hidden/ppermute | solution.py:294
  16.4 0.0 collective-permute-done.2.refs_4_
  16.4 0.0 copy-done.4
  16.4 0.0 copy-done.3
  16.4 0.0 copy-done.2
  16.4 0.0 copy-done.5
  16.5 3.0 %project.1 = (bf16[16,2432]{1,0:T(8,128)(2,1)S(1)}, bf16[16,2432]{1,0:T(8,128)(2,1)S(1)}, bf16[16,2432]{1,0:T(8,128)(2,1)S(1)}, bf16[16,2432]{1,0:T(8,128)(2,1)S(1)}, bf16[768,4096]{1,0:T(8,128)(2,1)S(1)}) custom-call(bf16[2048,4096]{1,0:T(8,128)(2,1)} %refs_0_.7, bf16[16,4096]{1,0:T(8,128)(2,1)S(1)} %copy-done.4, ...), custom_call_target="tpu_custom_call" | custom-call | flops 1207959552 | bytes 12648448 | tf_op jit(solution)/shard_map/project/project/pallas_call | solution.py:261
  19.5 0.0 copy-start
  19.5 0.0 copy-start.1
  19.5 1.6 %collective-permute-start.3 = (bf16[16,2432]{1,0:T(8,128)(2,1)S(1)}, bf16[16,2432]{1,0:T(8,128)(2,1)S(1)}, u32[]{:S(2)}, u32[]{:S(2)}) collective-permute-start(bf16[16,2432]{1,0:T(8,128)(2,1)S(1)} %get-tuple-element.28), channel_id=1, source_target_pairs={{0,8},{4,12},{8,0},{12,4},{1,9},{5,13},{9,1},{13,5},{2,10},{6,14},... | collective-permute-start | bytes 233480 | tf_op jit(solution)/shard_map/sum_gx/ppermute | solution.py:294
  21.0 0.0 collective-permute-start.4
  21.0 0.6 %collective-permute-start.5 = (bf16[16,2432]{1,0:T(8,128)(2,1)S(1)}, bf16[16,2432]{1,0:T(8,128)(2,1)S(1)}, u32[]{:S(2)}, u32[]{:S(2)}) collective-permute-start(bf16[16,2432]{1,0:T(8,128)(2,1)S(1)} %get-tuple-element.30), channel_id=1, source_target_pairs={{0,12},{4,8},{8,4},{12,0},{1,13},{5,9},{9,5},{13,1},{2,14},{6,10},... | collective-permute-start | bytes 233480 | tf_op jit(solution)/shard_map/sum_gx/ppermute | solution.py:294
  21.7 0.0 copy-done.6
  21.7 2.7 %fetch_output.2 = (f32[64,128]{1,0:T(8,128)S(1)}, f32[64,128]{1,0:T(8,128)S(1)}, s32[64,128]{1,0:T(8,128)S(1)}, bf16[512,4096]{1,0:T(8,128)(2,1)S(1)}) custom-call(bf16[2048,4096]{1,0:T(8,128)(2,1)} %refs_0_.7, bf16[16,2432]{1,0:T(8,128)(2,1)S(1)} %get-tuple-element.26.refs_1_, s32[4]{0:T(128)S(1)} %copy-done.6), custom_call_target="tpu_custom_call" | custom-call | bytes 8454144 | tf_op jit(solution)/shard_map/sum_gx/fetch_output/pallas_call | solution.py:261
  24.4 0.0 collective-permute-done.3.refs_2_
  24.4 0.0 collective-permute-done.4.refs_3_
  24.5 0.6 %collective-permute-done.5.refs_4_ = bf16[16,2432]{1,0:T(8,128)(2,1)S(1)} collective-permute-done((bf16[16,2432]{1,0:T(8,128)(2,1)S(1)}, bf16[16,2432]{1,0:T(8,128)(2,1)S(1)}, u32[]{:S(2)}, u32[]{:S(2)}) %collective-permute-start.5) | collective-permute-done | bytes 77856 | tf_op jit(solution)/shard_map/sum_gx/ppermute | solution.py:294
  25.0 0.1 combine.1
  25.2 0.5 collective-permute-start.6
  25.7 0.0 collective-permute-start.7
  25.7 2.2 %collective-permute-start.10 = (bf16[4,2432]{1,0:T(4,128)(2,1)S(1)}, bf16[4,2432]{1,0:T(4,128)(2,1)S(1)}, u32[]{:S(2)}, u32[]{:S(2)}) collective-permute-start(bf16[4,2432]{1,0:T(4,128)(2,1)S(1)} %get-tuple-element.38), channel_id=1, source_target_pairs={{0,7},{1,6},{2,5},{3,4},{4,3},{5,2},{6,1},{7,0},{8,15},{9,14},{10,... | collective-permute-start | bytes 58376 | tf_op jit(solution)/shard_map/to_owner/ppermute | solution.py:304
  27.9 0.7 %collective-permute-start.11 = (bf16[4,2432]{1,0:T(4,128)(2,1)S(1)}, bf16[4,2432]{1,0:T(4,128)(2,1)S(1)}, u32[]{:S(2)}, u32[]{:S(2)}) collective-permute-start(bf16[4,2432]{1,0:T(4,128)(2,1)S(1)} %get-tuple-element.39), channel_id=1, source_target_pairs={{0,5},{1,4},{2,7},{3,6},{4,1},{5,0},{6,3},{7,2},{8,13},{9,12},{10,... | collective-permute-start | bytes 58376 | tf_op jit(solution)/shard_map/to_owner/ppermute | solution.py:304
  28.6 0.0 collective-permute-done.6.refs_0_
  28.6 1.2 %collective-permute-done.7.refs_1_ = bf16[4,2432]{1,0:T(4,128)(2,1)S(1)} collective-permute-done((bf16[4,2432]{1,0:T(4,128)(2,1)S(1)}, bf16[4,2432]{1,0:T(4,128)(2,1)S(1)}, u32[]{:S(2)}, u32[]{:S(2)}) %collective-permute-start.7) | collective-permute-done | bytes 19488 | tf_op jit(solution)/shard_map/to_owner/ppermute | solution.py:304
  29.8 0.0 copy-done
  29.8 0.0 copy-done.1
  29.8 0.8 %attend.2 = (bf16[4,2048]{1,0:T(4,128)(2,1)S(1)}, bf16[4,2048]{1,0:T(4,128)(2,1)S(1)}) custom-call(bf16[4,2432]{1,0:T(4,128)(2,1)S(1)} %collective-permute-done.6.refs_0_, bf16[4,2432]{1,0:T(4,128)(2,1)S(1)} %collective-permute-done.7.refs_1_, bf16[4,256,512]{2,1,0:T(8,128)(2,1)S(1)} %copy-done, bf16[4,256,512]{2,1,0:T(8,128)(2,1)S(1)} %copy-done.1, ...), custom_call_target="tpu_custom_call" | custom-call | bytes 65536 | tf_op jit(solution)/shard_map/attend/attend/pallas_call | solution.py:261
  30.6 0.3 collective-permute-start.8
  30.9 0.0 collective-permute-start.9
  30.9 0.0 collective-permute-done.10.refs_0_
  30.9 0.3 collective-permute-done.11.refs_1_
  31.2 0.8 %attend.3 = (bf16[4,2048]{1,0:T(4,128)(2,1)S(1)}, bf16[4,2048]{1,0:T(4,128)(2,1)S(1)}) custom-call(bf16[4,2432]{1,0:T(4,128)(2,1)S(1)} %collective-permute-done.10.refs_0_, bf16[4,2432]{1,0:T(4,128)(2,1)S(1)} %collective-permute-done.11.refs_1_, bf16[4,256,512]{2,1,0:T(8,128)(2,1)S(1)} %copy-done, bf16[4,256,512]{2,1,0:T(8,128)(2,1)S(1)} %copy-done.1, ...), custom_call_target="tpu_custom_call" | custom-call | bytes 65536 | tf_op jit(solution)/shard_map/attend/attend/pallas_call | solution.py:261
  32.0 2.1 %collective-permute-start.12 = (bf16[4,2048]{1,0:T(4,128)(2,1)S(1)}, bf16[4,2048]{1,0:T(4,128)(2,1)S(1)}, u32[]{:S(2)}, u32[]{:S(2)}) collective-permute-start(bf16[4,2048]{1,0:T(4,128)(2,1)S(1)} %get-tuple-element.40), channel_id=1, source_target_pairs={{0,7},{1,6},{2,5},{3,4},{4,3},{5,2},{6,1},{7,0},{8,15},{9,14},{10,... | collective-permute-start | bytes 49160 | tf_op jit(solution)/shard_map/to_head_rows/ppermute | solution.py:304
  34.1 0.6 %collective-permute-start.13 = (bf16[4,2048]{1,0:T(4,128)(2,1)S(1)}, bf16[4,2048]{1,0:T(4,128)(2,1)S(1)}, u32[]{:S(2)}, u32[]{:S(2)}) collective-permute-start(bf16[4,2048]{1,0:T(4,128)(2,1)S(1)} %get-tuple-element.41), channel_id=1, source_target_pairs={{0,5},{1,4},{2,7},{3,6},{4,1},{5,0},{6,3},{7,2},{8,13},{9,12},{10,... | collective-permute-start | bytes 49160 | tf_op jit(solution)/shard_map/to_head_rows/ppermute | solution.py:304
  34.8 0.0 collective-permute-done.8.refs_0_
  34.8 0.1 collective-permute-done.9.refs_1_
  34.9 2.1 %collective-permute-done.12.refs_2_ = bf16[4,2048]{1,0:T(4,128)(2,1)S(1)} collective-permute-done((bf16[4,2048]{1,0:T(4,128)(2,1)S(1)}, bf16[4,2048]{1,0:T(4,128)(2,1)S(1)}, u32[]{:S(2)}, u32[]{:S(2)}) %collective-permute-start.12) | collective-permute-done | bytes 16416 | tf_op jit(solution)/shard_map/to_head_rows/ppermute | solution.py:304
  37.0 0.3 collective-permute-done.13.refs_3_
  37.4 1.2 %collective-permute-start.16 = (bf16[16,2048]{1,0:T(8,128)(2,1)S(1)}, bf16[16,2048]{1,0:T(8,128)(2,1)S(1)}, u32[]{:S(2)}, u32[]{:S(2)}) collective-permute-start(bf16[16,2048]{1,0:T(8,128)(2,1)S(1)} %assemble.1.refs_1_.refs_0_), channel_id=1, source_target_pairs={{0,12},{4,8},{8,4},{12,0},{1,13},{5,9},{9,5},{13,1},{2,14},{6,10},... | collective-permute-start | bytes 196616 | tf_op jit(solution)/shard_map/gather_gx/ppermute | solution.py:294
  38.6 0.3 collective-permute-start.15
  38.9 0.7 %collective-permute-start.14 = (bf16[16,2048]{1,0:T(8,128)(2,1)S(1)}, bf16[16,2048]{1,0:T(8,128)(2,1)S(1)}, u32[]{:S(2)}, u32[]{:S(2)}) collective-permute-start(bf16[16,2048]{1,0:T(8,128)(2,1)S(1)} %assemble.1.refs_1_.refs_0_), channel_id=1, source_target_pairs={{0,8},{4,12},{8,0},{12,4},{1,9},{5,13},{9,1},{13,5},{2,10},{6,14},... | collective-permute-start | bytes 196616 | tf_op jit(solution)/shard_map/gather_gx/ppermute | solution.py:294
  39.6 2.8 %fetch_output.3.refs_6_ = bf16[768,4096]{1,0:T(8,128)(2,1)S(1)} custom-call(bf16[2048,4096]{1,0:T(8,128)(2,1)} %refs_0_.7, bf16[16,2048]{1,0:T(8,128)(2,1)S(1)} %assemble.1.refs_1_.refs_0_), custom_call_target="tpu_custom_call" | custom-call | bytes 12648448 | tf_op jit(solution)/shard_map/gather_gx/fetch_output/pallas_call | solution.py:261
  42.4 0.0 collective-permute-done.16.refs_3_
  42.4 0.0 collective-permute-done.15.refs_2_
  42.4 0.8 %collective-permute-done.14.refs_1_ = bf16[16,2048]{1,0:T(8,128)(2,1)S(1)} collective-permute-done((bf16[16,2048]{1,0:T(8,128)(2,1)S(1)}, bf16[16,2048]{1,0:T(8,128)(2,1)S(1)}, u32[]{:S(2)}, u32[]{:S(2)}) %collective-permute-start.14) | collective-permute-done | bytes 65568 | tf_op jit(solution)/shard_map/gather_gx/ppermute | solution.py:294
  43.2 2.4 %output.1 = (bf16[16,4096]{1,0:T(8,128)(2,1)S(1)}, bf16[16,4096]{1,0:T(8,128)(2,1)S(1)}, bf16[16,4096]{1,0:T(8,128)(2,1)S(1)}, bf16[16,4096]{1,0:T(8,128)(2,1)S(1)}) custom-call(bf16[16,2048]{1,0:T(8,128)(2,1)S(1)} %assemble.1.refs_1_.refs_0_, bf16[16,2048]{1,0:T(8,128)(2,1)S(1)} %collective-permute-done.14.refs_1_, ...), custom_call_target="tpu_custom_call" | custom-call | flops 1073741824 | bytes 65536 | tf_op jit(solution)/shard_map/output/output/pallas_call | solution.py:261
  45.6 1.9 %collective-permute-start.17 = (bf16[16,4096]{1,0:T(8,128)(2,1)S(1)}, bf16[16,4096]{1,0:T(8,128)(2,1)S(1)}, u32[]{:S(2)}, u32[]{:S(2)}) collective-permute-start(bf16[16,4096]{1,0:T(8,128)(2,1)S(1)} %get-tuple-element.44), channel_id=1, source_target_pairs={{0,2},{1,3},{2,0},{3,1},{4,6},{5,7},{6,4},{7,5},{8,10},{9,11},{10,... | collective-permute-start | bytes 393224 | tf_op jit(solution)/shard_map/sum_gy/ppermute | solution.py:294
  47.5 0.6 %collective-permute-start.18 = (bf16[16,4096]{1,0:T(8,128)(2,1)S(1)}, bf16[16,4096]{1,0:T(8,128)(2,1)S(1)}, u32[]{:S(2)}, u32[]{:S(2)}) collective-permute-start(bf16[16,4096]{1,0:T(8,128)(2,1)S(1)} %get-tuple-element.45), channel_id=1, source_target_pairs={{0,1},{1,0},{2,3},{3,2},{4,5},{5,4},{6,7},{7,6},{8,9},{9,8},{10,11... | collective-permute-start | bytes 393224 | tf_op jit(solution)/shard_map/sum_gy/ppermute | solution.py:294
  48.1 1.9 %collective-permute-start.19 = (bf16[16,4096]{1,0:T(8,128)(2,1)S(1)}, bf16[16,4096]{1,0:T(8,128)(2,1)S(1)}, u32[]{:S(2)}, u32[]{:S(2)}) collective-permute-start(bf16[16,4096]{1,0:T(8,128)(2,1)S(1)} %get-tuple-element.46), channel_id=1, source_target_pairs={{0,3},{1,2},{2,1},{3,0},{4,7},{5,6},{6,5},{7,4},{8,11},{9,10},{10,... | collective-permute-start | bytes 393224 | tf_op jit(solution)/shard_map/sum_gy/ppermute | solution.py:294
  50.0 7.4 %collective-permute-done.17.refs_1_ = bf16[16,4096]{1,0:T(8,128)(2,1)S(1)} collective-permute-done((bf16[16,4096]{1,0:T(8,128)(2,1)S(1)}, bf16[16,4096]{1,0:T(8,128)(2,1)S(1)}, u32[]{:S(2)}, u32[]{:S(2)}) %collective-permute-start.17) | collective-permute-done | bytes 131104 | tf_op jit(solution)/shard_map/sum_gy/ppermute | solution.py:294
  57.4 0.0 collective-permute-done.18.refs_2_
  57.4 0.0 collective-permute-done.19.refs_3_
  57.4 0.7 %add.1 = bf16[16,4096]{1,0:T(8,128)(2,1)} custom-call(bf16[16,4096]{1,0:T(8,128)(2,1)S(1)} %get-tuple-element.43.refs_0_, bf16[16,4096]{1,0:T(8,128)(2,1)S(1)} %collective-permute-done.17.refs_1_, bf16[16,4096]{1,0:T(8,128)(2,1)S(1)} %collective-permute-done.18.refs_2_, bf16[16,4096]{1,0:T(8,128)(2,1)S(1)} %collective-permute-done.19.refs_3_), custom_call_target="tpu_custom_call" | custom-call | bytes 65536 | tf_op jit(solution)/shard_map/sum_gy/add/pallas_call | solution.py:261
  (1 shorter events, 0.0 us)
Async XLA Ops:
  0.0 16.4 %copy-start.4 = (bf16[16,4096]{1,0:T(8,128)(2,1)S(1)}, bf16[16,4096]{1,0:T(8,128)(2,1)}, u32[]{:S(2)}) copy-start(bf16[16,4096]{1,0:T(8,128)(2,1)} %refs_1_.1) | copy-start | bytes 393220
  0.0 16.4 %copy-start.3 = (bf16[4096,128]{1,0:T(8,128)(2,1)S(1)}, bf16[4096,128]{1,0:T(8,128)(2,1)}, u32[]{:S(2)}) copy-start(bf16[4096,128]{1,0:T(8,128)(2,1)} %refs_8_.1) | copy-start | bytes 3145732
  0.0 16.4 %copy-start.2 = (bf16[4096,128]{1,0:T(8,128)(2,1)S(1)}, bf16[4096,128]{1,0:T(8,128)(2,1)}, u32[]{:S(2)}) copy-start(bf16[4096,128]{1,0:T(8,128)(2,1)} %refs_7_.1) | copy-start | bytes 3145732
  0.0 16.4 %copy-start.5 = (bf16[4096]{0:T(1024)(128)(2,1)S(1)}, bf16[4096]{0:T(1024)(128)(2,1)}, u32[]{:S(2)}) copy-start(bf16[4096]{0:T(1024)(128)(2,1)} %refs_5_.1) | copy-start | bytes 24580
  0.0 11.6 %collective-permute-start.1 = (bf16[16,4096]{1,0:T(8,128)(2,1)}, bf16[16,4096]{1,0:T(8,128)(2,1)S(1)}, u32[]{:S(2)}, u32[]{:S(2)}) collective-permute-start(bf16[16,4096]{1,0:T(8,128)(2,1)} %refs_1_.1), channel_id=1, source_target_pairs={{0,3},{1,2},{2,1},{3,0},{4,7},{5,6},{6,5},{7,4},{8,11},{9,10},{10,... | collective-permute-start | bytes 393224 | tf_op jit(solution)/shard_map/gather_hidden/ppermute | solution.py:294
  5.1 11.3 %collective-permute-start = (bf16[16,4096]{1,0:T(8,128)(2,1)}, bf16[16,4096]{1,0:T(8,128)(2,1)S(1)}, u32[]{:S(2)}, u32[]{:S(2)}) collective-permute-start(bf16[16,4096]{1,0:T(8,128)(2,1)} %refs_1_.1), channel_id=1, source_target_pairs={{0,2},{1,3},{2,0},{3,1},{4,6},{5,7},{6,4},{7,5},{8,10},{9,11},{10,... | collective-permute-start | bytes 393224 | tf_op jit(solution)/shard_map/gather_hidden/ppermute | solution.py:294
  5.1 11.3 %collective-permute-start.2 = (bf16[16,4096]{1,0:T(8,128)(2,1)}, bf16[16,4096]{1,0:T(8,128)(2,1)S(1)}, u32[]{:S(2)}, u32[]{:S(2)}) collective-permute-start(bf16[16,4096]{1,0:T(8,128)(2,1)} %refs_1_.1), channel_id=1, source_target_pairs={{0,1},{1,0},{2,3},{3,2},{4,5},{5,4},{6,7},{7,6},{8,9},{9,8},{10,11... | collective-permute-start | bytes 393224 | tf_op jit(solution)/shard_map/gather_hidden/ppermute | solution.py:294
  11.6 10.1 %copy-start.6 = (s32[4]{0:T(128)S(1)}, s32[4]{0:T(128)}, u32[]{:S(2)}) copy-start(s32[4]{0:T(128)} %refs_2_.3) | copy-start | bytes 52
  19.5 10.4 %copy-start = (bf16[4,256,512]{2,1,0:T(8,128)(2,1)S(1)}, bf16[4,256,512]{2,1,0:T(8,128)(2,1)}, u32[]{:S(2)}) copy-start(bf16[4,256,512]{2,1,0:T(8,128)(2,1)} %refs_2_.5) | copy-start | bytes 3145732
  19.5 10.3 %copy-start.1 = (bf16[4,256,512]{2,1,0:T(8,128)(2,1)S(1)}, bf16[4,256,512]{2,1,0:T(8,128)(2,1)}, u32[]{:S(2)}) copy-start(bf16[4,256,512]{2,1,0:T(8,128)(2,1)} %refs_3_.3) | copy-start | bytes 3145732
  19.5 5.0 %collective-permute-start.3 = (bf16[16,2432]{1,0:T(8,128)(2,1)S(1)}, bf16[16,2432]{1,0:T(8,128)(2,1)S(1)}, u32[]{:S(2)}, u32[]{:S(2)}) collective-permute-start(bf16[16,2432]{1,0:T(8,128)(2,1)S(1)} %get-tuple-element.28), channel_id=1, source_target_pairs={{0,8},{4,12},{8,0},{12,4},{1,9},{5,13},{9,1},{13,5},{2,10},{6,14},... | collective-permute-start | bytes 233480 | tf_op jit(solution)/shard_map/sum_gx/ppermute | solution.py:294
  21.0 3.4 %collective-permute-start.4 = (bf16[16,2432]{1,0:T(8,128)(2,1)S(1)}, bf16[16,2432]{1,0:T(8,128)(2,1)S(1)}, u32[]{:S(2)}, u32[]{:S(2)}) collective-permute-start(bf16[16,2432]{1,0:T(8,128)(2,1)S(1)} %get-tuple-element.29), channel_id=1, source_target_pairs={{0,4},{4,0},{8,12},{12,8},{1,5},{5,1},{9,13},{13,9},{2,6},{6,2},{1... | collective-permute-start | bytes 233480 | tf_op jit(solution)/shard_map/sum_gx/ppermute | solution.py:294
  21.0 4.0 %collective-permute-start.5 = (bf16[16,2432]{1,0:T(8,128)(2,1)S(1)}, bf16[16,2432]{1,0:T(8,128)(2,1)S(1)}, u32[]{:S(2)}, u32[]{:S(2)}) collective-permute-start(bf16[16,2432]{1,0:T(8,128)(2,1)S(1)} %get-tuple-element.30), channel_id=1, source_target_pairs={{0,12},{4,8},{8,4},{12,0},{1,13},{5,9},{9,5},{13,1},{2,14},{6,10},... | collective-permute-start | bytes 233480 | tf_op jit(solution)/shard_map/sum_gx/ppermute | solution.py:294
  25.2 3.4 %collective-permute-start.6 = (bf16[4,2432]{1,0:T(4,128)(2,1)S(1)}, bf16[4,2432]{1,0:T(4,128)(2,1)S(1)}, u32[]{:S(2)}, u32[]{:S(2)}) collective-permute-start(bf16[4,2432]{1,0:T(4,128)(2,1)S(1)} %get-tuple-element.31), channel_id=1, source_target_pairs={{0,4},{1,5},{2,6},{3,7},{4,0},{5,1},{6,2},{7,3},{8,12},{9,13},{10,... | collective-permute-start | bytes 58376 | tf_op jit(solution)/shard_map/to_owner/ppermute | solution.py:304
  25.7 4.1 %collective-permute-start.7 = (bf16[4,2432]{1,0:T(4,128)(2,1)S(1)}, bf16[4,2432]{1,0:T(4,128)(2,1)S(1)}, u32[]{:S(2)}, u32[]{:S(2)}) collective-permute-start(bf16[4,2432]{1,0:T(4,128)(2,1)S(1)} %get-tuple-element.32), channel_id=1, source_target_pairs={{0,6},{1,7},{2,4},{3,5},{4,2},{5,3},{6,0},{7,1},{8,14},{9,15},{10,... | collective-permute-start | bytes 58376 | tf_op jit(solution)/shard_map/to_owner/ppermute | solution.py:304
  25.7 5.2 %collective-permute-start.10 = (bf16[4,2432]{1,0:T(4,128)(2,1)S(1)}, bf16[4,2432]{1,0:T(4,128)(2,1)S(1)}, u32[]{:S(2)}, u32[]{:S(2)}) collective-permute-start(bf16[4,2432]{1,0:T(4,128)(2,1)S(1)} %get-tuple-element.38), channel_id=1, source_target_pairs={{0,7},{1,6},{2,5},{3,4},{4,3},{5,2},{6,1},{7,0},{8,15},{9,14},{10,... | collective-permute-start | bytes 58376 | tf_op jit(solution)/shard_map/to_owner/ppermute | solution.py:304
  27.9 3.3 %collective-permute-start.11 = (bf16[4,2432]{1,0:T(4,128)(2,1)S(1)}, bf16[4,2432]{1,0:T(4,128)(2,1)S(1)}, u32[]{:S(2)}, u32[]{:S(2)}) collective-permute-start(bf16[4,2432]{1,0:T(4,128)(2,1)S(1)} %get-tuple-element.39), channel_id=1, source_target_pairs={{0,5},{1,4},{2,7},{3,6},{4,1},{5,0},{6,3},{7,2},{8,13},{9,12},{10,... | collective-permute-start | bytes 58376 | tf_op jit(solution)/shard_map/to_owner/ppermute | solution.py:304
  30.6 4.2 %collective-permute-start.8 = (bf16[4,2048]{1,0:T(4,128)(2,1)S(1)}, bf16[4,2048]{1,0:T(4,128)(2,1)S(1)}, u32[]{:S(2)}, u32[]{:S(2)}) collective-permute-start(bf16[4,2048]{1,0:T(4,128)(2,1)S(1)} %get-tuple-element.36), channel_id=1, source_target_pairs={{0,4},{1,5},{2,6},{3,7},{4,0},{5,1},{6,2},{7,3},{8,12},{9,13},{10,... | collective-permute-start | bytes 49160 | tf_op jit(solution)/shard_map/to_head_rows/ppermute | solution.py:304
  30.9 4.1 %collective-permute-start.9 = (bf16[4,2048]{1,0:T(4,128)(2,1)S(1)}, bf16[4,2048]{1,0:T(4,128)(2,1)S(1)}, u32[]{:S(2)}, u32[]{:S(2)}) collective-permute-start(bf16[4,2048]{1,0:T(4,128)(2,1)S(1)} %get-tuple-element.37), channel_id=1, source_target_pairs={{0,6},{1,7},{2,4},{3,5},{4,2},{5,3},{6,0},{7,1},{8,14},{9,15},{10,... | collective-permute-start | bytes 49160 | tf_op jit(solution)/shard_map/to_head_rows/ppermute | solution.py:304
  32.0 5.0 %collective-permute-start.12 = (bf16[4,2048]{1,0:T(4,128)(2,1)S(1)}, bf16[4,2048]{1,0:T(4,128)(2,1)S(1)}, u32[]{:S(2)}, u32[]{:S(2)}) collective-permute-start(bf16[4,2048]{1,0:T(4,128)(2,1)S(1)} %get-tuple-element.40), channel_id=1, source_target_pairs={{0,7},{1,6},{2,5},{3,4},{4,3},{5,2},{6,1},{7,0},{8,15},{9,14},{10,... | collective-permute-start | bytes 49160 | tf_op jit(solution)/shard_map/to_head_rows/ppermute | solution.py:304
  34.1 3.2 %collective-permute-start.13 = (bf16[4,2048]{1,0:T(4,128)(2,1)S(1)}, bf16[4,2048]{1,0:T(4,128)(2,1)S(1)}, u32[]{:S(2)}, u32[]{:S(2)}) collective-permute-start(bf16[4,2048]{1,0:T(4,128)(2,1)S(1)} %get-tuple-element.41), channel_id=1, source_target_pairs={{0,5},{1,4},{2,7},{3,6},{4,1},{5,0},{6,3},{7,2},{8,13},{9,12},{10,... | collective-permute-start | bytes 49160 | tf_op jit(solution)/shard_map/to_head_rows/ppermute | solution.py:304
  37.4 5.0 %collective-permute-start.16 = (bf16[16,2048]{1,0:T(8,128)(2,1)S(1)}, bf16[16,2048]{1,0:T(8,128)(2,1)S(1)}, u32[]{:S(2)}, u32[]{:S(2)}) collective-permute-start(bf16[16,2048]{1,0:T(8,128)(2,1)S(1)} %assemble.1.refs_1_.refs_0_), channel_id=1, source_target_pairs={{0,12},{4,8},{8,4},{12,0},{1,13},{5,9},{9,5},{13,1},{2,14},{6,10},... | collective-permute-start | bytes 196616 | tf_op jit(solution)/shard_map/gather_gx/ppermute | solution.py:294
  38.6 3.8 %collective-permute-start.15 = (bf16[16,2048]{1,0:T(8,128)(2,1)S(1)}, bf16[16,2048]{1,0:T(8,128)(2,1)S(1)}, u32[]{:S(2)}, u32[]{:S(2)}) collective-permute-start(bf16[16,2048]{1,0:T(8,128)(2,1)S(1)} %assemble.1.refs_1_.refs_0_), channel_id=1, source_target_pairs={{0,4},{4,0},{8,12},{12,8},{1,5},{5,1},{9,13},{13,9},{2,6},{6,2},{1... | collective-permute-start | bytes 196616 | tf_op jit(solution)/shard_map/gather_gx/ppermute | solution.py:294
  38.9 4.3 %collective-permute-start.14 = (bf16[16,2048]{1,0:T(8,128)(2,1)S(1)}, bf16[16,2048]{1,0:T(8,128)(2,1)S(1)}, u32[]{:S(2)}, u32[]{:S(2)}) collective-permute-start(bf16[16,2048]{1,0:T(8,128)(2,1)S(1)} %assemble.1.refs_1_.refs_0_), channel_id=1, source_target_pairs={{0,8},{4,12},{8,0},{12,4},{1,9},{5,13},{9,1},{13,5},{2,10},{6,14},... | collective-permute-start | bytes 196616 | tf_op jit(solution)/shard_map/gather_gx/ppermute | solution.py:294
  45.6 11.8 %collective-permute-start.17 = (bf16[16,4096]{1,0:T(8,128)(2,1)S(1)}, bf16[16,4096]{1,0:T(8,128)(2,1)S(1)}, u32[]{:S(2)}, u32[]{:S(2)}) collective-permute-start(bf16[16,4096]{1,0:T(8,128)(2,1)S(1)} %get-tuple-element.44), channel_id=1, source_target_pairs={{0,2},{1,3},{2,0},{3,1},{4,6},{5,7},{6,4},{7,5},{8,10},{9,11},{10,... | collective-permute-start | bytes 393224 | tf_op jit(solution)/shard_map/sum_gy/ppermute | solution.py:294
  47.5 9.9 %collective-permute-start.18 = (bf16[16,4096]{1,0:T(8,128)(2,1)S(1)}, bf16[16,4096]{1,0:T(8,128)(2,1)S(1)}, u32[]{:S(2)}, u32[]{:S(2)}) collective-permute-start(bf16[16,4096]{1,0:T(8,128)(2,1)S(1)} %get-tuple-element.45), channel_id=1, source_target_pairs={{0,1},{1,0},{2,3},{3,2},{4,5},{5,4},{6,7},{7,6},{8,9},{9,8},{10,11... | collective-permute-start | bytes 393224 | tf_op jit(solution)/shard_map/sum_gy/ppermute | solution.py:294
  48.1 9.3 %collective-permute-start.19 = (bf16[16,4096]{1,0:T(8,128)(2,1)S(1)}, bf16[16,4096]{1,0:T(8,128)(2,1)S(1)}, u32[]{:S(2)}, u32[]{:S(2)}) collective-permute-start(bf16[16,4096]{1,0:T(8,128)(2,1)S(1)} %get-tuple-element.46), channel_id=1, source_target_pairs={{0,3},{1,2},{2,1},{3,0},{4,7},{5,6},{6,5},{7,4},{8,11},{9,10},{10,... | collective-permute-start | bytes 393224 | tf_op jit(solution)/shard_map/sum_gy/ppermute | solution.py:294

commit v7 on v6

--- a/solution.py
+++ b/solution.py
@@ -105,7 +105,7 @@
     count = len(offsets)
     pieces = refs[:count]
     keys, values, cosines, sines, filled = refs[count : count + 5]
-    outs = refs[count + 5 :]
+    outs, rows_of = refs[count + 5 : -1], refs[-1]
     share, slots = keys.shape[0], keys.shape[1]
     rows = share * group
     scale = 1.0 / HEAD_SIZE**0.5
@@ -117,11 +117,20 @@
     )
     row_scale = lax.rsqrt(squares / features + EPSILON)
     row_scales = spread(row_scale, group)
-    item = lax.broadcasted_iota(jnp.int32, (rows, 1), 0) % share
     valid = lax.broadcasted_iota(jnp.int32, (rows, slots), 1) < filled[:, :1]
+
+    def per_head(sequences):
+        return jnp.concatenate(
+            [
+                jnp.broadcast_to(sequences[n : n + 1], (group, HEAD_SIZE))
+                for n in range(share)
+            ],
+            axis=0,
+        )
+
     states, scores = [], []
-    for piece, offset in zip(pieces, offsets):
-        piece = piece[...].astype(jnp.float32)
+    for index, offset in enumerate(offsets):
+        piece = pieces[index][...].astype(jnp.float32)
         head = me ^ offset
         lanes = pl.ds(pl.multiple_of(head * HEAD_SIZE, HEAD_SIZE), HEAD_SIZE)
         query = jnp.concatenate(
@@ -129,28 +138,33 @@
         )
         query = query * row_scales
         query = query * cosine + pltpu.roll(query, HEAD_SIZE // 2, 1) * sine
-        query = query.astype(jnp.bfloat16)
+        rows_of[index] = query.astype(jnp.bfloat16).astype(jnp.float32)
         first = group * HEAD_SIZE
-        fresh_key = spread(piece[:, first : first + HEAD_SIZE], group) * row_scales
-        fresh_key = fresh_key * cosine + pltpu.roll(fresh_key, HEAD_SIZE // 2, 1) * sine
-        fresh_key = fresh_key.astype(jnp.bfloat16).astype(jnp.float32)
+        fresh_key = piece[:, first : first + HEAD_SIZE] * row_scale
+        fresh_key = (
+            fresh_key * cosine[:share] + pltpu.roll(fresh_key, HEAD_SIZE // 2, 1) * sine[:share]
+        )
+        fresh_key = per_head(fresh_key.astype(jnp.bfloat16).astype(jnp.float32))
         first = first + HEAD_SIZE
-        fresh_value = spread(piece[:, first : first + HEAD_SIZE], group) * row_scales
-        fresh_value = fresh_value.astype(jnp.bfloat16).astype(jnp.float32)
-        own = jnp.sum(query.astype(jnp.float32) * fresh_key, axis=1, keepdims=True) * scale
+        fresh_value = piece[:, first : first + HEAD_SIZE] * row_scale
+        fresh_value = per_head(fresh_value.astype(jnp.bfloat16).astype(jnp.float32))
+        queries = [rows_of[index, pl.ds(n, group, stride=share), :] for n in range(share)]
+        own = scale * jnp.sum(
+            jnp.concatenate(queries, axis=0) * fresh_key, axis=1, keepdims=True
+        )
         states.append((lanes, own, fresh_value))
-        products = [
-            lax.dot_general(
-                query,
-                keys[n, :, lanes],
-                (((1,), (1,)), ((), ())),
-                preferred_element_type=jnp.float32,
-            )
-            for n in range(share)
-        ]
-        score = products[0]
-        for n in range(1, share):
-            score = jnp.where(item == n, products[n], score)
+        score = jnp.concatenate(
+            [
+                lax.dot_general(
+                    queries[n].astype(jnp.bfloat16),
+                    keys[n, :, lanes],
+                    (((1,), (1,)), ((), ())),
+                    preferred_element_type=jnp.float32,
+                )
+                for n in range(share)
+            ],
+            axis=0,
+        )
         scores.append(jnp.where(valid, score * scale, -1e30))
     tops = [
         jnp.maximum(jnp.max(score, axis=1, keepdims=True), own)
@@ -159,19 +173,27 @@
     weights = [
         jnp.where(valid, jnp.exp(score - top), 0.0) for score, top in zip(scores, tops)
     ]
-    for offset, (lanes, own, fresh_value) in enumerate(states):
-        own_weight = jnp.exp(own - tops[offset])
-        total = jnp.sum(weights[offset], axis=1, keepdims=True) + own_weight
-        mixed = own_weight.astype(jnp.bfloat16).astype(jnp.float32) * fresh_value
+    for index, (lanes, own, fresh_value) in enumerate(states):
+        own_weight = jnp.exp(own - tops[index])
+        total = jnp.sum(weights[index], axis=1, keepdims=True) + own_weight
+        rounded = weights[index].astype(jnp.bfloat16)
+        mixed = jnp.concatenate(
+            [
+                jnp.dot(
+                    rounded[n * group : (n + 1) * group],
+                    values[n, :, lanes],
+                    preferred_element_type=jnp.float32,
+                )
+                for n in range(share)
+            ],
+            axis=0,
+        )
+        mixed = mixed + own_weight.astype(jnp.bfloat16).astype(jnp.float32) * fresh_value
+        mixed = mixed / total
         for n in range(share):
-            mixed = mixed + jnp.dot(
-                jnp.where(item == n, weights[offset], 0.0).astype(jnp.bfloat16),
-                values[n, :, lanes],
-                preferred_element_type=jnp.float32,
-            )
-        mixed = mixed / total
-        outs[offset][...] = jnp.concatenate(
-            [mixed[h * share : (h + 1) * share] for h in range(group)], axis=1
+            rows_of[index, pl.ds(n, group, stride=share), :] = mixed[n * group : (n + 1) * group]
+        outs[index][...] = jnp.concatenate(
+            [rows_of[index, h * share : (h + 1) * share, :] for h in range(group)], axis=1
         ).astype(jnp.bfloat16)
 
 
@@ -222,15 +244,18 @@
     item = lax.broadcasted_iota(jnp.int32, (rows, HEAD_SIZE), 0) % share
     column = lax.broadcasted_iota(jnp.int32, (rows, HEAD_SIZE), 1)
     half = HEAD_SIZE // 2
+    sequence = lax.broadcasted_iota(jnp.int32, (rows, HEAD_SIZE), 0) // (rows // share)
     length = jnp.zeros((rows, HEAD_SIZE), jnp.int32)
+    slots = length
     for n in range(share):
         length = jnp.where(item == n, lengths[n], length)
+        slots = jnp.where(sequence == n, lengths[n], slots)
     power = (column % half).astype(jnp.float32) * (2.0 / HEAD_SIZE)
     angles = length.astype(jnp.float32) * jnp.exp(-math.log(500000.0) * power)
     sine = jnp.sin(angles)
     cosines[...] = jnp.cos(angles)
     sines[...] = jnp.where(column < half, -sine, sine)
-    filled[...] = length
+    filled[...] = slots
 
 
 def loading(kernel, loads, counts, *refs):
@@ -395,7 +420,7 @@
                 results, _ = call(
                     functools.partial(attend_kernel, offsets, group, features),
                     [array((share, query_columns))] * len(offsets),
-                    [],
+                    [pltpu.VMEM((len(offsets), share * group, HEAD_SIZE), jnp.float32)],
                     [
                         *(owned[k] for k in offsets),
                         stored_key_cache,

time: 58.8 us -> 58.6 us (level)
  no operation moved by 1% of the time
where the time goes in v7:
time: 58.6 us; the launch traced here: 58 us
  starting transfers between devices  21.1 us (36%)
  Pallas kernels  18.9 us (32%)
  waiting for transfers between devices  17.8 us (30%)
    pallas_call x10, Pallas kernels, call(): pl.pallas_call(functools.partial(loading, kernel, parts, (len(after), len...  18.9 us
    ppermute x12, starting transfers between devices, exchange(): lax.ppermute(pieces[offset], axis, [(n, n ^ offset) for n in range(count)])  14.6 us
    ppermute x12, waiting for transfers between devices, exchange(): lax.ppermute(pieces[offset], axis, [(n, n ^ offset) for n in range(count)])  13.6 us
    ppermute x8, starting transfers between devices, crossing_exchange(): lax.ppermute(pieces[offset], ('gx', 'gy'), [(n, n ^ count ^ offset) for n...  6.5 us
    ppermute x8, waiting for transfers between devices, crossing_exchange(): lax.ppermute(pieces[offset], ('gx', 'gy'), [(n, n ^ count ^ offset) for n...  4.12 us
  transfers between devices with their start and end apart: 20, of which 9 were waited for; matrix products, arithmetic and copies ran while one was open for 0% of the time, Pallas kernels for 22%

profile of v7, /device:TPU:0, one launch (start us, length us, event | category | flops | bytes accessed | tf_op | source)
XLA Modules:
  0.0 58.0 jit_solution(4611310453674729321)
XLA Ops:
  0.0 0.0 copy-start.4
  0.0 0.0 copy-start.3
  0.0 0.0 copy-start.2
  0.0 0.0 copy-start.5
  0.0 5.1 %collective-permute-start.1 = (bf16[16,4096]{1,0:T(8,128)(2,1)}, bf16[16,4096]{1,0:T(8,128)(2,1)S(1)}, u32[]{:S(2)}, u32[]{:S(2)}) collective-permute-start(bf16[16,4096]{1,0:T(8,128)(2,1)} %refs_1_.1), channel_id=1, source_target_pairs={{0,3},{1,2},{2,1},{3,0},{4,7},{5,6},{6,5},{7,4},{8,11},{9,10},{10,... | collective-permute-start | bytes 393224 | tf_op jit(solution)/shard_map/gather_hidden/ppermute | solution.py:319
  5.1 0.0 collective-permute-start
  5.1 0.6 %collective-permute-start.2 = (bf16[16,4096]{1,0:T(8,128)(2,1)}, bf16[16,4096]{1,0:T(8,128)(2,1)S(1)}, u32[]{:S(2)}, u32[]{:S(2)}) collective-permute-start(bf16[16,4096]{1,0:T(8,128)(2,1)} %refs_1_.1), channel_id=1, source_target_pairs={{0,1},{1,0},{2,3},{3,2},{4,5},{5,4},{6,7},{7,6},{8,9},{9,8},{10,11... | collective-permute-start | bytes 393224 | tf_op jit(solution)/shard_map/gather_hidden/ppermute | solution.py:319
  5.8 5.8 %fetch_query.1.refs_6_ = bf16[4096,2048]{1,0:T(8,128)(2,1)S(1)} custom-call(bf16[4096,2048]{1,0:T(8,128)(2,1)} %refs_0_.4), custom_call_target="tpu_custom_call" | custom-call | bytes 33619968 | tf_op jit(solution)/shard_map/fetch_query/fetch_query/pallas_call | solution.py:286
  11.6 0.0 copy-start.6
  11.6 0.0 collective-permute-done.1.refs_3_
  11.6 4.8 %collective-permute-done.refs_2_ = bf16[16,4096]{1,0:T(8,128)(2,1)S(1)} collective-permute-done((bf16[16,4096]{1,0:T(8,128)(2,1)}, bf16[16,4096]{1,0:T(8,128)(2,1)S(1)}, u32[]{:S(2)}, u32[]{:S(2)}) %collective-permute-start) | collective-permute-done | bytes 131104 | tf_op jit(solution)/shard_map/gather_hidden/ppermute | solution.py:319
  16.4 0.0 collective-permute-done.2.refs_4_
  16.4 0.0 copy-done.4
  16.4 0.0 copy-done.3
  16.4 0.0 copy-done.2
  16.4 0.0 copy-done.5
  16.5 3.0 %project.1 = (bf16[16,2432]{1,0:T(8,128)(2,1)S(1)}, bf16[16,2432]{1,0:T(8,128)(2,1)S(1)}, bf16[16,2432]{1,0:T(8,128)(2,1)S(1)}, bf16[16,2432]{1,0:T(8,128)(2,1)S(1)}, bf16[768,4096]{1,0:T(8,128)(2,1)S(1)}) custom-call(bf16[2048,4096]{1,0:T(8,128)(2,1)} %refs_0_.7, bf16[16,4096]{1,0:T(8,128)(2,1)S(1)} %copy-done.4, ...), custom_call_target="tpu_custom_call" | custom-call | flops 1207959552 | bytes 12648448 | tf_op jit(solution)/shard_map/project/project/pallas_call | solution.py:286
  19.5 0.0 copy-start
  19.5 0.0 copy-start.1
  19.5 1.6 %collective-permute-start.3 = (bf16[16,2432]{1,0:T(8,128)(2,1)S(1)}, bf16[16,2432]{1,0:T(8,128)(2,1)S(1)}, u32[]{:S(2)}, u32[]{:S(2)}) collective-permute-start(bf16[16,2432]{1,0:T(8,128)(2,1)S(1)} %get-tuple-element.28), channel_id=1, source_target_pairs={{0,8},{4,12},{8,0},{12,4},{1,9},{5,13},{9,1},{13,5},{2,10},{6,14},... | collective-permute-start | bytes 233480 | tf_op jit(solution)/shard_map/sum_gx/ppermute | solution.py:319
  21.0 0.0 collective-permute-start.4
  21.0 0.6 %collective-permute-start.5 = (bf16[16,2432]{1,0:T(8,128)(2,1)S(1)}, bf16[16,2432]{1,0:T(8,128)(2,1)S(1)}, u32[]{:S(2)}, u32[]{:S(2)}) collective-permute-start(bf16[16,2432]{1,0:T(8,128)(2,1)S(1)} %get-tuple-element.30), channel_id=1, source_target_pairs={{0,12},{4,8},{8,4},{12,0},{1,13},{5,9},{9,5},{13,1},{2,14},{6,10},... | collective-permute-start | bytes 233480 | tf_op jit(solution)/shard_map/sum_gx/ppermute | solution.py:319
  21.7 0.0 copy-done.6
  21.7 2.7 %fetch_output.2 = (f32[64,128]{1,0:T(8,128)S(1)}, f32[64,128]{1,0:T(8,128)S(1)}, s32[64,128]{1,0:T(8,128)S(1)}, bf16[512,4096]{1,0:T(8,128)(2,1)S(1)}) custom-call(bf16[2048,4096]{1,0:T(8,128)(2,1)} %refs_0_.7, bf16[16,2432]{1,0:T(8,128)(2,1)S(1)} %get-tuple-element.26.refs_1_, s32[4]{0:T(128)S(1)} %copy-done.6), custom_call_target="tpu_custom_call" | custom-call | bytes 8454144 | tf_op jit(solution)/shard_map/sum_gx/fetch_output/pallas_call | solution.py:286
  24.4 0.0 collective-permute-done.3.refs_2_
  24.4 0.0 collective-permute-done.4.refs_3_
  24.5 0.6 %collective-permute-done.5.refs_4_ = bf16[16,2432]{1,0:T(8,128)(2,1)S(1)} collective-permute-done((bf16[16,2432]{1,0:T(8,128)(2,1)S(1)}, bf16[16,2432]{1,0:T(8,128)(2,1)S(1)}, u32[]{:S(2)}, u32[]{:S(2)}) %collective-permute-start.5) | collective-permute-done | bytes 77856 | tf_op jit(solution)/shard_map/sum_gx/ppermute | solution.py:319
  25.0 0.1 combine.1
  25.2 0.5 collective-permute-start.6
  25.7 0.0 collective-permute-start.7
  25.7 2.2 %collective-permute-start.10 = (bf16[4,2432]{1,0:T(4,128)(2,1)S(1)}, bf16[4,2432]{1,0:T(4,128)(2,1)S(1)}, u32[]{:S(2)}, u32[]{:S(2)}) collective-permute-start(bf16[4,2432]{1,0:T(4,128)(2,1)S(1)} %get-tuple-element.38), channel_id=1, source_target_pairs={{0,7},{1,6},{2,5},{3,4},{4,3},{5,2},{6,1},{7,0},{8,15},{9,14},{10,... | collective-permute-start | bytes 58376 | tf_op jit(solution)/shard_map/to_owner/ppermute | solution.py:329
  27.9 0.7 %collective-permute-start.11 = (bf16[4,2432]{1,0:T(4,128)(2,1)S(1)}, bf16[4,2432]{1,0:T(4,128)(2,1)S(1)}, u32[]{:S(2)}, u32[]{:S(2)}) collective-permute-start(bf16[4,2432]{1,0:T(4,128)(2,1)S(1)} %get-tuple-element.39), channel_id=1, source_target_pairs={{0,5},{1,4},{2,7},{3,6},{4,1},{5,0},{6,3},{7,2},{8,13},{9,12},{10,... | collective-permute-start | bytes 58376 | tf_op jit(solution)/shard_map/to_owner/ppermute | solution.py:329
  28.6 0.0 collective-permute-done.6.refs_0_
  28.6 1.2 %collective-permute-done.7.refs_1_ = bf16[4,2432]{1,0:T(4,128)(2,1)S(1)} collective-permute-done((bf16[4,2432]{1,0:T(4,128)(2,1)S(1)}, bf16[4,2432]{1,0:T(4,128)(2,1)S(1)}, u32[]{:S(2)}, u32[]{:S(2)}) %collective-permute-start.7) | collective-permute-done | bytes 19488 | tf_op jit(solution)/shard_map/to_owner/ppermute | solution.py:329
  29.8 0.0 copy-done
  29.8 0.0 copy-done.1
  29.8 0.7 %attend.2 = (bf16[4,2048]{1,0:T(4,128)(2,1)S(1)}, bf16[4,2048]{1,0:T(4,128)(2,1)S(1)}) custom-call(bf16[4,2432]{1,0:T(4,128)(2,1)S(1)} %collective-permute-done.6.refs_0_, bf16[4,2432]{1,0:T(4,128)(2,1)S(1)} %collective-permute-done.7.refs_1_, bf16[4,256,512]{2,1,0:T(8,128)(2,1)S(1)} %copy-done, bf16[4,256,512]{2,1,0:T(8,128)(2,1)S(1)} %copy-done.1, ...), custom_call_target="tpu_custom_call" | custom-call | bytes 65536 | tf_op jit(solution)/shard_map/attend/attend/pallas_call | solution.py:286
  30.5 0.3 collective-permute-start.8
  30.8 0.1 collective-permute-start.9
  30.9 0.0 collective-permute-done.10.refs_0_
  30.9 0.4 collective-permute-done.11.refs_1_
  31.2 0.7 %attend.3 = (bf16[4,2048]{1,0:T(4,128)(2,1)S(1)}, bf16[4,2048]{1,0:T(4,128)(2,1)S(1)}) custom-call(bf16[4,2432]{1,0:T(4,128)(2,1)S(1)} %collective-permute-done.10.refs_0_, bf16[4,2432]{1,0:T(4,128)(2,1)S(1)} %collective-permute-done.11.refs_1_, bf16[4,256,512]{2,1,0:T(8,128)(2,1)S(1)} %copy-done, bf16[4,256,512]{2,1,0:T(8,128)(2,1)S(1)} %copy-done.1, ...), custom_call_target="tpu_custom_call" | custom-call | bytes 65536 | tf_op jit(solution)/shard_map/attend/attend/pallas_call | solution.py:286
  31.9 2.1 %collective-permute-start.12 = (bf16[4,2048]{1,0:T(4,128)(2,1)S(1)}, bf16[4,2048]{1,0:T(4,128)(2,1)S(1)}, u32[]{:S(2)}, u32[]{:S(2)}) collective-permute-start(bf16[4,2048]{1,0:T(4,128)(2,1)S(1)} %get-tuple-element.40), channel_id=1, source_target_pairs={{0,7},{1,6},{2,5},{3,4},{4,3},{5,2},{6,1},{7,0},{8,15},{9,14},{10,... | collective-permute-start | bytes 49160 | tf_op jit(solution)/shard_map/to_head_rows/ppermute | solution.py:329
  34.0 0.6 %collective-permute-start.13 = (bf16[4,2048]{1,0:T(4,128)(2,1)S(1)}, bf16[4,2048]{1,0:T(4,128)(2,1)S(1)}, u32[]{:S(2)}, u32[]{:S(2)}) collective-permute-start(bf16[4,2048]{1,0:T(4,128)(2,1)S(1)} %get-tuple-element.41), channel_id=1, source_target_pairs={{0,5},{1,4},{2,7},{3,6},{4,1},{5,0},{6,3},{7,2},{8,13},{9,12},{10,... | collective-permute-start | bytes 49160 | tf_op jit(solution)/shard_map/to_head_rows/ppermute | solution.py:329
  34.7 0.0 collective-permute-done.8.refs_0_
  34.7 0.2 collective-permute-done.9.refs_1_
  34.9 2.1 %collective-permute-done.12.refs_2_ = bf16[4,2048]{1,0:T(4,128)(2,1)S(1)} collective-permute-done((bf16[4,2048]{1,0:T(4,128)(2,1)S(1)}, bf16[4,2048]{1,0:T(4,128)(2,1)S(1)}, u32[]{:S(2)}, u32[]{:S(2)}) %collective-permute-start.12) | collective-permute-done | bytes 16416 | tf_op jit(solution)/shard_map/to_head_rows/ppermute | solution.py:329
  37.0 0.2 collective-permute-done.13.refs_3_
  37.2 1.2 %collective-permute-start.16 = (bf16[16,2048]{1,0:T(8,128)(2,1)S(1)}, bf16[16,2048]{1,0:T(8,128)(2,1)S(1)}, u32[]{:S(2)}, u32[]{:S(2)}) collective-permute-start(bf16[16,2048]{1,0:T(8,128)(2,1)S(1)} %assemble.1.refs_1_.refs_0_), channel_id=1, source_target_pairs={{0,12},{4,8},{8,4},{12,0},{1,13},{5,9},{9,5},{13,1},{2,14},{6,10},... | collective-permute-start | bytes 196616 | tf_op jit(solution)/shard_map/gather_gx/ppermute | solution.py:319
  38.5 0.3 collective-permute-start.15
  38.8 0.7 %collective-permute-start.14 = (bf16[16,2048]{1,0:T(8,128)(2,1)S(1)}, bf16[16,2048]{1,0:T(8,128)(2,1)S(1)}, u32[]{:S(2)}, u32[]{:S(2)}) collective-permute-start(bf16[16,2048]{1,0:T(8,128)(2,1)S(1)} %assemble.1.refs_1_.refs_0_), channel_id=1, source_target_pairs={{0,8},{4,12},{8,0},{12,4},{1,9},{5,13},{9,1},{13,5},{2,10},{6,14},... | collective-permute-start | bytes 196616 | tf_op jit(solution)/shard_map/gather_gx/ppermute | solution.py:319
  39.4 2.8 %fetch_output.3.refs_6_ = bf16[768,4096]{1,0:T(8,128)(2,1)S(1)} custom-call(bf16[2048,4096]{1,0:T(8,128)(2,1)} %refs_0_.7, bf16[16,2048]{1,0:T(8,128)(2,1)S(1)} %assemble.1.refs_1_.refs_0_), custom_call_target="tpu_custom_call" | custom-call | bytes 12648448 | tf_op jit(solution)/shard_map/gather_gx/fetch_output/pallas_call | solution.py:286
  42.2 0.0 collective-permute-done.16.refs_3_
  42.3 0.0 collective-permute-done.15.refs_2_
  42.3 0.8 %collective-permute-done.14.refs_1_ = bf16[16,2048]{1,0:T(8,128)(2,1)S(1)} collective-permute-done((bf16[16,2048]{1,0:T(8,128)(2,1)S(1)}, bf16[16,2048]{1,0:T(8,128)(2,1)S(1)}, u32[]{:S(2)}, u32[]{:S(2)}) %collective-permute-start.14) | collective-permute-done | bytes 65568 | tf_op jit(solution)/shard_map/gather_gx/ppermute | solution.py:319
  43.1 2.4 %output.1 = (bf16[16,4096]{1,0:T(8,128)(2,1)S(1)}, bf16[16,4096]{1,0:T(8,128)(2,1)S(1)}, bf16[16,4096]{1,0:T(8,128)(2,1)S(1)}, bf16[16,4096]{1,0:T(8,128)(2,1)S(1)}) custom-call(bf16[16,2048]{1,0:T(8,128)(2,1)S(1)} %assemble.1.refs_1_.refs_0_, bf16[16,2048]{1,0:T(8,128)(2,1)S(1)} %collective-permute-done.14.refs_1_, ...), custom_call_target="tpu_custom_call" | custom-call | flops 1073741824 | bytes 65536 | tf_op jit(solution)/shard_map/output/output/pallas_call | solution.py:286
  45.5 1.9 %collective-permute-start.17 = (bf16[16,4096]{1,0:T(8,128)(2,1)S(1)}, bf16[16,4096]{1,0:T(8,128)(2,1)S(1)}, u32[]{:S(2)}, u32[]{:S(2)}) collective-permute-start(bf16[16,4096]{1,0:T(8,128)(2,1)S(1)} %get-tuple-element.44), channel_id=1, source_target_pairs={{0,2},{1,3},{2,0},{3,1},{4,6},{5,7},{6,4},{7,5},{8,10},{9,11},{10,... | collective-permute-start | bytes 393224 | tf_op jit(solution)/shard_map/sum_gy/ppermute | solution.py:319
  47.3 0.6 %collective-permute-start.18 = (bf16[16,4096]{1,0:T(8,128)(2,1)S(1)}, bf16[16,4096]{1,0:T(8,128)(2,1)S(1)}, u32[]{:S(2)}, u32[]{:S(2)}) collective-permute-start(bf16[16,4096]{1,0:T(8,128)(2,1)S(1)} %get-tuple-element.45), channel_id=1, source_target_pairs={{0,1},{1,0},{2,3},{3,2},{4,5},{5,4},{6,7},{7,6},{8,9},{9,8},{10,11... | collective-permute-start | bytes 393224 | tf_op jit(solution)/shard_map/sum_gy/ppermute | solution.py:319
  48.0 1.9 %collective-permute-start.19 = (bf16[16,4096]{1,0:T(8,128)(2,1)S(1)}, bf16[16,4096]{1,0:T(8,128)(2,1)S(1)}, u32[]{:S(2)}, u32[]{:S(2)}) collective-permute-start(bf16[16,4096]{1,0:T(8,128)(2,1)S(1)} %get-tuple-element.46), channel_id=1, source_target_pairs={{0,3},{1,2},{2,1},{3,0},{4,7},{5,6},{6,5},{7,4},{8,11},{9,10},{10,... | collective-permute-start | bytes 393224 | tf_op jit(solution)/shard_map/sum_gy/ppermute | solution.py:319
  49.9 7.4 %collective-permute-done.17.refs_1_ = bf16[16,4096]{1,0:T(8,128)(2,1)S(1)} collective-permute-done((bf16[16,4096]{1,0:T(8,128)(2,1)S(1)}, bf16[16,4096]{1,0:T(8,128)(2,1)S(1)}, u32[]{:S(2)}, u32[]{:S(2)}) %collective-permute-start.17) | collective-permute-done | bytes 131104 | tf_op jit(solution)/shard_map/sum_gy/ppermute | solution.py:319
  57.3 0.0 collective-permute-done.18.refs_2_
  57.3 0.0 collective-permute-done.19.refs_3_
  57.3 0.7 %add.1 = bf16[16,4096]{1,0:T(8,128)(2,1)} custom-call(bf16[16,4096]{1,0:T(8,128)(2,1)S(1)} %get-tuple-element.43.refs_0_, bf16[16,4096]{1,0:T(8,128)(2,1)S(1)} %collective-permute-done.17.refs_1_, bf16[16,4096]{1,0:T(8,128)(2,1)S(1)} %collective-permute-done.18.refs_2_, bf16[16,4096]{1,0:T(8,128)(2,1)S(1)} %collective-permute-done.19.refs_3_), custom_call_target="tpu_custom_call" | custom-call | bytes 65536 | tf_op jit(solution)/shard_map/sum_gy/add/pallas_call | solution.py:286
  (1 shorter events, 0.0 us)
Async XLA Ops:
  0.0 16.4 %copy-start.4 = (bf16[16,4096]{1,0:T(8,128)(2,1)S(1)}, bf16[16,4096]{1,0:T(8,128)(2,1)}, u32[]{:S(2)}) copy-start(bf16[16,4096]{1,0:T(8,128)(2,1)} %refs_1_.1) | copy-start | bytes 393220
  0.0 16.4 %copy-start.3 = (bf16[4096,128]{1,0:T(8,128)(2,1)S(1)}, bf16[4096,128]{1,0:T(8,128)(2,1)}, u32[]{:S(2)}) copy-start(bf16[4096,128]{1,0:T(8,128)(2,1)} %refs_8_.1) | copy-start | bytes 3145732
  0.0 16.4 %copy-start.2 = (bf16[4096,128]{1,0:T(8,128)(2,1)S(1)}, bf16[4096,128]{1,0:T(8,128)(2,1)}, u32[]{:S(2)}) copy-start(bf16[4096,128]{1,0:T(8,128)(2,1)} %refs_7_.1) | copy-start | bytes 3145732
  0.0 16.4 %copy-start.5 = (bf16[4096]{0:T(1024)(128)(2,1)S(1)}, bf16[4096]{0:T(1024)(128)(2,1)}, u32[]{:S(2)}) copy-start(bf16[4096]{0:T(1024)(128)(2,1)} %refs_5_.1) | copy-start | bytes 24580
  0.0 11.6 %collective-permute-start.1 = (bf16[16,4096]{1,0:T(8,128)(2,1)}, bf16[16,4096]{1,0:T(8,128)(2,1)S(1)}, u32[]{:S(2)}, u32[]{:S(2)}) collective-permute-start(bf16[16,4096]{1,0:T(8,128)(2,1)} %refs_1_.1), channel_id=1, source_target_pairs={{0,3},{1,2},{2,1},{3,0},{4,7},{5,6},{6,5},{7,4},{8,11},{9,10},{10,... | collective-permute-start | bytes 393224 | tf_op jit(solution)/shard_map/gather_hidden/ppermute | solution.py:319
  5.1 11.3 %collective-permute-start = (bf16[16,4096]{1,0:T(8,128)(2,1)}, bf16[16,4096]{1,0:T(8,128)(2,1)S(1)}, u32[]{:S(2)}, u32[]{:S(2)}) collective-permute-start(bf16[16,4096]{1,0:T(8,128)(2,1)} %refs_1_.1), channel_id=1, source_target_pairs={{0,2},{1,3},{2,0},{3,1},{4,6},{5,7},{6,4},{7,5},{8,10},{9,11},{10,... | collective-permute-start | bytes 393224 | tf_op jit(solution)/shard_map/gather_hidden/ppermute | solution.py:319
  5.1 11.3 %collective-permute-start.2 = (bf16[16,4096]{1,0:T(8,128)(2,1)}, bf16[16,4096]{1,0:T(8,128)(2,1)S(1)}, u32[]{:S(2)}, u32[]{:S(2)}) collective-permute-start(bf16[16,4096]{1,0:T(8,128)(2,1)} %refs_1_.1), channel_id=1, source_target_pairs={{0,1},{1,0},{2,3},{3,2},{4,5},{5,4},{6,7},{7,6},{8,9},{9,8},{10,11... | collective-permute-start | bytes 393224 | tf_op jit(solution)/shard_map/gather_hidden/ppermute | solution.py:319
  11.6 10.1 %copy-start.6 = (s32[4]{0:T(128)S(1)}, s32[4]{0:T(128)}, u32[]{:S(2)}) copy-start(s32[4]{0:T(128)} %refs_2_.3) | copy-start | bytes 52
  19.5 10.4 %copy-start = (bf16[4,256,512]{2,1,0:T(8,128)(2,1)S(1)}, bf16[4,256,512]{2,1,0:T(8,128)(2,1)}, u32[]{:S(2)}) copy-start(bf16[4,256,512]{2,1,0:T(8,128)(2,1)} %refs_2_.5) | copy-start | bytes 3145732
  19.5 10.3 %copy-start.1 = (bf16[4,256,512]{2,1,0:T(8,128)(2,1)S(1)}, bf16[4,256,512]{2,1,0:T(8,128)(2,1)}, u32[]{:S(2)}) copy-start(bf16[4,256,512]{2,1,0:T(8,128)(2,1)} %refs_3_.3) | copy-start | bytes 3145732
  19.5 5.0 %collective-permute-start.3 = (bf16[16,2432]{1,0:T(8,128)(2,1)S(1)}, bf16[16,2432]{1,0:T(8,128)(2,1)S(1)}, u32[]{:S(2)}, u32[]{:S(2)}) collective-permute-start(bf16[16,2432]{1,0:T(8,128)(2,1)S(1)} %get-tuple-element.28), channel_id=1, source_target_pairs={{0,8},{4,12},{8,0},{12,4},{1,9},{5,13},{9,1},{13,5},{2,10},{6,14},... | collective-permute-start | bytes 233480 | tf_op jit(solution)/shard_map/sum_gx/ppermute | solution.py:319
  21.0 3.4 %collective-permute-start.4 = (bf16[16,2432]{1,0:T(8,128)(2,1)S(1)}, bf16[16,2432]{1,0:T(8,128)(2,1)S(1)}, u32[]{:S(2)}, u32[]{:S(2)}) collective-permute-start(bf16[16,2432]{1,0:T(8,128)(2,1)S(1)} %get-tuple-element.29), channel_id=1, source_target_pairs={{0,4},{4,0},{8,12},{12,8},{1,5},{5,1},{9,13},{13,9},{2,6},{6,2},{1... | collective-permute-start | bytes 233480 | tf_op jit(solution)/shard_map/sum_gx/ppermute | solution.py:319
  21.0 4.0 %collective-permute-start.5 = (bf16[16,2432]{1,0:T(8,128)(2,1)S(1)}, bf16[16,2432]{1,0:T(8,128)(2,1)S(1)}, u32[]{:S(2)}, u32[]{:S(2)}) collective-permute-start(bf16[16,2432]{1,0:T(8,128)(2,1)S(1)} %get-tuple-element.30), channel_id=1, source_target_pairs={{0,12},{4,8},{8,4},{12,0},{1,13},{5,9},{9,5},{13,1},{2,14},{6,10},... | collective-permute-start | bytes 233480 | tf_op jit(solution)/shard_map/sum_gx/ppermute | solution.py:319
  25.2 3.4 %collective-permute-start.6 = (bf16[4,2432]{1,0:T(4,128)(2,1)S(1)}, bf16[4,2432]{1,0:T(4,128)(2,1)S(1)}, u32[]{:S(2)}, u32[]{:S(2)}) collective-permute-start(bf16[4,2432]{1,0:T(4,128)(2,1)S(1)} %get-tuple-element.31), channel_id=1, source_target_pairs={{0,4},{1,5},{2,6},{3,7},{4,0},{5,1},{6,2},{7,3},{8,12},{9,13},{10,... | collective-permute-start | bytes 58376 | tf_op jit(solution)/shard_map/to_owner/ppermute | solution.py:329
  25.7 4.1 %collective-permute-start.7 = (bf16[4,2432]{1,0:T(4,128)(2,1)S(1)}, bf16[4,2432]{1,0:T(4,128)(2,1)S(1)}, u32[]{:S(2)}, u32[]{:S(2)}) collective-permute-start(bf16[4,2432]{1,0:T(4,128)(2,1)S(1)} %get-tuple-element.32), channel_id=1, source_target_pairs={{0,6},{1,7},{2,4},{3,5},{4,2},{5,3},{6,0},{7,1},{8,14},{9,15},{10,... | collective-permute-start | bytes 58376 | tf_op jit(solution)/shard_map/to_owner/ppermute | solution.py:329
  25.7 5.2 %collective-permute-start.10 = (bf16[4,2432]{1,0:T(4,128)(2,1)S(1)}, bf16[4,2432]{1,0:T(4,128)(2,1)S(1)}, u32[]{:S(2)}, u32[]{:S(2)}) collective-permute-start(bf16[4,2432]{1,0:T(4,128)(2,1)S(1)} %get-tuple-element.38), channel_id=1, source_target_pairs={{0,7},{1,6},{2,5},{3,4},{4,3},{5,2},{6,1},{7,0},{8,15},{9,14},{10,... | collective-permute-start | bytes 58376 | tf_op jit(solution)/shard_map/to_owner/ppermute | solution.py:329
  27.9 3.3 %collective-permute-start.11 = (bf16[4,2432]{1,0:T(4,128)(2,1)S(1)}, bf16[4,2432]{1,0:T(4,128)(2,1)S(1)}, u32[]{:S(2)}, u32[]{:S(2)}) collective-permute-start(bf16[4,2432]{1,0:T(4,128)(2,1)S(1)} %get-tuple-element.39), channel_id=1, source_target_pairs={{0,5},{1,4},{2,7},{3,6},{4,1},{5,0},{6,3},{7,2},{8,13},{9,12},{10,... | collective-permute-start | bytes 58376 | tf_op jit(solution)/shard_map/to_owner/ppermute | solution.py:329
  30.5 4.2 %collective-permute-start.8 = (bf16[4,2048]{1,0:T(4,128)(2,1)S(1)}, bf16[4,2048]{1,0:T(4,128)(2,1)S(1)}, u32[]{:S(2)}, u32[]{:S(2)}) collective-permute-start(bf16[4,2048]{1,0:T(4,128)(2,1)S(1)} %get-tuple-element.36), channel_id=1, source_target_pairs={{0,4},{1,5},{2,6},{3,7},{4,0},{5,1},{6,2},{7,3},{8,12},{9,13},{10,... | collective-permute-start | bytes 49160 | tf_op jit(solution)/shard_map/to_head_rows/ppermute | solution.py:329
  30.8 4.1 %collective-permute-start.9 = (bf16[4,2048]{1,0:T(4,128)(2,1)S(1)}, bf16[4,2048]{1,0:T(4,128)(2,1)S(1)}, u32[]{:S(2)}, u32[]{:S(2)}) collective-permute-start(bf16[4,2048]{1,0:T(4,128)(2,1)S(1)} %get-tuple-element.37), channel_id=1, source_target_pairs={{0,6},{1,7},{2,4},{3,5},{4,2},{5,3},{6,0},{7,1},{8,14},{9,15},{10,... | collective-permute-start | bytes 49160 | tf_op jit(solution)/shard_map/to_head_rows/ppermute | solution.py:329
  31.9 5.0 %collective-permute-start.12 = (bf16[4,2048]{1,0:T(4,128)(2,1)S(1)}, bf16[4,2048]{1,0:T(4,128)(2,1)S(1)}, u32[]{:S(2)}, u32[]{:S(2)}) collective-permute-start(bf16[4,2048]{1,0:T(4,128)(2,1)S(1)} %get-tuple-element.40), channel_id=1, source_target_pairs={{0,7},{1,6},{2,5},{3,4},{4,3},{5,2},{6,1},{7,0},{8,15},{9,14},{10,... | collective-permute-start | bytes 49160 | tf_op jit(solution)/shard_map/to_head_rows/ppermute | solution.py:329
  34.0 3.2 %collective-permute-start.13 = (bf16[4,2048]{1,0:T(4,128)(2,1)S(1)}, bf16[4,2048]{1,0:T(4,128)(2,1)S(1)}, u32[]{:S(2)}, u32[]{:S(2)}) collective-permute-start(bf16[4,2048]{1,0:T(4,128)(2,1)S(1)} %get-tuple-element.41), channel_id=1, source_target_pairs={{0,5},{1,4},{2,7},{3,6},{4,1},{5,0},{6,3},{7,2},{8,13},{9,12},{10,... | collective-permute-start | bytes 49160 | tf_op jit(solution)/shard_map/to_head_rows/ppermute | solution.py:329
  37.2 5.0 %collective-permute-start.16 = (bf16[16,2048]{1,0:T(8,128)(2,1)S(1)}, bf16[16,2048]{1,0:T(8,128)(2,1)S(1)}, u32[]{:S(2)}, u32[]{:S(2)}) collective-permute-start(bf16[16,2048]{1,0:T(8,128)(2,1)S(1)} %assemble.1.refs_1_.refs_0_), channel_id=1, source_target_pairs={{0,12},{4,8},{8,4},{12,0},{1,13},{5,9},{9,5},{13,1},{2,14},{6,10},... | collective-permute-start | bytes 196616 | tf_op jit(solution)/shard_map/gather_gx/ppermute | solution.py:319
  38.5 3.8 %collective-permute-start.15 = (bf16[16,2048]{1,0:T(8,128)(2,1)S(1)}, bf16[16,2048]{1,0:T(8,128)(2,1)S(1)}, u32[]{:S(2)}, u32[]{:S(2)}) collective-permute-start(bf16[16,2048]{1,0:T(8,128)(2,1)S(1)} %assemble.1.refs_1_.refs_0_), channel_id=1, source_target_pairs={{0,4},{4,0},{8,12},{12,8},{1,5},{5,1},{9,13},{13,9},{2,6},{6,2},{1... | collective-permute-start | bytes 196616 | tf_op jit(solution)/shard_map/gather_gx/ppermute | solution.py:319
  38.8 4.3 %collective-permute-start.14 = (bf16[16,2048]{1,0:T(8,128)(2,1)S(1)}, bf16[16,2048]{1,0:T(8,128)(2,1)S(1)}, u32[]{:S(2)}, u32[]{:S(2)}) collective-permute-start(bf16[16,2048]{1,0:T(8,128)(2,1)S(1)} %assemble.1.refs_1_.refs_0_), channel_id=1, source_target_pairs={{0,8},{4,12},{8,0},{12,4},{1,9},{5,13},{9,1},{13,5},{2,10},{6,14},... | collective-permute-start | bytes 196616 | tf_op jit(solution)/shard_map/gather_gx/ppermute | solution.py:319
  45.5 11.8 %collective-permute-start.17 = (bf16[16,4096]{1,0:T(8,128)(2,1)S(1)}, bf16[16,4096]{1,0:T(8,128)(2,1)S(1)}, u32[]{:S(2)}, u32[]{:S(2)}) collective-permute-start(bf16[16,4096]{1,0:T(8,128)(2,1)S(1)} %get-tuple-element.44), channel_id=1, source_target_pairs={{0,2},{1,3},{2,0},{3,1},{4,6},{5,7},{6,4},{7,5},{8,10},{9,11},{10,... | collective-permute-start | bytes 393224 | tf_op jit(solution)/shard_map/sum_gy/ppermute | solution.py:319
  47.3 9.9 %collective-permute-start.18 = (bf16[16,4096]{1,0:T(8,128)(2,1)S(1)}, bf16[16,4096]{1,0:T(8,128)(2,1)S(1)}, u32[]{:S(2)}, u32[]{:S(2)}) collective-permute-start(bf16[16,4096]{1,0:T(8,128)(2,1)S(1)} %get-tuple-element.45), channel_id=1, source_target_pairs={{0,1},{1,0},{2,3},{3,2},{4,5},{5,4},{6,7},{7,6},{8,9},{9,8},{10,11... | collective-permute-start | bytes 393224 | tf_op jit(solution)/shard_map/sum_gy/ppermute | solution.py:319
  48.0 9.3 %collective-permute-start.19 = (bf16[16,4096]{1,0:T(8,128)(2,1)S(1)}, bf16[16,4096]{1,0:T(8,128)(2,1)S(1)}, u32[]{:S(2)}, u32[]{:S(2)}) collective-permute-start(bf16[16,4096]{1,0:T(8,128)(2,1)S(1)} %get-tuple-element.46), channel_id=1, source_target_pairs={{0,3},{1,2},{2,1},{3,0},{4,7},{5,6},{6,5},{7,4},{8,11},{9,10},{10,... | collective-permute-start | bytes 393224 | tf_op jit(solution)/shard_map/sum_gy/ppermute | solution.py:319

commit v8 on v7

--- a/solution.py
+++ b/solution.py
@@ -94,13 +94,6 @@
         outs[offset][...] = held[me ^ offset].astype(jnp.bfloat16)
 
 
-def spread(rows, group):
-    repeat = min(group, max(1, 8 // rows.shape[0]))
-    tile = jnp.concatenate([rows] * repeat, axis=0) if repeat > 1 else rows
-    wide = jnp.broadcast_to(tile[None], (group // repeat, *tile.shape))
-    return wide.reshape(group * rows.shape[0], rows.shape[1])
-
-
 def attend_kernel(offsets, group, features, *refs):
     count = len(offsets)
     pieces = refs[:count]
@@ -116,7 +109,6 @@
         pieces[0][:, width - LANES :].astype(jnp.float32), axis=1, keepdims=True
     )
     row_scale = lax.rsqrt(squares / features + EPSILON)
-    row_scales = spread(row_scale, group)
     valid = lax.broadcasted_iota(jnp.int32, (rows, slots), 1) < filled[:, :1]
 
     def per_head(sequences):
@@ -130,23 +122,22 @@
 
     states, scores = [], []
     for index, offset in enumerate(offsets):
-        piece = pieces[index][...].astype(jnp.float32)
+        piece = pieces[index][...].astype(jnp.float32) * row_scale
         head = me ^ offset
         lanes = pl.ds(pl.multiple_of(head * HEAD_SIZE, HEAD_SIZE), HEAD_SIZE)
         query = jnp.concatenate(
             [piece[:, h * HEAD_SIZE : (h + 1) * HEAD_SIZE] for h in range(group)], axis=0
         )
-        query = query * row_scales
         query = query * cosine + pltpu.roll(query, HEAD_SIZE // 2, 1) * sine
         rows_of[index] = query.astype(jnp.bfloat16).astype(jnp.float32)
         first = group * HEAD_SIZE
-        fresh_key = piece[:, first : first + HEAD_SIZE] * row_scale
+        fresh_key = piece[:, first : first + HEAD_SIZE]
         fresh_key = (
             fresh_key * cosine[:share] + pltpu.roll(fresh_key, HEAD_SIZE // 2, 1) * sine[:share]
         )
         fresh_key = per_head(fresh_key.astype(jnp.bfloat16).astype(jnp.float32))
         first = first + HEAD_SIZE
-        fresh_value = piece[:, first : first + HEAD_SIZE] * row_scale
+        fresh_value = piece[:, first : first + HEAD_SIZE]
         fresh_value = per_head(fresh_value.astype(jnp.bfloat16).astype(jnp.float32))
         queries = [rows_of[index, pl.ds(n, group, stride=share), :] for n in range(share)]
         own = scale * jnp.sum(

time: 58.6 us -> 58.4 us (level)
  no operation moved by 1% of the time
where the time goes in v8:
time: 58.4 us; the launch traced here: 57.9 us
  starting transfers between devices  21.1 us (36%)
  Pallas kernels  18.8 us (32%)
  waiting for transfers between devices  17.9 us (31%)
    pallas_call x10, Pallas kernels, call(): pl.pallas_call(functools.partial(loading, kernel, parts, (len(after), len...  18.8 us
    ppermute x12, starting transfers between devices, exchange(): lax.ppermute(pieces[offset], axis, [(n, n ^ offset) for n in range(count)])  14.6 us
    ppermute x12, waiting for transfers between devices, exchange(): lax.ppermute(pieces[offset], axis, [(n, n ^ offset) for n in range(count)])  13.6 us
    ppermute x8, starting transfers between devices, crossing_exchange(): lax.ppermute(pieces[offset], ('gx', 'gy'), [(n, n ^ count ^ offset) for n...  6.43 us
    ppermute x8, waiting for transfers between devices, crossing_exchange(): lax.ppermute(pieces[offset], ('gx', 'gy'), [(n, n ^ count ^ offset) for n...  4.21 us
  transfers between devices with their start and end apart: 20, of which 9 were waited for; matrix products, arithmetic and copies ran while one was open for 0% of the time, Pallas kernels for 22%

profile of v8, /device:TPU:0, one launch (start us, length us, event | category | flops | bytes accessed | tf_op | source)
XLA Modules:
  0.0 57.9 jit_solution(17287984999359143920)
XLA Ops:
  0.0 0.0 copy-start.4
  0.0 0.0 copy-start.3
  0.0 0.0 copy-start.2
  0.0 0.0 copy-start.5
  0.0 5.1 %collective-permute-start.1 = (bf16[16,4096]{1,0:T(8,128)(2,1)}, bf16[16,4096]{1,0:T(8,128)(2,1)S(1)}, u32[]{:S(2)}, u32[]{:S(2)}) collective-permute-start(bf16[16,4096]{1,0:T(8,128)(2,1)} %refs_1_.1), channel_id=1, source_target_pairs={{0,3},{1,2},{2,1},{3,0},{4,7},{5,6},{6,5},{7,4},{8,11},{9,10},{10,... | collective-permute-start | bytes 393224 | tf_op jit(solution)/shard_map/gather_hidden/ppermute | solution.py:310
  5.1 0.0 collective-permute-start
  5.1 0.6 %collective-permute-start.2 = (bf16[16,4096]{1,0:T(8,128)(2,1)}, bf16[16,4096]{1,0:T(8,128)(2,1)S(1)}, u32[]{:S(2)}, u32[]{:S(2)}) collective-permute-start(bf16[16,4096]{1,0:T(8,128)(2,1)} %refs_1_.1), channel_id=1, source_target_pairs={{0,1},{1,0},{2,3},{3,2},{4,5},{5,4},{6,7},{7,6},{8,9},{9,8},{10,11... | collective-permute-start | bytes 393224 | tf_op jit(solution)/shard_map/gather_hidden/ppermute | solution.py:310
  5.8 5.8 %fetch_query.1.refs_6_ = bf16[4096,2048]{1,0:T(8,128)(2,1)S(1)} custom-call(bf16[4096,2048]{1,0:T(8,128)(2,1)} %refs_0_.4), custom_call_target="tpu_custom_call" | custom-call | bytes 33619968 | tf_op jit(solution)/shard_map/fetch_query/fetch_query/pallas_call | solution.py:277
  11.6 0.0 copy-start.6
  11.6 0.0 collective-permute-done.1.refs_3_
  11.6 4.8 %collective-permute-done.refs_2_ = bf16[16,4096]{1,0:T(8,128)(2,1)S(1)} collective-permute-done((bf16[16,4096]{1,0:T(8,128)(2,1)}, bf16[16,4096]{1,0:T(8,128)(2,1)S(1)}, u32[]{:S(2)}, u32[]{:S(2)}) %collective-permute-start) | collective-permute-done | bytes 131104 | tf_op jit(solution)/shard_map/gather_hidden/ppermute | solution.py:310
  16.4 0.0 collective-permute-done.2.refs_4_
  16.4 0.0 copy-done.4
  16.4 0.0 copy-done.3
  16.4 0.0 copy-done.2
  16.4 0.0 copy-done.5
  16.5 3.0 %project.1 = (bf16[16,2432]{1,0:T(8,128)(2,1)S(1)}, bf16[16,2432]{1,0:T(8,128)(2,1)S(1)}, bf16[16,2432]{1,0:T(8,128)(2,1)S(1)}, bf16[16,2432]{1,0:T(8,128)(2,1)S(1)}, bf16[768,4096]{1,0:T(8,128)(2,1)S(1)}) custom-call(bf16[2048,4096]{1,0:T(8,128)(2,1)} %refs_0_.7, bf16[16,4096]{1,0:T(8,128)(2,1)S(1)} %copy-done.4, ...), custom_call_target="tpu_custom_call" | custom-call | flops 1207959552 | bytes 12648448 | tf_op jit(solution)/shard_map/project/project/pallas_call | solution.py:277
  19.5 0.0 copy-start
  19.5 0.0 copy-start.1
  19.5 1.6 %collective-permute-start.3 = (bf16[16,2432]{1,0:T(8,128)(2,1)S(1)}, bf16[16,2432]{1,0:T(8,128)(2,1)S(1)}, u32[]{:S(2)}, u32[]{:S(2)}) collective-permute-start(bf16[16,2432]{1,0:T(8,128)(2,1)S(1)} %get-tuple-element.28), channel_id=1, source_target_pairs={{0,8},{4,12},{8,0},{12,4},{1,9},{5,13},{9,1},{13,5},{2,10},{6,14},... | collective-permute-start | bytes 233480 | tf_op jit(solution)/shard_map/sum_gx/ppermute | solution.py:310
  21.0 0.0 collective-permute-start.4
  21.0 0.6 %collective-permute-start.5 = (bf16[16,2432]{1,0:T(8,128)(2,1)S(1)}, bf16[16,2432]{1,0:T(8,128)(2,1)S(1)}, u32[]{:S(2)}, u32[]{:S(2)}) collective-permute-start(bf16[16,2432]{1,0:T(8,128)(2,1)S(1)} %get-tuple-element.30), channel_id=1, source_target_pairs={{0,12},{4,8},{8,4},{12,0},{1,13},{5,9},{9,5},{13,1},{2,14},{6,10},... | collective-permute-start | bytes 233480 | tf_op jit(solution)/shard_map/sum_gx/ppermute | solution.py:310
  21.7 0.0 copy-done.6
  21.7 2.7 %fetch_output.2 = (f32[64,128]{1,0:T(8,128)S(1)}, f32[64,128]{1,0:T(8,128)S(1)}, s32[64,128]{1,0:T(8,128)S(1)}, bf16[512,4096]{1,0:T(8,128)(2,1)S(1)}) custom-call(bf16[2048,4096]{1,0:T(8,128)(2,1)} %refs_0_.7, bf16[16,2432]{1,0:T(8,128)(2,1)S(1)} %get-tuple-element.26.refs_1_, s32[4]{0:T(128)S(1)} %copy-done.6), custom_call_target="tpu_custom_call" | custom-call | bytes 8454144 | tf_op jit(solution)/shard_map/sum_gx/fetch_output/pallas_call | solution.py:277
  24.4 0.0 collective-permute-done.3.refs_2_
  24.4 0.0 collective-permute-done.4.refs_3_
  24.5 0.6 %collective-permute-done.5.refs_4_ = bf16[16,2432]{1,0:T(8,128)(2,1)S(1)} collective-permute-done((bf16[16,2432]{1,0:T(8,128)(2,1)S(1)}, bf16[16,2432]{1,0:T(8,128)(2,1)S(1)}, u32[]{:S(2)}, u32[]{:S(2)}) %collective-permute-start.5) | collective-permute-done | bytes 77856 | tf_op jit(solution)/shard_map/sum_gx/ppermute | solution.py:310
  25.0 0.1 combine.1
  25.2 0.5 collective-permute-start.6
  25.7 0.0 collective-permute-start.7
  25.7 2.2 %collective-permute-start.10 = (bf16[4,2432]{1,0:T(4,128)(2,1)S(1)}, bf16[4,2432]{1,0:T(4,128)(2,1)S(1)}, u32[]{:S(2)}, u32[]{:S(2)}) collective-permute-start(bf16[4,2432]{1,0:T(4,128)(2,1)S(1)} %get-tuple-element.38), channel_id=1, source_target_pairs={{0,7},{1,6},{2,5},{3,4},{4,3},{5,2},{6,1},{7,0},{8,15},{9,14},{10,... | collective-permute-start | bytes 58376 | tf_op jit(solution)/shard_map/to_owner/ppermute | solution.py:320
  27.9 0.7 %collective-permute-start.11 = (bf16[4,2432]{1,0:T(4,128)(2,1)S(1)}, bf16[4,2432]{1,0:T(4,128)(2,1)S(1)}, u32[]{:S(2)}, u32[]{:S(2)}) collective-permute-start(bf16[4,2432]{1,0:T(4,128)(2,1)S(1)} %get-tuple-element.39), channel_id=1, source_target_pairs={{0,5},{1,4},{2,7},{3,6},{4,1},{5,0},{6,3},{7,2},{8,13},{9,12},{10,... | collective-permute-start | bytes 58376 | tf_op jit(solution)/shard_map/to_owner/ppermute | solution.py:320
  28.6 0.0 collective-permute-done.6.refs_0_
  28.6 1.2 %collective-permute-done.7.refs_1_ = bf16[4,2432]{1,0:T(4,128)(2,1)S(1)} collective-permute-done((bf16[4,2432]{1,0:T(4,128)(2,1)S(1)}, bf16[4,2432]{1,0:T(4,128)(2,1)S(1)}, u32[]{:S(2)}, u32[]{:S(2)}) %collective-permute-start.7) | collective-permute-done | bytes 19488 | tf_op jit(solution)/shard_map/to_owner/ppermute | solution.py:320
  29.8 0.0 copy-done
  29.8 0.0 copy-done.1
  29.8 0.6 %attend.2 = (bf16[4,2048]{1,0:T(4,128)(2,1)S(1)}, bf16[4,2048]{1,0:T(4,128)(2,1)S(1)}) custom-call(bf16[4,2432]{1,0:T(4,128)(2,1)S(1)} %collective-permute-done.6.refs_0_, bf16[4,2432]{1,0:T(4,128)(2,1)S(1)} %collective-permute-done.7.refs_1_, bf16[4,256,512]{2,1,0:T(8,128)(2,1)S(1)} %copy-done, bf16[4,256,512]{2,1,0:T(8,128)(2,1)S(1)} %copy-done.1, ...), custom_call_target="tpu_custom_call" | custom-call | bytes 65536 | tf_op jit(solution)/shard_map/attend/attend/pallas_call | solution.py:277
  30.4 0.3 collective-permute-start.8
  30.7 0.1 collective-permute-start.9
  30.8 0.0 collective-permute-done.10.refs_0_
  30.8 0.5 collective-permute-done.11.refs_1_
  31.2 0.6 %attend.3 = (bf16[4,2048]{1,0:T(4,128)(2,1)S(1)}, bf16[4,2048]{1,0:T(4,128)(2,1)S(1)}) custom-call(bf16[4,2432]{1,0:T(4,128)(2,1)S(1)} %collective-permute-done.10.refs_0_, bf16[4,2432]{1,0:T(4,128)(2,1)S(1)} %collective-permute-done.11.refs_1_, bf16[4,256,512]{2,1,0:T(8,128)(2,1)S(1)} %copy-done, bf16[4,256,512]{2,1,0:T(8,128)(2,1)S(1)} %copy-done.1, ...), custom_call_target="tpu_custom_call" | custom-call | bytes 65536 | tf_op jit(solution)/shard_map/attend/attend/pallas_call | solution.py:277
  31.9 2.0 %collective-permute-start.12 = (bf16[4,2048]{1,0:T(4,128)(2,1)S(1)}, bf16[4,2048]{1,0:T(4,128)(2,1)S(1)}, u32[]{:S(2)}, u32[]{:S(2)}) collective-permute-start(bf16[4,2048]{1,0:T(4,128)(2,1)S(1)} %get-tuple-element.40), channel_id=1, source_target_pairs={{0,7},{1,6},{2,5},{3,4},{4,3},{5,2},{6,1},{7,0},{8,15},{9,14},{10,... | collective-permute-start | bytes 49160 | tf_op jit(solution)/shard_map/to_head_rows/ppermute | solution.py:320
  33.9 0.6 %collective-permute-start.13 = (bf16[4,2048]{1,0:T(4,128)(2,1)S(1)}, bf16[4,2048]{1,0:T(4,128)(2,1)S(1)}, u32[]{:S(2)}, u32[]{:S(2)}) collective-permute-start(bf16[4,2048]{1,0:T(4,128)(2,1)S(1)} %get-tuple-element.41), channel_id=1, source_target_pairs={{0,5},{1,4},{2,7},{3,6},{4,1},{5,0},{6,3},{7,2},{8,13},{9,12},{10,... | collective-permute-start | bytes 49160 | tf_op jit(solution)/shard_map/to_head_rows/ppermute | solution.py:320
  34.5 0.0 collective-permute-done.8.refs_0_
  34.5 0.3 collective-permute-done.9.refs_1_
  34.8 2.1 %collective-permute-done.12.refs_2_ = bf16[4,2048]{1,0:T(4,128)(2,1)S(1)} collective-permute-done((bf16[4,2048]{1,0:T(4,128)(2,1)S(1)}, bf16[4,2048]{1,0:T(4,128)(2,1)S(1)}, u32[]{:S(2)}, u32[]{:S(2)}) %collective-permute-start.12) | collective-permute-done | bytes 16416 | tf_op jit(solution)/shard_map/to_head_rows/ppermute | solution.py:320
  36.9 0.2 collective-permute-done.13.refs_3_
  37.1 1.3 %collective-permute-start.16 = (bf16[16,2048]{1,0:T(8,128)(2,1)S(1)}, bf16[16,2048]{1,0:T(8,128)(2,1)S(1)}, u32[]{:S(2)}, u32[]{:S(2)}) collective-permute-start(bf16[16,2048]{1,0:T(8,128)(2,1)S(1)} %assemble.1.refs_1_.refs_0_), channel_id=1, source_target_pairs={{0,12},{4,8},{8,4},{12,0},{1,13},{5,9},{9,5},{13,1},{2,14},{6,10},... | collective-permute-start | bytes 196616 | tf_op jit(solution)/shard_map/gather_gx/ppermute | solution.py:310
  38.4 0.3 collective-permute-start.15
  38.7 0.7 %collective-permute-start.14 = (bf16[16,2048]{1,0:T(8,128)(2,1)S(1)}, bf16[16,2048]{1,0:T(8,128)(2,1)S(1)}, u32[]{:S(2)}, u32[]{:S(2)}) collective-permute-start(bf16[16,2048]{1,0:T(8,128)(2,1)S(1)} %assemble.1.refs_1_.refs_0_), channel_id=1, source_target_pairs={{0,8},{4,12},{8,0},{12,4},{1,9},{5,13},{9,1},{13,5},{2,10},{6,14},... | collective-permute-start | bytes 196616 | tf_op jit(solution)/shard_map/gather_gx/ppermute | solution.py:310
  39.3 2.8 %fetch_output.3.refs_6_ = bf16[768,4096]{1,0:T(8,128)(2,1)S(1)} custom-call(bf16[2048,4096]{1,0:T(8,128)(2,1)} %refs_0_.7, bf16[16,2048]{1,0:T(8,128)(2,1)S(1)} %assemble.1.refs_1_.refs_0_), custom_call_target="tpu_custom_call" | custom-call | bytes 12648448 | tf_op jit(solution)/shard_map/gather_gx/fetch_output/pallas_call | solution.py:277
  42.1 0.0 collective-permute-done.16.refs_3_
  42.1 0.0 collective-permute-done.15.refs_2_
  42.1 0.8 %collective-permute-done.14.refs_1_ = bf16[16,2048]{1,0:T(8,128)(2,1)S(1)} collective-permute-done((bf16[16,2048]{1,0:T(8,128)(2,1)S(1)}, bf16[16,2048]{1,0:T(8,128)(2,1)S(1)}, u32[]{:S(2)}, u32[]{:S(2)}) %collective-permute-start.14) | collective-permute-done | bytes 65568 | tf_op jit(solution)/shard_map/gather_gx/ppermute | solution.py:310
  43.0 2.4 %output.1 = (bf16[16,4096]{1,0:T(8,128)(2,1)S(1)}, bf16[16,4096]{1,0:T(8,128)(2,1)S(1)}, bf16[16,4096]{1,0:T(8,128)(2,1)S(1)}, bf16[16,4096]{1,0:T(8,128)(2,1)S(1)}) custom-call(bf16[16,2048]{1,0:T(8,128)(2,1)S(1)} %assemble.1.refs_1_.refs_0_, bf16[16,2048]{1,0:T(8,128)(2,1)S(1)} %collective-permute-done.14.refs_1_, ...), custom_call_target="tpu_custom_call" | custom-call | flops 1073741824 | bytes 65536 | tf_op jit(solution)/shard_map/output/output/pallas_call | solution.py:277
  45.3 1.9 %collective-permute-start.17 = (bf16[16,4096]{1,0:T(8,128)(2,1)S(1)}, bf16[16,4096]{1,0:T(8,128)(2,1)S(1)}, u32[]{:S(2)}, u32[]{:S(2)}) collective-permute-start(bf16[16,4096]{1,0:T(8,128)(2,1)S(1)} %get-tuple-element.44), channel_id=1, source_target_pairs={{0,2},{1,3},{2,0},{3,1},{4,6},{5,7},{6,4},{7,5},{8,10},{9,11},{10,... | collective-permute-start | bytes 393224 | tf_op jit(solution)/shard_map/sum_gy/ppermute | solution.py:310
  47.2 0.7 %collective-permute-start.18 = (bf16[16,4096]{1,0:T(8,128)(2,1)S(1)}, bf16[16,4096]{1,0:T(8,128)(2,1)S(1)}, u32[]{:S(2)}, u32[]{:S(2)}) collective-permute-start(bf16[16,4096]{1,0:T(8,128)(2,1)S(1)} %get-tuple-element.45), channel_id=1, source_target_pairs={{0,1},{1,0},{2,3},{3,2},{4,5},{5,4},{6,7},{7,6},{8,9},{9,8},{10,11... | collective-permute-start | bytes 393224 | tf_op jit(solution)/shard_map/sum_gy/ppermute | solution.py:310
  47.9 1.9 %collective-permute-start.19 = (bf16[16,4096]{1,0:T(8,128)(2,1)S(1)}, bf16[16,4096]{1,0:T(8,128)(2,1)S(1)}, u32[]{:S(2)}, u32[]{:S(2)}) collective-permute-start(bf16[16,4096]{1,0:T(8,128)(2,1)S(1)} %get-tuple-element.46), channel_id=1, source_target_pairs={{0,3},{1,2},{2,1},{3,0},{4,7},{5,6},{6,5},{7,4},{8,11},{9,10},{10,... | collective-permute-start | bytes 393224 | tf_op jit(solution)/shard_map/sum_gy/ppermute | solution.py:310
  49.8 7.3 %collective-permute-done.17.refs_1_ = bf16[16,4096]{1,0:T(8,128)(2,1)S(1)} collective-permute-done((bf16[16,4096]{1,0:T(8,128)(2,1)S(1)}, bf16[16,4096]{1,0:T(8,128)(2,1)S(1)}, u32[]{:S(2)}, u32[]{:S(2)}) %collective-permute-start.17) | collective-permute-done | bytes 131104 | tf_op jit(solution)/shard_map/sum_gy/ppermute | solution.py:310
  57.1 0.0 collective-permute-done.18.refs_2_
  57.2 0.0 collective-permute-done.19.refs_3_
  57.2 0.7 %add.1 = bf16[16,4096]{1,0:T(8,128)(2,1)} custom-call(bf16[16,4096]{1,0:T(8,128)(2,1)S(1)} %get-tuple-element.43.refs_0_, bf16[16,4096]{1,0:T(8,128)(2,1)S(1)} %collective-permute-done.17.refs_1_, bf16[16,4096]{1,0:T(8,128)(2,1)S(1)} %collective-permute-done.18.refs_2_, bf16[16,4096]{1,0:T(8,128)(2,1)S(1)} %collective-permute-done.19.refs_3_), custom_call_target="tpu_custom_call" | custom-call | bytes 65536 | tf_op jit(solution)/shard_map/sum_gy/add/pallas_call | solution.py:277
  (1 shorter events, 0.0 us)
Async XLA Ops:
  0.0 16.4 %copy-start.4 = (bf16[16,4096]{1,0:T(8,128)(2,1)S(1)}, bf16[16,4096]{1,0:T(8,128)(2,1)}, u32[]{:S(2)}) copy-start(bf16[16,4096]{1,0:T(8,128)(2,1)} %refs_1_.1) | copy-start | bytes 393220
  0.0 16.4 %copy-start.3 = (bf16[4096,128]{1,0:T(8,128)(2,1)S(1)}, bf16[4096,128]{1,0:T(8,128)(2,1)}, u32[]{:S(2)}) copy-start(bf16[4096,128]{1,0:T(8,128)(2,1)} %refs_8_.1) | copy-start | bytes 3145732
  0.0 16.4 %copy-start.2 = (bf16[4096,128]{1,0:T(8,128)(2,1)S(1)}, bf16[4096,128]{1,0:T(8,128)(2,1)}, u32[]{:S(2)}) copy-start(bf16[4096,128]{1,0:T(8,128)(2,1)} %refs_7_.1) | copy-start | bytes 3145732
  0.0 16.4 %copy-start.5 = (bf16[4096]{0:T(1024)(128)(2,1)S(1)}, bf16[4096]{0:T(1024)(128)(2,1)}, u32[]{:S(2)}) copy-start(bf16[4096]{0:T(1024)(128)(2,1)} %refs_5_.1) | copy-start | bytes 24580
  0.0 11.6 %collective-permute-start.1 = (bf16[16,4096]{1,0:T(8,128)(2,1)}, bf16[16,4096]{1,0:T(8,128)(2,1)S(1)}, u32[]{:S(2)}, u32[]{:S(2)}) collective-permute-start(bf16[16,4096]{1,0:T(8,128)(2,1)} %refs_1_.1), channel_id=1, source_target_pairs={{0,3},{1,2},{2,1},{3,0},{4,7},{5,6},{6,5},{7,4},{8,11},{9,10},{10,... | collective-permute-start | bytes 393224 | tf_op jit(solution)/shard_map/gather_hidden/ppermute | solution.py:310
  5.1 11.3 %collective-permute-start = (bf16[16,4096]{1,0:T(8,128)(2,1)}, bf16[16,4096]{1,0:T(8,128)(2,1)S(1)}, u32[]{:S(2)}, u32[]{:S(2)}) collective-permute-start(bf16[16,4096]{1,0:T(8,128)(2,1)} %refs_1_.1), channel_id=1, source_target_pairs={{0,2},{1,3},{2,0},{3,1},{4,6},{5,7},{6,4},{7,5},{8,10},{9,11},{10,... | collective-permute-start | bytes 393224 | tf_op jit(solution)/shard_map/gather_hidden/ppermute | solution.py:310
  5.1 11.3 %collective-permute-start.2 = (bf16[16,4096]{1,0:T(8,128)(2,1)}, bf16[16,4096]{1,0:T(8,128)(2,1)S(1)}, u32[]{:S(2)}, u32[]{:S(2)}) collective-permute-start(bf16[16,4096]{1,0:T(8,128)(2,1)} %refs_1_.1), channel_id=1, source_target_pairs={{0,1},{1,0},{2,3},{3,2},{4,5},{5,4},{6,7},{7,6},{8,9},{9,8},{10,11... | collective-permute-start | bytes 393224 | tf_op jit(solution)/shard_map/gather_hidden/ppermute | solution.py:310
  11.6 10.1 %copy-start.6 = (s32[4]{0:T(128)S(1)}, s32[4]{0:T(128)}, u32[]{:S(2)}) copy-start(s32[4]{0:T(128)} %refs_2_.3) | copy-start | bytes 52
  19.5 10.4 %copy-start = (bf16[4,256,512]{2,1,0:T(8,128)(2,1)S(1)}, bf16[4,256,512]{2,1,0:T(8,128)(2,1)}, u32[]{:S(2)}) copy-start(bf16[4,256,512]{2,1,0:T(8,128)(2,1)} %refs_2_.5) | copy-start | bytes 3145732
  19.5 10.3 %copy-start.1 = (bf16[4,256,512]{2,1,0:T(8,128)(2,1)S(1)}, bf16[4,256,512]{2,1,0:T(8,128)(2,1)}, u32[]{:S(2)}) copy-start(bf16[4,256,512]{2,1,0:T(8,128)(2,1)} %refs_3_.3) | copy-start | bytes 3145732
  19.5 5.0 %collective-permute-start.3 = (bf16[16,2432]{1,0:T(8,128)(2,1)S(1)}, bf16[16,2432]{1,0:T(8,128)(2,1)S(1)}, u32[]{:S(2)}, u32[]{:S(2)}) collective-permute-start(bf16[16,2432]{1,0:T(8,128)(2,1)S(1)} %get-tuple-element.28), channel_id=1, source_target_pairs={{0,8},{4,12},{8,0},{12,4},{1,9},{5,13},{9,1},{13,5},{2,10},{6,14},... | collective-permute-start | bytes 233480 | tf_op jit(solution)/shard_map/sum_gx/ppermute | solution.py:310
  21.0 3.4 %collective-permute-start.4 = (bf16[16,2432]{1,0:T(8,128)(2,1)S(1)}, bf16[16,2432]{1,0:T(8,128)(2,1)S(1)}, u32[]{:S(2)}, u32[]{:S(2)}) collective-permute-start(bf16[16,2432]{1,0:T(8,128)(2,1)S(1)} %get-tuple-element.29), channel_id=1, source_target_pairs={{0,4},{4,0},{8,12},{12,8},{1,5},{5,1},{9,13},{13,9},{2,6},{6,2},{1... | collective-permute-start | bytes 233480 | tf_op jit(solution)/shard_map/sum_gx/ppermute | solution.py:310
  21.0 4.0 %collective-permute-start.5 = (bf16[16,2432]{1,0:T(8,128)(2,1)S(1)}, bf16[16,2432]{1,0:T(8,128)(2,1)S(1)}, u32[]{:S(2)}, u32[]{:S(2)}) collective-permute-start(bf16[16,2432]{1,0:T(8,128)(2,1)S(1)} %get-tuple-element.30), channel_id=1, source_target_pairs={{0,12},{4,8},{8,4},{12,0},{1,13},{5,9},{9,5},{13,1},{2,14},{6,10},... | collective-permute-start | bytes 233480 | tf_op jit(solution)/shard_map/sum_gx/ppermute | solution.py:310
  25.2 3.4 %collective-permute-start.6 = (bf16[4,2432]{1,0:T(4,128)(2,1)S(1)}, bf16[4,2432]{1,0:T(4,128)(2,1)S(1)}, u32[]{:S(2)}, u32[]{:S(2)}) collective-permute-start(bf16[4,2432]{1,0:T(4,128)(2,1)S(1)} %get-tuple-element.31), channel_id=1, source_target_pairs={{0,4},{1,5},{2,6},{3,7},{4,0},{5,1},{6,2},{7,3},{8,12},{9,13},{10,... | collective-permute-start | bytes 58376 | tf_op jit(solution)/shard_map/to_owner/ppermute | solution.py:320
  25.7 4.1 %collective-permute-start.7 = (bf16[4,2432]{1,0:T(4,128)(2,1)S(1)}, bf16[4,2432]{1,0:T(4,128)(2,1)S(1)}, u32[]{:S(2)}, u32[]{:S(2)}) collective-permute-start(bf16[4,2432]{1,0:T(4,128)(2,1)S(1)} %get-tuple-element.32), channel_id=1, source_target_pairs={{0,6},{1,7},{2,4},{3,5},{4,2},{5,3},{6,0},{7,1},{8,14},{9,15},{10,... | collective-permute-start | bytes 58376 | tf_op jit(solution)/shard_map/to_owner/ppermute | solution.py:320
  25.7 5.1 %collective-permute-start.10 = (bf16[4,2432]{1,0:T(4,128)(2,1)S(1)}, bf16[4,2432]{1,0:T(4,128)(2,1)S(1)}, u32[]{:S(2)}, u32[]{:S(2)}) collective-permute-start(bf16[4,2432]{1,0:T(4,128)(2,1)S(1)} %get-tuple-element.38), channel_id=1, source_target_pairs={{0,7},{1,6},{2,5},{3,4},{4,3},{5,2},{6,1},{7,0},{8,15},{9,14},{10,... | collective-permute-start | bytes 58376 | tf_op jit(solution)/shard_map/to_owner/ppermute | solution.py:320
  27.9 3.3 %collective-permute-start.11 = (bf16[4,2432]{1,0:T(4,128)(2,1)S(1)}, bf16[4,2432]{1,0:T(4,128)(2,1)S(1)}, u32[]{:S(2)}, u32[]{:S(2)}) collective-permute-start(bf16[4,2432]{1,0:T(4,128)(2,1)S(1)} %get-tuple-element.39), channel_id=1, source_target_pairs={{0,5},{1,4},{2,7},{3,6},{4,1},{5,0},{6,3},{7,2},{8,13},{9,12},{10,... | collective-permute-start | bytes 58376 | tf_op jit(solution)/shard_map/to_owner/ppermute | solution.py:320
  30.4 4.1 %collective-permute-start.8 = (bf16[4,2048]{1,0:T(4,128)(2,1)S(1)}, bf16[4,2048]{1,0:T(4,128)(2,1)S(1)}, u32[]{:S(2)}, u32[]{:S(2)}) collective-permute-start(bf16[4,2048]{1,0:T(4,128)(2,1)S(1)} %get-tuple-element.36), channel_id=1, source_target_pairs={{0,4},{1,5},{2,6},{3,7},{4,0},{5,1},{6,2},{7,3},{8,12},{9,13},{10,... | collective-permute-start | bytes 49160 | tf_op jit(solution)/shard_map/to_head_rows/ppermute | solution.py:320
  30.7 4.1 %collective-permute-start.9 = (bf16[4,2048]{1,0:T(4,128)(2,1)S(1)}, bf16[4,2048]{1,0:T(4,128)(2,1)S(1)}, u32[]{:S(2)}, u32[]{:S(2)}) collective-permute-start(bf16[4,2048]{1,0:T(4,128)(2,1)S(1)} %get-tuple-element.37), channel_id=1, source_target_pairs={{0,6},{1,7},{2,4},{3,5},{4,2},{5,3},{6,0},{7,1},{8,14},{9,15},{10,... | collective-permute-start | bytes 49160 | tf_op jit(solution)/shard_map/to_head_rows/ppermute | solution.py:320
  31.9 5.0 %collective-permute-start.12 = (bf16[4,2048]{1,0:T(4,128)(2,1)S(1)}, bf16[4,2048]{1,0:T(4,128)(2,1)S(1)}, u32[]{:S(2)}, u32[]{:S(2)}) collective-permute-start(bf16[4,2048]{1,0:T(4,128)(2,1)S(1)} %get-tuple-element.40), channel_id=1, source_target_pairs={{0,7},{1,6},{2,5},{3,4},{4,3},{5,2},{6,1},{7,0},{8,15},{9,14},{10,... | collective-permute-start | bytes 49160 | tf_op jit(solution)/shard_map/to_head_rows/ppermute | solution.py:320
  33.9 3.2 %collective-permute-start.13 = (bf16[4,2048]{1,0:T(4,128)(2,1)S(1)}, bf16[4,2048]{1,0:T(4,128)(2,1)S(1)}, u32[]{:S(2)}, u32[]{:S(2)}) collective-permute-start(bf16[4,2048]{1,0:T(4,128)(2,1)S(1)} %get-tuple-element.41), channel_id=1, source_target_pairs={{0,5},{1,4},{2,7},{3,6},{4,1},{5,0},{6,3},{7,2},{8,13},{9,12},{10,... | collective-permute-start | bytes 49160 | tf_op jit(solution)/shard_map/to_head_rows/ppermute | solution.py:320
  37.1 5.0 %collective-permute-start.16 = (bf16[16,2048]{1,0:T(8,128)(2,1)S(1)}, bf16[16,2048]{1,0:T(8,128)(2,1)S(1)}, u32[]{:S(2)}, u32[]{:S(2)}) collective-permute-start(bf16[16,2048]{1,0:T(8,128)(2,1)S(1)} %assemble.1.refs_1_.refs_0_), channel_id=1, source_target_pairs={{0,12},{4,8},{8,4},{12,0},{1,13},{5,9},{9,5},{13,1},{2,14},{6,10},... | collective-permute-start | bytes 196616 | tf_op jit(solution)/shard_map/gather_gx/ppermute | solution.py:310
  38.4 3.7 %collective-permute-start.15 = (bf16[16,2048]{1,0:T(8,128)(2,1)S(1)}, bf16[16,2048]{1,0:T(8,128)(2,1)S(1)}, u32[]{:S(2)}, u32[]{:S(2)}) collective-permute-start(bf16[16,2048]{1,0:T(8,128)(2,1)S(1)} %assemble.1.refs_1_.refs_0_), channel_id=1, source_target_pairs={{0,4},{4,0},{8,12},{12,8},{1,5},{5,1},{9,13},{13,9},{2,6},{6,2},{1... | collective-permute-start | bytes 196616 | tf_op jit(solution)/shard_map/gather_gx/ppermute | solution.py:310
  38.7 4.3 %collective-permute-start.14 = (bf16[16,2048]{1,0:T(8,128)(2,1)S(1)}, bf16[16,2048]{1,0:T(8,128)(2,1)S(1)}, u32[]{:S(2)}, u32[]{:S(2)}) collective-permute-start(bf16[16,2048]{1,0:T(8,128)(2,1)S(1)} %assemble.1.refs_1_.refs_0_), channel_id=1, source_target_pairs={{0,8},{4,12},{8,0},{12,4},{1,9},{5,13},{9,1},{13,5},{2,10},{6,14},... | collective-permute-start | bytes 196616 | tf_op jit(solution)/shard_map/gather_gx/ppermute | solution.py:310
  45.3 11.8 %collective-permute-start.17 = (bf16[16,4096]{1,0:T(8,128)(2,1)S(1)}, bf16[16,4096]{1,0:T(8,128)(2,1)S(1)}, u32[]{:S(2)}, u32[]{:S(2)}) collective-permute-start(bf16[16,4096]{1,0:T(8,128)(2,1)S(1)} %get-tuple-element.44), channel_id=1, source_target_pairs={{0,2},{1,3},{2,0},{3,1},{4,6},{5,7},{6,4},{7,5},{8,10},{9,11},{10,... | collective-permute-start | bytes 393224 | tf_op jit(solution)/shard_map/sum_gy/ppermute | solution.py:310
  47.2 10.0 %collective-permute-start.18 = (bf16[16,4096]{1,0:T(8,128)(2,1)S(1)}, bf16[16,4096]{1,0:T(8,128)(2,1)S(1)}, u32[]{:S(2)}, u32[]{:S(2)}) collective-permute-start(bf16[16,4096]{1,0:T(8,128)(2,1)S(1)} %get-tuple-element.45), channel_id=1, source_target_pairs={{0,1},{1,0},{2,3},{3,2},{4,5},{5,4},{6,7},{7,6},{8,9},{9,8},{10,11... | collective-permute-start | bytes 393224 | tf_op jit(solution)/shard_map/sum_gy/ppermute | solution.py:310
  47.9 9.3 %collective-permute-start.19 = (bf16[16,4096]{1,0:T(8,128)(2,1)S(1)}, bf16[16,4096]{1,0:T(8,128)(2,1)S(1)}, u32[]{:S(2)}, u32[]{:S(2)}) collective-permute-start(bf16[16,4096]{1,0:T(8,128)(2,1)S(1)} %get-tuple-element.46), channel_id=1, source_target_pairs={{0,3},{1,2},{2,1},{3,0},{4,7},{5,6},{6,5},{7,4},{8,11},{9,10},{10,... | collective-permute-start | bytes 393224 | tf_op jit(solution)/shard_map/sum_gy/ppermute | solution.py:310
